TPU v7x, 512 devices: a whole 4x8x8 slice. The times are simulated.
512 devices in a mesh: dp: 32 (over x, z_lo, core), ctx: 16 (over y, z_hi).
Axes of the slice: x: 4, y: 8, z: 8 (z_hi: 2, z_lo: 4; z = z_hi * 4 + z_lo), core: 2. Of those that a mesh axis runs over, the one named last changes fastest.
Arguments:
- query_raw: bfloat16 [32, 2048, 1024], P('dp', 'ctx'), may hold values from -40 to 40
- key_raw: bfloat16 [32, 2048, 128], P('dp', 'ctx'), may hold values from -40 to 40
- values: bfloat16 [32, 2048, 128], P('dp', 'ctx'), may hold values from -6 to 6
- out_grad: bfloat16 [32, 2048, 1024], P('dp', 'ctx'), may hold values from -6 to 6
- doc_lengths: int32 [32, 32], P('dp'), may hold values from 0 to 2048, as said below
- query_gain: float32 [128], replicated, may hold values from 0.5 to 5.5
- key_gain: float32 [128], replicated, may hold values from 0.5 to 5.5
Outputs:
- output: bfloat16 [32, 2048, 1024], P('dp', 'ctx')
- query_raw_grad: bfloat16 [32, 2048, 1024], P('dp', 'ctx')
- key_raw_grad: bfloat16 [32, 2048, 128], P('dp', 'ctx')
- values_grad: bfloat16 [32, 2048, 128], P('dp', 'ctx')
- query_gain_grad: float32 [128], replicated
- key_gain_grad: float32 [128], replicated
Inputs may be any that keep to these rules, and one draw needn't show every extreme that they name: `doc_lengths`: the lengths of each micro-batch sum to 2048; entries that are 0 come after all nonzero ones.
All inputs are finite; a program needn't handle non-finite values.
Results may differ from a plain program's by a relative error of at most 0.03.
The roundings to bfloat16 on the way count: a program that leaves them out, or rounds other values in their place, can miss the bound.
Values may be sent and summed in bfloat16 or wider, within the bound.
No kernel may reach another device: no remote copies, remote signals or barrier semaphores. Data moves between devices by JAX's collectives and lax.ppermute only.
A program may use at most 128 MiB of HBM per device.

v0:
```python
import math

import jax
import jax.numpy as jnp
from jax import lax
from jax.sharding import PartitionSpec as P

rope_theta = 1000000.0
norm_epsilon = 1e-06
masked_value = -1e30


def rope_tables(positions, head_width):
    half_width = head_width // 2
    exponent = jnp.arange(half_width, dtype=jnp.float32) * (2.0 / head_width)
    frequency = jnp.power(jnp.float32(rope_theta), -exponent)
    angles = positions.astype(jnp.float32)[:, None] * frequency[None, :]
    return (jnp.cos(angles), jnp.sin(angles))


def rotate(vector, cosine, sine_table):
    half_width = vector.shape[-1] // 2
    lower_half = vector[..., :half_width]
    upper_half = vector[..., half_width:]
    return jnp.concatenate(
        [
            lower_half * cosine - upper_half * sine_table,
            upper_half * cosine + lower_half * sine_table,
        ],
        axis=-1,
    )


def normalize(raw_rows, gain_vector):
    as_float = raw_rows.astype(jnp.float32)
    inverse = lax.rsqrt(jnp.mean(as_float * as_float, axis=-1, keepdims=True) + norm_epsilon)
    unit_rows = as_float * inverse
    return (unit_rows * gain_vector, unit_rows, inverse)


def norm_back(upstream, unit_rows, inverse, gain_vector):
    scaled = upstream * gain_vector
    return inverse * (scaled - unit_rows * jnp.mean(scaled * unit_rows, axis=-1, keepdims=True))


def token_starts(doc_ends, first_token, tok_count):
    tokens = first_token + jnp.arange(tok_count, dtype=jnp.int32)
    before = doc_ends[None, :] <= tokens[:, None]
    return jnp.max(jnp.where(before, doc_ends[None, :], 0), axis=1)


def body(query_raw, key_raw, values, out_grad, doc_lengths, query_gain, key_gain):
    tok_count = query_raw.shape[1]
    head_width = key_raw.shape[2]
    head_count = query_raw.shape[2] // head_width
    row_count = tok_count * head_count
    key_count = tok_count * lax.axis_size("ctx")
    key_block = math.gcd(key_count, 512)
    block_count = key_count // key_block
    score_scale = head_width ** (-0.5)
    first_token = lax.axis_index("ctx") * tok_count
    doc_ends = jnp.cumsum(doc_lengths[0])
    doc_starts = token_starts(doc_ends, first_token, tok_count)
    cosine, sine_table = rope_tables(
        first_token + jnp.arange(tok_count, dtype=jnp.int32) - doc_starts, head_width
    )
    query_normed, query_unit, query_inverse = normalize(
        query_raw[0].reshape(tok_count, head_count, head_width), query_gain
    )
    queries = rotate(query_normed, cosine[:, None, :], sine_table[:, None, :]).astype(jnp.bfloat16)
    key_normed, key_unit, key_inverse = normalize(key_raw[0], key_gain)
    key_rows = rotate(key_normed, cosine, sine_table).astype(jnp.bfloat16)
    value_rows = values[0]
    key_all, value_all = (
        lax.all_gather(key_rows, "ctx", axis=0, tiled=True),
        lax.all_gather(value_rows, "ctx", axis=0, tiled=True),
    )
    query_rows = queries.reshape(row_count, head_width)
    grad_rows = out_grad[0].reshape(row_count, head_width)
    row_token = first_token + jnp.arange(row_count, dtype=jnp.int32) // head_count
    row_start = jnp.repeat(doc_starts, head_count)

    def tile_scores(offset):
        key_block_rows = lax.dynamic_slice_in_dim(key_all, offset, key_block, 0)
        columns = offset + jnp.arange(key_block, dtype=jnp.int32)
        allowed = (columns[None, :] >= row_start[:, None]) & (
            columns[None, :] <= row_token[:, None]
        )
        scores = (
            jnp.einsum("rd,kd->rk", query_rows, key_block_rows, preferred_element_type=jnp.float32)
            * score_scale
        )
        return (allowed, jnp.where(allowed, scores, masked_value))

    def find_total(block_index, running):
        offset = block_index * key_block
        allowed, scores = tile_scores(offset)
        new_max = jnp.maximum(running[0], jnp.max(scores, axis=1, keepdims=True))
        terms = jnp.where(allowed, jnp.exp(scores - new_max), 0.0)
        return (
            new_max,
            running[1] * jnp.exp(running[0] - new_max) + jnp.sum(terms, axis=1, keepdims=True),
        )

    start_max = jnp.full((row_count, 1), masked_value, jnp.float32)
    start_sum = jnp.zeros((row_count, 1), jnp.float32)
    row_max, row_sum = lax.fori_loop(0, block_count, find_total, (start_max, start_sum))
    log_total = row_max + jnp.log(row_sum)

    def add_values(block_index, output_sum):
        offset = block_index * key_block
        allowed, scores = tile_scores(offset)
        weights = jnp.where(allowed, jnp.exp(scores - log_total), 0.0).astype(jnp.bfloat16)
        value_block = lax.dynamic_slice_in_dim(value_all, offset, key_block, 0)
        return output_sum + jnp.dot(weights, value_block, preferred_element_type=jnp.float32)

    output = lax.fori_loop(
        0, block_count, add_values, jnp.zeros((row_count, head_width), jnp.float32)
    ).astype(jnp.bfloat16)
    row_delta = jnp.sum(
        grad_rows.astype(jnp.float32) * output.astype(jnp.float32), axis=1, keepdims=True
    )

    def back_tile(offset):
        allowed, scores = tile_scores(offset)
        prob_tile = jnp.where(allowed, jnp.exp(scores - log_total), 0.0)
        value_block = lax.dynamic_slice_in_dim(value_all, offset, key_block, 0)
        prob_grad = jnp.einsum(
            "rd,kd->rk", grad_rows, value_block, preferred_element_type=jnp.float32
        )
        score_grad = (prob_tile * (prob_grad - row_delta)).astype(jnp.bfloat16)
        key_block_rows = lax.dynamic_slice_in_dim(key_all, offset, key_block, 0)
        return (prob_tile, score_grad, key_block_rows)

    zero_rows = jnp.zeros((row_count, head_width), jnp.float32)

    def query_and_key_step(query_grad, block_index):
        offset = block_index * key_block
        prob_tile, score_grad, key_block_rows = back_tile(offset)
        new_grad = query_grad + jnp.dot(
            score_grad, key_block_rows, preferred_element_type=jnp.float32
        )
        key_part = jnp.einsum(
            "rk,rd->kd", score_grad, query_rows, preferred_element_type=jnp.float32
        )
        value_part = jnp.einsum(
            "rk,rd->kd",
            prob_tile.astype(jnp.bfloat16),
            grad_rows,
            preferred_element_type=jnp.float32,
        )
        new_grad, key_part, value_part = (new_grad, key_part, value_part)
        return (new_grad, (key_part, value_part))

    query_grad, stacked = lax.scan(query_and_key_step, zero_rows, jnp.arange(block_count))
    key_terms = stacked[0].reshape(key_count, head_width)
    value_terms = stacked[1].reshape(key_count, head_width)
    key_grad_own, value_grad_own = (
        lax.psum_scatter(key_terms, "ctx", scatter_dimension=0, tiled=True),
        lax.psum_scatter(value_terms, "ctx", scatter_dimension=0, tiled=True),
    )
    query_back = rotate(
        (query_grad * score_scale).reshape(tok_count, head_count, head_width),
        cosine[:, None, :],
        -sine_table[:, None, :],
    )
    key_back = rotate(key_grad_own * score_scale, cosine, -sine_table)
    query_raw_grad = (
        norm_back(query_back, query_unit, query_inverse, query_gain)
        .reshape(1, tok_count, head_count * head_width)
        .astype(jnp.bfloat16)
    )
    key_raw_grad = (
        norm_back(key_back, key_unit, key_inverse, key_gain)
        .reshape(1, tok_count, head_width)
        .astype(jnp.bfloat16)
    )
    query_gain_grad, key_gain_grad = lax.psum(
        (jnp.sum(query_back * query_unit, axis=(0, 1)), jnp.sum(key_back * key_unit, axis=0)),
        ("dp", "ctx"),
    )
    values_grad = value_grad_own.astype(jnp.bfloat16).reshape(1, tok_count, head_width)
    return (
        output.reshape(1, tok_count, head_count * head_width),
        query_raw_grad,
        key_raw_grad,
        values_grad,
        query_gain_grad,
        key_gain_grad,
    )


def solution(mesh):
    return jax.shard_map(
        body,
        mesh=mesh,
        in_specs=(
            P("dp", "ctx", None),
            P("dp", "ctx", None),
            P("dp", "ctx", None),
            P("dp", "ctx", None),
            P("dp", None),
            P(),
            P(),
        ),
        out_specs=(
            P("dp", "ctx", None),
            P("dp", "ctx", None),
            P("dp", "ctx", None),
            P("dp", "ctx", None),
            P(),
            P(),
        ),
        check_vma=False,
    )
```

profile of v0, /device:TPU:1, one launch (start us, length us, event | category | flops | bytes accessed | tf_op | source)
XLA Modules:
  0.0 641.8 jit_solution(15061655184923233575)
XLA Ops:
  7.3 1.1 reshape_squeeze.4
  12.1 55.2 %all_gather.6 = bf16[2048,128]{1,0:T(8,128)(2,1)S(1)} all-gather(bf16[128,128]{1,0:T(8,128)(2,1)S(1)} %pad_maximum_fusion.3), channel_id=1, replica_groups=mesh['dp'=32,'ctx'=16] {'ctx'}, dimensions={0}, use_global_device_ids=true | all-gather | bytes 557056 | tf_op jit(solution)/shard_map/all_gather | solution.py:75
  67.3 1.0 convert_bitcast_fusion
  69.9 6.6 %while.45 = (s32[]{:T(128)}, f32[1024,1]{0,1:T(1,128)S(1)}, f32[1024,1]{0,1:T(1,128)S(1)}, bf16[2048,128]{1,0:T(8,128)(2,1)S(1)}, bf16[1024,128]{1,0:T(8,128)(2,...) while((s32[]{:T(128)}, f32[1024,1]{0,1:T(1,128)S(1)}, ...), condition=%wide.region_7.8_spmd.clone, body=%wide.region_4.7_spmd.clone.sunk | while | flops 141572608 | bytes 4680378 | solution.py:107
  76.5 53.5 %all-gather = bf16[1,2048,128]{2,1,0:T(8,128)(2,1)} all-gather(bf16[1,128,128]{2,1,0:T(8,128)(2,1)S(1)} %copy-done.10), channel_id=2, replica_groups=mesh['dp'=32,'ctx'=16] {'ctx'}, dimensions={1}, use_global_device_ids=true | all-gather | bytes 557056 | tf_op jit(solution)/shard_map/all_gather | solution.py:76
  130.0 13.2 %while.46 = (s32[]{:T(128)}, f32[1024,128]{1,0:T(8,128)}, bf16[2048,128]{1,0:T(8,128)(2,1)S(1)}, bf16[1024,128]{1,0:T(8,128)(2,1)S(1)}, f32[1024,1]{0,1:T(1,128)...) while((s32[]{:T(128)}, f32[1024,128]{1,0:T(8,128)}, ...), condition=%wide.region_9.10_spmd.clone, body=%wide.region_8.9_spmd.clone.sunk | while | flops 272901632 | bytes 1607868 | solution.py:117
  130.2 2.9 fusion.134
  133.3 3.1 fusion.134
  136.7 3.1 fusion.134
  140.0 3.1 fusion.134
  143.2 1.9 multiply_reduce_fusion.2
  145.0 37.0 %while.47 = (s32[]{:T(128)}, f32[1024,128]{1,0:T(8,128)}, f32[4,512,128]{2,1,0:T(8,128)}, f32[4,512,128]{2,1,0:T(8,128)}, s32[4]{0:T(128)S(1)}, /*index=5*/bf16[...) while((s32[]{:T(128)}, f32[1024,128]{1,0:T(8,128)}, ...), condition=%wide.region_12.13_spmd.clone, body=%wide.region_11.12_spmd.clone.sunk | while | flops 677127680 | bytes 18814052 | solution.py:155
  147.3 1.3 fusion.147
  148.6 2.2 convolution_add_fusion.2
  150.8 2.1 fusion.148
  152.9 1.2 fusion.149
  156.4 1.3 fusion.147
  157.7 2.4 convolution_add_fusion.2
  160.1 2.1 fusion.148
  162.2 1.2 fusion.149
  165.7 1.3 fusion.147
  167.1 2.4 convolution_add_fusion.2
  169.4 2.1 fusion.148
  171.5 1.2 fusion.149
  175.0 1.3 fusion.147
  176.4 2.4 convolution_add_fusion.2
  178.7 2.1 fusion.148
  180.9 1.2 fusion.149
  184.2 227.0 %reduce-scatter.3.cloned.1.call-done = f32[128,128]{1,0:T(8,128)} async-done(((f32[2048,128]{1,0:T(8,128)}), f32[128,128]{1,0:T(8,128)}) %reduce-scatter.3.cloned.1.call-update) | async-done | bytes 65552 | tf_op jit(solution)/shard_map/reduce_scatter | solution.py:159
  414.7 101.9 %all-reduce = (f32[128]{0:T(128)}, f32[128]{0:T(128)}) all-reduce(f32[128]{0:T(128)S(1)} %bitcast_reduce_fusion, f32[128]{0:T(128)S(1)} %get-tuple-element.456), channel_id=1, replica_groups=mesh['dp'=32,'ctx'=16] {'dp','ctx'}, use_global_device_ids=true, to_apply=%region_19.20 | all-reduce | flops 256 | bytes 2048 | tf_op jit(solution)/shard_map/psum | solution.py:178
  517.4 116.2 %reduce-scatter.5.cloned.1.call-done = f32[128,128]{1,0:T(8,128)} async-done(((f32[2048,128]{1,0:T(8,128)}), f32[128,128]{1,0:T(8,128)}) %reduce-scatter.5.cloned.1.call-update) | async-done | bytes 65552 | tf_op jit(solution)/shard_map/reduce_scatter | solution.py:160
  633.5 1.5 convert_bitcast_fusion.2
  (218 shorter events, 24.6 us)
Async XLA Ops:
  7.2 404.0 %reduce-scatter.3.cloned.1.call-start = ((), (), s32[]{:S(2)}) async-start(), calls=%async_computation.2 | async-start | bytes 1114112 | tf_op jit(solution)/shard_map/reduce_scatter | solution.py:159
  7.2 4.9 copy-start.17
  7.3 61.9 %copy-start.11 = (f32[128]{0:T(128)S(1)}, f32[128]{0:T(128)}, u32[]{:S(2)}) copy-start(f32[128]{0:T(128)} %param.18) | copy-start | bytes 1540
  9.4 2.7 copy-start.19
  69.9 6.6 %copy-start.10 = (bf16[1,128,128]{2,1,0:T(8,128)(2,1)S(1)}, bf16[1,128,128]{2,1,0:T(8,128)(2,1)}, u32[]{:S(2)}) copy-start(bf16[1,128,128]{2,1,0:T(8,128)(2,1)} %param.15) | copy-start | bytes 98308
  145.0 1.5 copy-start.21
  145.0 2.2 copy-start.1
  145.0 2.2 copy-start.15
  145.0 2.2 copy-start.5
  152.9 1.2 copy-start.16
  152.9 1.2 copy-start.22
  154.1 1.5 copy-start.21
  154.1 2.2 copy-start.1
  154.1 2.2 copy-start.15
  154.1 2.2 copy-start.5
  162.2 1.2 copy-start.22
  163.4 1.5 copy-start.21
  163.4 2.2 copy-start.1
  163.4 2.2 copy-start.15
  163.5 2.2 copy-start.5
  172.7 1.5 copy-start.21
  172.7 2.2 copy-start.1
  172.7 2.2 copy-start.15
  172.8 2.2 copy-start.5
  182.1 1.8 copy-start
  182.1 451.4 %reduce-scatter.5.cloned.1.call-start = ((), (), s32[]{:S(2)}) async-start(), calls=%async_computation.3 | async-start | bytes 1114112 | tf_op jit(solution)/shard_map/reduce_scatter | solution.py:160
  182.1 229.9 %copy-start.18 = (f32[64]{0:T(128)S(1)}, f32[64]{0:T(128)}, u32[]{:S(2)}) copy-start(f32[64]{0:T(128)} %copy-done.17) | copy-start | bytes 772
  182.1 229.9 %copy-start.20 = (f32[128]{0:T(128)S(1)}, f32[128]{0:T(128)}, u32[]{:S(2)}) copy-start(f32[128]{0:T(128)} %copy-done.19) | copy-start | bytes 1540
  183.9 228.8 %copy-start.4 = (f32[16,8,8,128]{3,2,1,0:T(8,128)S(1)}, f32[16,8,8,128]{3,2,1,0:T(8,128)}, u32[]{:S(2)}) copy-start(f32[16,8,8,128]{3,2,1,0:T(8,128)} %copy-done.3) | copy-start | bytes 1572868
  413.3 1.3 copy-start.9
  413.3 1.2 copy-start.12
  413.3 1.2 copy-start.14
  (17 other events, 18.6 us)
Sparse Core Ops, SparseCore 0:
  182.2 228.9 reduce-scatter.2
  416.3 217.1 reduce-scatter.4
where the time goes:
time: 647 us; the launch traced here: 642 us
  waiting for transfers between devices  344 us (53%)
  blocking collectives  211 us (33%)
  matrix products  45.4 us (7%)
  other arithmetic  14.6 us (2%)
  between operations  14.5 us (2%)
  local copies, waits for them, and re-layouts  9.25 us (1%)
    reduce_scatter x1, waiting for transfers between devices, body(): lax.psum_scatter(key_terms, 'ctx', scatter_dimension=0, tiled=True)  227 us
    reduce_scatter x1, waiting for transfers between devices, body(): lax.psum_scatter(value_terms, 'ctx', scatter_dimension=0, tiled=True)  116 us
    psum x1, blocking collectives, body(): lax.psum((jnp.sum(query_back * query_unit, axis=(0, 1)), jnp.sum(key_back...  102 us
    all_gather x1, blocking collectives, body(): lax.all_gather(key_rows, 'ctx', axis=0, tiled=True)  55.2 us
    all_gather x1, blocking collectives, body(): lax.all_gather(value_rows, 'ctx', axis=0, tiled=True)  53.5 us
  transfers between devices with their start and end apart: 2, of which 2 were waited for; matrix products, arithmetic and copies ran while one was open for 1% of the time, Pallas kernels for 0%

commit v1 on v0

v1 whole, which is shorter than its diff:
```python
import functools
import math

import jax
import jax.numpy as jnp
from jax import lax
from jax.experimental import pallas as pl
from jax.experimental.pallas import tpu as pltpu
from jax.sharding import PartitionSpec as P

rope_theta = 1000000.0
norm_epsilon = 1e-06
masked_value = -1e30
D = 128
F32 = jnp.float32
BF16 = jnp.bfloat16
VM = pl.BlockSpec(memory_space=pltpu.VMEM)
SM = pl.BlockSpec(memory_space=pltpu.SMEM)
SCALE = D ** (-0.5)
LOG2E = math.log2(math.e)
GAIN_ROWS = 16


def dot(a, b):
    return jnp.dot(a, b, preferred_element_type=F32)


def sin_cos(angle):
    turns = jnp.floor(angle * (2.0 / math.pi) + 0.5)
    r = angle - turns * 1.5703125
    r = r - turns * 4.837512969970703125e-4
    r = r - turns * 7.549789948768648e-8
    r2 = r * r
    s = r + r * r2 * (-1.6666654611e-1 + r2 * (8.3321608736e-3 + r2 * -1.9515295891e-4))
    c = 1.0 - 0.5 * r2 + r2 * r2 * (
        4.166664568298827e-2 + r2 * (-1.388731625493765e-3 + r2 * 2.443315711809948e-5)
    )
    quarter = turns.astype(jnp.int32)
    odd = (quarter & 1) == 1
    sin_part = jnp.where(odd, c, s)
    cos_part = jnp.where(odd, s, c)
    sin_part = jnp.where((quarter & 2) == 2, -sin_part, sin_part)
    cos_part = jnp.where(((quarter + 1) & 2) == 2, -cos_part, cos_part)
    return sin_part, cos_part


def starts_of(lengths, tokens):
    end = jnp.int32(0)
    start = jnp.zeros_like(tokens)
    for d in range(lengths.shape[1]):
        end = end + lengths[0, d]
        start = jnp.where(tokens >= end, end, start)
    return start


def rotate(x, cosine, sine):
    return x * cosine + pltpu.roll(x, D // 2, 1) * sine


def rotate_back(x, cosine, sine):
    return x * cosine - pltpu.roll(x, D // 2, 1) * sine


def unit_of(raw):
    x = raw.astype(F32)
    inverse = lax.rsqrt(jnp.mean(x * x, axis=1, keepdims=True) + norm_epsilon)
    return x * inverse, inverse


def prep_kernel(
    heads, token_ref, lengths, freq, q_raw, dout, q_gain,
    cos_ref, sin_ref, cos_own, sin_own, q_ref, qt_ref, do_ref, dot_ref, pos_ref,
):
    tokens_own = q_raw.shape[0]
    seq = cos_ref.shape[0]
    row = lax.broadcasted_iota(jnp.int32, (D, D), 0)
    lane = lax.broadcasted_iota(jnp.int32, (D, D), 1)
    tokens = row * D + lane
    positions = tokens - starts_of(lengths, tokens)
    pos_ref[...] = positions.astype(F32).T
    first_lanes = lane < D // 2
    for i in range(seq // D):
        angle = pos_ref[:, i : i + 1] * freq[...]
        s, c = sin_cos(angle)
        cos_ref[i * D : (i + 1) * D, :] = c
        sin_ref[i * D : (i + 1) * D, :] = jnp.where(first_lanes, -s, s)
    first = pl.multiple_of(token_ref[0], tokens_own)
    cosine = cos_ref[pl.ds(first, tokens_own), :]
    sine = sin_ref[pl.ds(first, tokens_own), :]
    cos_own[...] = cosine
    sin_own[...] = sine
    for h in range(heads):
        cols = slice(h * D, (h + 1) * D)
        rows = slice(h * tokens_own, (h + 1) * tokens_own)
        unit, _ = unit_of(q_raw[:, cols])
        q = rotate(unit * q_gain[...], cosine, sine)
        q_ref[rows, :] = q.astype(BF16)
        qt_ref[:, rows] = q.T.astype(BF16)
        g = dout[:, cols]
        do_ref[rows, :] = g
        dot_ref[:, rows] = g.astype(F32).T.astype(BF16)


def attend_kernel(
    heads, token_ref, lengths, kv, cos_ref, sin_ref, cos_own, sin_own, q_ref, qt_ref, do_ref, dot_ref,
    q_raw, q_gain, k_gain,
    out_ref, dq_ref, dkv_ref, gains_ref,
    s_buf, w_buf, k_buf, kt_buf, vt_buf, ot_buf, dqt_buf, max_buf, sum_buf, row_buf, kg_buf,
):
    blocks, kb, _ = kv.shape
    tokens_own = q_raw.shape[0]
    cols_all = heads * tokens_own
    cc = 2 * tokens_own
    chunks = cols_all // cc
    first = token_ref[0]
    end = jnp.int32(0)
    low = jnp.int32(0)
    for d in range(lengths.shape[1]):
        end = end + lengths[0, d]
        low = jnp.where(end <= first, end, low)
    lo = low // kb
    hi = (first + tokens_own - 1) // kb + 1
    tok = first + lax.broadcasted_iota(jnp.int32, (8, tokens_own), 1)
    start_row = starts_of(lengths, tok)[:1]
    tok_row = tok[:1]
    dkv_ref[...] = jnp.zeros_like(dkv_ref)
    max_buf[...] = jnp.full_like(max_buf, masked_value)
    sum_buf[...] = jnp.zeros_like(sum_buf)
    ot_buf[...] = jnp.zeros_like(ot_buf)
    dqt_buf[...] = jnp.zeros_like(dqt_buf)
    kg_buf[...] = jnp.zeros_like(kg_buf)
    factor = SCALE * LOG2E

    def block_rows(b):
        return pl.ds(pl.multiple_of(b * kb, kb), kb)

    def scores_step(b, carry):
        rows = block_rows(b)
        unit, _ = unit_of(kv[b, :, :D])
        k = rotate(unit * k_gain[...], cos_ref[rows, :], sin_ref[rows, :])
        k_rows = k.astype(BF16)
        k_buf[b] = k_rows
        kt_buf[b] = k.T.astype(BF16)
        vt_buf[b] = kv[b, :, D:].astype(F32).T.astype(BF16)
        key = b * kb + lax.broadcasted_iota(jnp.int32, (kb, tokens_own), 0)
        allowed = (key >= start_row) & (key <= tok_row)
        bias = jnp.where(allowed, 0.0, masked_value)
        for c in range(chunks):
            cs = slice(c * cc, (c + 1) * cc)
            s = dot(k_rows, qt_ref[:, cs]) * factor + jnp.concatenate([bias, bias], 1)
            s_buf[b, :, cs] = s
            max_buf[:, cs] = jnp.maximum(max_buf[:, cs], jnp.max(s.reshape(kb // 8, 8, cc), axis=0))
        return carry

    lax.fori_loop(lo, hi, scores_step, 0)
    row_buf[:1, :] = jnp.max(max_buf[...], axis=0, keepdims=True)

    def exp_step(b, carry):
        for c in range(chunks):
            cs = slice(c * cc, (c + 1) * cc)
            e = jnp.exp2(s_buf[b, :, cs] - row_buf[:1, cs])
            s_buf[b, :, cs] = e
            sum_buf[:, cs] += jnp.sum(e.reshape(kb // 8, 8, cc), axis=0)
        return carry

    lax.fori_loop(lo, hi, exp_step, 0)
    row_buf[:1, :] = 1.0 / jnp.sum(sum_buf[...], axis=0, keepdims=True)

    def values_step(b, carry):
        dv = jnp.zeros((kb, D), F32)
        for c in range(chunks):
            cs = slice(c * cc, (c + 1) * cc)
            prob = s_buf[b, :, cs] * row_buf[:1, cs]
            s_buf[b, :, cs] = prob
            w = prob.astype(BF16)
            ot_buf[:, cs] += dot(vt_buf[b], w)
            dv = dv + dot(w, do_ref[cs, :])
        dkv_ref[b, :kb, D:] = dv.astype(BF16)
        return carry

    lax.fori_loop(lo, hi, values_step, 0)
    for h in range(heads):
        hs = slice(h * tokens_own, (h + 1) * tokens_own)
        ot = ot_buf[:, hs].astype(BF16).astype(F32)
        out_ref[:, h * D : (h + 1) * D] = ot.T.astype(BF16)
        row_buf[:1, hs] = jnp.sum(ot * dot_ref[:, hs].astype(F32), axis=0, keepdims=True)

    def back_step(b, carry):
        rows = block_rows(b)
        dk = jnp.zeros((kb, D), F32)
        v_rows = kv[b, :, D:]
        for c in range(chunks):
            cs = slice(c * cc, (c + 1) * cc)
            dp = dot(v_rows, dot_ref[:, cs])
            ds = (s_buf[b, :, cs] * (dp - row_buf[:1, cs])).astype(BF16)
            dk = dk + dot(ds, q_ref[cs, :])
            dqt_buf[:, cs] += dot(kt_buf[b], ds)
        dk = dk * SCALE
        dkv_ref[b, :kb, :D] = dk.astype(BF16)
        unit, _ = unit_of(kv[b, :, :D])
        terms = rotate_back(dk, cos_ref[rows, :], sin_ref[rows, :]) * unit
        kg_buf[...] += jnp.sum(terms.reshape(kb // 8, 8, D), axis=0)
        return carry

    lax.fori_loop(lo, hi, back_step, 0)
    cosine = cos_own[...]
    sine = sin_own[...]
    q_sum = jnp.zeros((8, D), F32)
    for h in range(heads):
        hs = slice(h * tokens_own, (h + 1) * tokens_own)
        back = rotate_back(dqt_buf[:, hs].T * SCALE, cosine, sine)
        unit, inverse = unit_of(q_raw[:, h * D : (h + 1) * D])
        q_sum = q_sum + jnp.sum((back * unit).reshape(tokens_own // 8, 8, D), axis=0)
        scaled = back * q_gain[...]
        mean = jnp.mean(scaled * unit, axis=1, keepdims=True)
        dq_ref[:, h * D : (h + 1) * D] = (inverse * (scaled - unit * mean)).astype(BF16)
    gains_ref[:, :D] = jnp.broadcast_to(jnp.sum(q_sum, axis=0, keepdims=True), (8, D))
    gains_ref[:, D:] = jnp.broadcast_to(jnp.sum(kg_buf[...], axis=0, keepdims=True), (8, D))
    total = gains_ref[:1, :]
    high = total.astype(BF16).astype(F32)
    middle = (total - high).astype(BF16).astype(F32)
    lowest = total - high - middle
    row = lax.broadcasted_iota(jnp.int32, (GAIN_ROWS, 2 * D), 0)
    tail = jnp.where(row == 0, high, jnp.where(row == 1, middle, jnp.where(row == 2, lowest, 0.0)))
    for b in range(blocks):
        dkv_ref[b, kb:, :] = tail.astype(BF16)


def finish_kernel(own_ref, other_ref, k_raw, k_gain, cos_own, sin_own, dk_ref, dv_ref):
    total = own_ref[...] + other_ref[...].astype(F32)
    unit, inverse = unit_of(k_raw[...])
    back = rotate_back(total[:, :D], cos_own[...], sin_own[...])
    scaled = back * k_gain[...]
    mean = jnp.mean(scaled * unit, axis=1, keepdims=True)
    dk_ref[...] = (inverse * (scaled - unit * mean)).astype(BF16)
    dv_ref[...] = total[:, D:].astype(BF16)


def call_prep(token, lengths, freq, q_raw, dout, q_gain, seq, **kw):
    tokens_own, width = q_raw.shape
    heads = width // D
    rows = heads * tokens_own
    shapes = [
        ((seq, D), F32), ((seq, D), F32), ((tokens_own, D), F32), ((tokens_own, D), F32),
        ((rows, D), BF16), ((D, rows), BF16), ((rows, D), BF16), ((D, rows), BF16),
    ]
    return pl.pallas_call(
        functools.partial(prep_kernel, heads),
        out_shape=[jax.ShapeDtypeStruct(s, t) for s, t in shapes],
        in_specs=[SM, SM, VM, VM, VM, VM],
        out_specs=[VM] * len(shapes),
        scratch_shapes=[pltpu.VMEM((D, D), F32)],
        compiler_params=pltpu.CompilerParams(vmem_limit_bytes=32 * 2**20),
        cost_estimate=pl.CostEstimate(flops=40_000_000, bytes_accessed=4_000_000, transcendentals=0),
        name="prep",
        **kw,
    )(token, lengths, freq, q_raw, dout, q_gain)


def call_attend(token, lengths, kv, prepared, q_raw, q_gain, k_gain, **kw):
    tokens_own, width = q_raw.shape
    heads = width // D
    blocks, kb, _ = kv.shape
    rows = heads * tokens_own
    shapes = [
        ((tokens_own, width), BF16), ((tokens_own, width), BF16),
        ((blocks, kb + GAIN_ROWS, 2 * D), BF16), ((8, 2 * D), F32),
    ]
    scratch = [
        pltpu.VMEM((blocks, kb, rows), F32), pltpu.VMEM((8, 128), F32),
        pltpu.VMEM((blocks, kb, D), BF16), pltpu.VMEM((blocks, D, kb), BF16),
        pltpu.VMEM((blocks, D, kb), BF16), pltpu.VMEM((D, rows), F32), pltpu.VMEM((D, rows), F32),
        pltpu.VMEM((8, rows), F32), pltpu.VMEM((8, rows), F32), pltpu.VMEM((8, rows), F32),
        pltpu.VMEM((8, D), F32),
    ]
    return pl.pallas_call(
        functools.partial(attend_kernel, heads),
        out_shape=[jax.ShapeDtypeStruct(s, t) for s, t in shapes],
        in_specs=[SM, SM] + [VM] * 12,
        out_specs=[VM] * len(shapes),
        scratch_shapes=scratch,
        compiler_params=pltpu.CompilerParams(vmem_limit_bytes=40 * 2**20),
        cost_estimate=pl.CostEstimate(flops=3_200_000_000, bytes_accessed=8_000_000, transcendentals=2_000_000),
        name="attend",
        **kw,
    )(token, lengths, kv, *prepared, q_raw, q_gain, k_gain)


def call_finish(own, other, k_raw, k_gain, cos_own, sin_own, **kw):
    shape = jax.ShapeDtypeStruct(k_raw.shape, BF16)
    return pl.pallas_call(
        finish_kernel,
        out_shape=[shape, shape],
        in_specs=[VM] * 6,
        out_specs=[VM] * 2,
        name="finish",
        **kw,
    )(own, other, k_raw, k_gain, cos_own, sin_own)


def frequency_row():
    exponent = jnp.arange(D // 2, dtype=F32) * (2.0 / D)
    frequency = jnp.power(F32(rope_theta), -exponent)
    return jnp.concatenate([frequency, frequency])[None, :]


def sum_parts(received, kb):
    return jnp.sum(received[:, :kb].astype(F32), axis=0)


def body(query_raw, key_raw, values, out_grad, doc_lengths, query_gain, key_gain):
    tokens_own = query_raw.shape[1]
    ctx = lax.axis_size("ctx")
    dp = lax.axis_size("dp")
    seq = tokens_own * ctx
    kb = 2 * tokens_own
    half = ctx // 2
    me = lax.axis_index("ctx")
    side = me % 2
    token = (me * tokens_own)[None].astype(jnp.int32)
    q_gain = query_gain[None, :]
    k_gain = key_gain[None, :]
    columns = [[2 * y + z for y in range(half)] for z in range(2)]
    swap = [(i, i ^ 1) for i in range(ctx)]

    kv_own = jnp.concatenate([key_raw[0], values[0]], axis=1)
    kv_other = lax.ppermute(kv_own, "ctx", swap)
    prepared = call_prep(token, doc_lengths, frequency_row(), query_raw[0], out_grad[0], q_gain, seq)
    pair = jnp.where(
        side == 0,
        jnp.concatenate([kv_own, kv_other], axis=0),
        jnp.concatenate([kv_other, kv_own], axis=0),
    )
    kv = lax.all_to_all(
        jnp.broadcast_to(pair[None], (half, kb, 2 * D)), "ctx", 0, 0, axis_index_groups=columns
    )
    output, dq, dkv, _ = call_attend(
        token, doc_lengths, kv, prepared, query_raw[0], q_gain, k_gain
    )
    received = lax.all_to_all(dkv, "ctx", 0, 0, axis_index_groups=columns)
    summed = sum_parts(received, kb)
    gains = jnp.sum(received[:, kb : kb + 3].astype(F32), axis=(0, 1))
    own = lax.dynamic_slice_in_dim(summed, side * tokens_own, tokens_own, 0)
    theirs = lax.dynamic_slice_in_dim(summed, (1 - side) * tokens_own, tokens_own, 0)
    other = lax.ppermute(theirs.astype(BF16), "ctx", swap)
    groups = [
        [d * ctx + 2 * y + z for d in range(dp) for z in range(2)] for y in range(half)
    ]
    spread = lax.all_to_all(
        jnp.broadcast_to(gains[None, None], (2 * dp, 1, 2 * D)),
        ("dp", "ctx"), 0, 0, axis_index_groups=groups,
    )
    gains = jnp.sum(spread, axis=(0, 1))
    dk, dv = call_finish(own, other, key_raw[0], k_gain, prepared[2], prepared[3])
    return (output[None], dq[None], dk[None], dv[None], gains[:D], gains[D:])


def solution(mesh):
    return jax.shard_map(
        body,
        mesh=mesh,
        in_specs=(
            P("dp", "ctx", None),
            P("dp", "ctx", None),
            P("dp", "ctx", None),
            P("dp", "ctx", None),
            P("dp", None),
            P(),
            P(),
        ),
        out_specs=(
            P("dp", "ctx", None),
            P("dp", "ctx", None),
            P("dp", "ctx", None),
            P("dp", "ctx", None),
            P(),
            P(),
        ),
        check_vma=False,
    )
```

time: 647 us -> 128 us (0.20)
  waiting for transfers between devices: 344 us -> 51.2 us
  blocking collectives: 211 us -> 0 us
  starting transfers between devices: 0.08 us -> 55.4 us
  matrix products: 45.4 us -> 0 us
  between operations: 14.5 us -> 0.73 us
  other arithmetic: 14.6 us -> 2.01 us
  Pallas kernels: 0 us -> 10.7 us
    reduce_scatter x2 -> x0, waiting for transfers between devices: 343 us -> none  [the longest x1 227 us: body(): lax.psum_scatter(key_terms, 'ctx', scatter_dimension=0, tiled=True)]
    all_gather x2 -> x0, blocking collectives: 109 us -> none  [the longest x1 55.2 us: body(): lax.all_gather(key_rows, 'ctx', axis=0, tiled=True)]
    psum x1 -> x0, blocking collectives: 102 us -> none  [body(): lax.psum((jnp.sum(query_back * query_unit, axis=(0, 1)), jnp.sum(key_back...]
    all_to_all x0 -> x3, waiting for transfers between devices: none -> 48.2 us  [the longest x1 26.1 us: body(): received = lax.all_to_all(dkv, 'ctx', 0, 0, axis_index_groups=columns)]
    dot_general x28 -> x0, matrix products: 45.4 us -> none  [the longest x4 12.3 us: add_values(): jnp.dot(weights, value_block, preferred_element_type=jnp.float32)]
    all_to_all x0 -> x3, starting transfers between devices: none -> 36.7 us  [the longest x1 16.5 us: body(): lax.all_to_all(jnp.broadcast_to(gains[None, None], (2 * dp, 1, 2 * D)), (...]
    ppermute x0 -> x2, starting transfers between devices: none -> 18.7 us  [the longest x1 11.5 us: body(): kv_other = lax.ppermute(kv_own, 'ctx', swap)]
    pallas_call x0 -> x3, Pallas kernels: none -> 10.7 us  [the longest x1 5.43 us: call_attend(): pl.pallas_call(functools.partial(attend_kernel, heads), out_shape=[jax.Sh...]
  transfers between devices with their start and end apart: 2 -> 5, of which waited for: 2 -> 4; matrix products, arithmetic and copies ran while one was open for 1% -> 1% of each run, Pallas kernels for 0% -> 4%
where the time goes in v1:
time: 128 us; the launch traced here: 127 us
  starting transfers between devices  55.4 us (43%)
  waiting for transfers between devices  51.2 us (40%)
  Pallas kernels  10.7 us (8%)
  local copies, waits for them, and re-layouts  7.43 us (6%)
  other arithmetic  2.01 us (2%)
    all_to_all x1, waiting for transfers between devices, body(): received = lax.all_to_all(dkv, 'ctx', 0, 0, axis_index_groups=columns)  26.1 us
    all_to_all x1, waiting for transfers between devices, body(): lax.all_to_all(jnp.broadcast_to(pair[None], (half, kb, 2 * D)), 'ctx', 0,...  22 us
    all_to_all x1, starting transfers between devices, body(): lax.all_to_all(jnp.broadcast_to(gains[None, None], (2 * dp, 1, 2 * D)), (...  16.5 us
    all_to_all x1, starting transfers between devices, body(): received = lax.all_to_all(dkv, 'ctx', 0, 0, axis_index_groups=columns)  13.3 us
    ppermute x1, starting transfers between devices, body(): kv_other = lax.ppermute(kv_own, 'ctx', swap)  11.5 us
    ppermute x1, starting transfers between devices, body(): other = lax.ppermute(theirs.astype(BF16), 'ctx', swap)  7.2 us
    all_to_all x1, starting transfers between devices, body(): lax.all_to_all(jnp.broadcast_to(pair[None], (half, kb, 2 * D)), 'ctx', 0,...  6.96 us
    pallas_call x1, Pallas kernels, call_attend(): pl.pallas_call(functools.partial(attend_kernel, heads), out_shape=[jax.Sh...  5.43 us
  transfers between devices with their start and end apart: 5, of which 4 were waited for; matrix products, arithmetic and copies ran while one was open for 1% of the time, Pallas kernels for 4%

profile of v1, /device:TPU:1, one launch (start us, length us, event | category | flops | bytes accessed | tf_op | source)
XLA Modules:
  0.0 127.4 jit_solution(575093138768936319)
XLA Ops:
  0.6 0.8 pad_maximum_fusion
  1.4 11.5 %collective-permute-start = (bf16[128,256]{1,0:T(8,128)(2,1)S(1)}, bf16[128,256]{1,0:T(8,128)(2,1)S(1)}, u32[]{:S(2)}, u32[]{:S(2)}) collective-permute-start(bf16[128,256]{1,0:T(8,128)(2,1)S(1)} %pad_maximum_fusion), channel_id=1, source_target_pairs={{0,1},{1,0},{2,3},{3,2},{4,5},{5,4},{6,7},{7,6},{8,9},{9,8},{10,11... | collective-permute-start | bytes 196616 | tf_op jit(solution)/shard_map/ppermute | solution.py:327
  12.9 1.7 %collective-permute-done = bf16[128,256]{1,0:T(8,128)(2,1)S(1)} collective-permute-done((bf16[128,256]{1,0:T(8,128)(2,1)S(1)}, bf16[128,256]{1,0:T(8,128)(2,1)S(1)}, u32[]{:S(2)}, u32[]{:S(2)}) %collective-permute-start) | collective-permute-done | bytes 65568 | tf_op jit(solution)/shard_map/ppermute | solution.py:327
  14.6 0.9 maximum_select_fusion
  15.5 1.0 broadcast_in_dim.37
  16.5 0.0 copy-start.4
  16.5 7.0 %all-to-all-start = ((bf16[8,256,256]{2,1,0:T(8,128)(2,1)}), bf16[8,256,256]{2,1,0:T(8,128)(2,1)S(1)}, u32[]{:S(2)}, u32[]{:S(2)}) async-start(bf16[8,256,256]{2,1,0:T(8,128)(2,1)} %broadcast_in_dim.37), calls=%async_computation | async-start | bytes 2097152 | tf_op jit(solution)/shard_map/all_to_all | solution.py:334
  23.5 0.1 maximum_bitcast_fusion.freq
  23.6 0.0 copy-done
  23.6 0.0 copy-done.1
  23.6 0.0 copy-done.6
  23.6 3.5 %prep.1 = (f32[2048,128]{1,0:T(8,128)S(1)}, f32[2048,128]{1,0:T(8,128)S(1)}, f32[128,128]{1,0:T(8,128)S(1)}, f32[128,128]{1,0:T(8,128)S(1)}, bf16[1024,128]{1,0:...) custom-call(s32[1]{0:T(128)} %bitcast.token_ref, ...), custom_call_target="tpu_custom_call" | custom-call | flops 40000000 | bytes 4000000 | tf_op jit(solution)/shard_map/prep/pallas_call | solution.py:247
  27.1 0.0 copy-start.7
  27.1 1.0 copy-done.7
  28.1 0.7 copy-done.9
  28.8 22.0 %all-to-all-done.kv = bf16[8,256,256]{2,1,0:T(8,128)(2,1)S(1)} async-done(((bf16[8,256,256]{2,1,0:T(8,128)(2,1)}), bf16[8,256,256]{2,1,0:T(8,128)(2,1)S(1)}, u32[]{:S(2)}, u32[]{:S(2)}) %all-to-all-start) | async-done | bytes 1048608 | tf_op jit(solution)/shard_map/all_to_all | solution.py:334
  50.8 1.2 copy-done.8
  52.1 0.9 copy-done.10
  53.0 5.4 %attend.1 = (bf16[128,1024]{1,0:T(8,128)(2,1)}, bf16[128,1024]{1,0:T(8,128)(2,1)}, bf16[8,272,256]{2,1,0:T(8,128)(2,1)}, f32[8,256]{1,0:T(8,128)}) custom-call(s32[1]{0:T(128)} %bitcast.token_ref, s32[1,32]{1,0:T(1,128)S(1)} %copy-done.5, bf16[8,256,256]{2,1,0:T(8,128)(2,1)S(1)} %all-to-all-done.kv, f32[2048,128]{1,0:T(8,128)S(1)} %get-tuple-element.19.cos_ref, ...), custom_call_target="tpu_custom_call" | custom-call | flops 3200000000 | bytes 8000000 | tf_op jit(solution)/shard_map/attend/pallas_call | solution.py:276
  58.4 13.3 %all-to-all-start.1 = ((bf16[8,272,256]{2,1,0:T(8,128)(2,1)}), bf16[8,272,256]{2,1,0:T(8,128)(2,1)S(1)}, u32[]{:S(2)}, u32[]{:S(2)}) async-start(bf16[8,272,256]{2,1,0:T(8,128)(2,1)} %get-tuple-element.29), calls=%async_computation.1 | async-start | bytes 2228224 | tf_op jit(solution)/shard_map/all_to_all | solution.py:340
  71.7 26.1 %all-to-all-done.1 = bf16[8,272,256]{2,1,0:T(8,128)(2,1)S(1)} async-done(((bf16[8,272,256]{2,1,0:T(8,128)(2,1)}), bf16[8,272,256]{2,1,0:T(8,128)(2,1)S(1)}, u32[]{:S(2)}, u32[]{:S(2)}) %all-to-all-start.1) | async-done | bytes 1114144 | tf_op jit(solution)/shard_map/all_to_all | solution.py:340
  97.8 0.7 broadcast_in_dim.45
  98.5 16.5 %all-to-all-start.2 = ((f32[64,1,256]{2,1,0:T(1,128)}), f32[64,1,256]{2,1,0:T(1,128)S(1)}, u32[]{:S(2)}, u32[]{:S(2)}) async-start(f32[64,1,256]{2,1,0:T(1,128)} %broadcast_in_dim.45), calls=%async_computation.2 | async-start | bytes 131072 | tf_op jit(solution)/shard_map/all_to_all | solution.py:349
  115.0 0.1 convert_reduce_fusion
  115.2 7.2 %collective-permute-start.1 = (bf16[128,256]{1,0:T(8,128)(2,1)S(1)}, bf16[128,256]{1,0:T(8,128)(2,1)S(1)}, u32[]{:S(2)}, u32[]{:S(2)}) collective-permute-start(bf16[128,256]{1,0:T(8,128)(2,1)S(1)} %dynamic-slice_convert_fusion), channel_id=1, source_target_pairs={{0,1},{1,0},{2,3},{3,2},{4,5},{5,4},{6,7},{7,6},{8,9},{9,8},{10,11... | collective-permute-start | bytes 196616 | tf_op jit(solution)/shard_map/ppermute | solution.py:345
  122.4 0.7 constant_dynamic-slice_fusion.own_ref
  123.0 1.3 %collective-permute-done.1.other_ref = bf16[128,256]{1,0:T(8,128)(2,1)S(1)} collective-permute-done((bf16[128,256]{1,0:T(8,128)(2,1)S(1)}, bf16[128,256]{1,0:T(8,128)(2,1)S(1)}, u32[]{:S(2)}, u32[]{:S(2)}) %collective-permute-start.1) | collective-permute-done | bytes 65568 | tf_op jit(solution)/shard_map/ppermute | solution.py:345
  124.4 0.6 copy-done.11
  125.0 1.8 %finish.1 = (bf16[128,128]{1,0:T(8,128)(2,1)}, bf16[128,128]{1,0:T(8,128)(2,1)}) custom-call(f32[128,256]{1,0:T(8,128)} %constant_dynamic-slice_fusion.own_ref, bf16[128,256]{1,0:T(8,128)(2,1)} %copy-done.11, bf16[128,128]{1,0:T(8,128)(2,1)} %bitcast.22, f32[1,128]{1,0:T(1,128)} %bitcast.16, f32[128,128]{1,0:T(8,128)} %copy-done.2, f32[128,128]{1,0:T(8,128)} %copy-done.3), custom_call_target="tpu_custom_call" | custom-call | tf_op jit(solution)/shard_map/finish/pallas_call | solution.py:291
  126.8 0.0 all-to-all-done.2
  126.8 0.1 reduce_sum.29
  126.9 0.5 fusion
  (17 shorter events, 0.1 us)
Async XLA Ops:
  1.4 13.2 %collective-permute-start = (bf16[128,256]{1,0:T(8,128)(2,1)S(1)}, bf16[128,256]{1,0:T(8,128)(2,1)S(1)}, u32[]{:S(2)}, u32[]{:S(2)}) collective-permute-start(bf16[128,256]{1,0:T(8,128)(2,1)S(1)} %pad_maximum_fusion), channel_id=1, source_target_pairs={{0,1},{1,0},{2,3},{3,2},{4,5},{5,4},{6,7},{7,6},{8,9},{9,8},{10,11... | collective-permute-start | bytes 196616 | tf_op jit(solution)/shard_map/ppermute | solution.py:327
  16.5 7.1 %copy-start = (bf16[1,128,1024]{2,1,0:T(8,128)(2,1)S(1)}, bf16[1,128,1024]{2,1,0:T(8,128)(2,1)}, u32[]{:S(2)}) copy-start(bf16[1,128,1024]{2,1,0:T(8,128)(2,1)} %param.10) | copy-start | bytes 786436
  16.5 7.1 %copy-start.1 = (bf16[1,128,1024]{2,1,0:T(8,128)(2,1)S(1)}, bf16[1,128,1024]{2,1,0:T(8,128)(2,1)}, u32[]{:S(2)}) copy-start(bf16[1,128,1024]{2,1,0:T(8,128)(2,1)} %param.7) | copy-start | bytes 786436
  16.5 7.1 %copy-start.5 = (s32[1,32]{1,0:T(1,128)S(1)}, s32[1,32]{1,0:T(1,128)}, u32[]{:S(2)}) copy-start(s32[1,32]{1,0:T(1,128)} %lengths.3) | copy-start | bytes 388
  16.5 7.1 %copy-start.6 = (f32[128]{0:T(128)S(1)}, f32[128]{0:T(128)}, u32[]{:S(2)}) copy-start(f32[128]{0:T(128)} %param.12) | copy-start | bytes 1540
  16.5 34.3 %copy-start.4 = (f32[128]{0:T(128)S(1)}, f32[128]{0:T(128)}, u32[]{:S(2)}) copy-start(f32[128]{0:T(128)} %param.13) | copy-start | bytes 1540
  16.5 34.3 %all-to-all-start = ((bf16[8,256,256]{2,1,0:T(8,128)(2,1)}), bf16[8,256,256]{2,1,0:T(8,128)(2,1)S(1)}, u32[]{:S(2)}, u32[]{:S(2)}) async-start(bf16[8,256,256]{2,1,0:T(8,128)(2,1)} %broadcast_in_dim.37), calls=%async_computation | async-start | bytes 2097152 | tf_op jit(solution)/shard_map/all_to_all | solution.py:334
  27.1 1.0 copy-start.7
  28.1 0.7 copy-start.9
  28.8 29.7 %copy-start.2 = (f32[128,128]{1,0:T(8,128)}, f32[128,128]{1,0:T(8,128)S(1)}, u32[]{:S(2)}) copy-start(f32[128,128]{1,0:T(8,128)S(1)} %get-tuple-element.21.cos_own) | copy-start | bytes 196612
  28.8 29.7 %copy-start.3 = (f32[128,128]{1,0:T(8,128)}, f32[128,128]{1,0:T(8,128)S(1)}, u32[]{:S(2)}) copy-start(f32[128,128]{1,0:T(8,128)S(1)} %get-tuple-element.22.sin_own) | copy-start | bytes 196612
  50.8 1.2 copy-start.8
  52.1 0.9 copy-start.10
  58.4 39.4 %all-to-all-start.1 = ((bf16[8,272,256]{2,1,0:T(8,128)(2,1)}), bf16[8,272,256]{2,1,0:T(8,128)(2,1)S(1)}, u32[]{:S(2)}, u32[]{:S(2)}) async-start(bf16[8,272,256]{2,1,0:T(8,128)(2,1)} %get-tuple-element.29), calls=%async_computation.1 | async-start | bytes 2228224 | tf_op jit(solution)/shard_map/all_to_all | solution.py:340
  98.5 28.3 %all-to-all-start.2 = ((f32[64,1,256]{2,1,0:T(1,128)}), f32[64,1,256]{2,1,0:T(1,128)S(1)}, u32[]{:S(2)}, u32[]{:S(2)}) async-start(f32[64,1,256]{2,1,0:T(1,128)} %broadcast_in_dim.45), calls=%async_computation.2 | async-start | bytes 131072 | tf_op jit(solution)/shard_map/all_to_all | solution.py:349
  115.2 9.2 %collective-permute-start.1 = (bf16[128,256]{1,0:T(8,128)(2,1)S(1)}, bf16[128,256]{1,0:T(8,128)(2,1)S(1)}, u32[]{:S(2)}, u32[]{:S(2)}) collective-permute-start(bf16[128,256]{1,0:T(8,128)(2,1)S(1)} %dynamic-slice_convert_fusion), channel_id=1, source_target_pairs={{0,1},{1,0},{2,3},{3,2},{4,5},{5,4},{6,7},{7,6},{8,9},{9,8},{10,11... | collective-permute-start | bytes 196616 | tf_op jit(solution)/shard_map/ppermute | solution.py:345
  124.4 0.6 copy-start.11

commit v2 on v1

v2 whole, which is shorter than its diff:
```python
import functools
import math

import jax
import jax.numpy as jnp
from jax import lax
from jax.experimental import pallas as pl
from jax.experimental.pallas import tpu as pltpu
from jax.sharding import PartitionSpec as P

rope_theta = 1000000.0
norm_epsilon = 1e-06
masked_value = -1e30
D = 128
F32 = jnp.float32
BF16 = jnp.bfloat16
VM = pl.BlockSpec(memory_space=pltpu.VMEM)
SM = pl.BlockSpec(memory_space=pltpu.SMEM)
SCALE = D ** (-0.5)
LOG2E = math.log2(math.e)


def dot(a, b):
    return jnp.dot(a, b, preferred_element_type=F32)


def sin_cos(angle):
    turns = jnp.floor(angle * (2.0 / math.pi) + 0.5)
    r = angle - turns * 1.5703125
    r = r - turns * 4.837512969970703125e-4
    r = r - turns * 7.549789948768648e-8
    r2 = r * r
    s = r + r * r2 * (-1.6666654611e-1 + r2 * (8.3321608736e-3 + r2 * -1.9515295891e-4))
    c = 1.0 - 0.5 * r2 + r2 * r2 * (
        4.166664568298827e-2 + r2 * (-1.388731625493765e-3 + r2 * 2.443315711809948e-5)
    )
    quarter = turns.astype(jnp.int32)
    odd = (quarter & 1) == 1
    sin_part = jnp.where(odd, c, s)
    cos_part = jnp.where(odd, s, c)
    sin_part = jnp.where((quarter & 2) == 2, -sin_part, sin_part)
    cos_part = jnp.where(((quarter + 1) & 2) == 2, -cos_part, cos_part)
    return sin_part, cos_part


def starts_of(lengths, tokens):
    end = jnp.int32(0)
    start = jnp.zeros_like(tokens)
    for d in range(lengths.shape[1]):
        end = end + lengths[0, d]
        start = jnp.where(tokens >= end, end, start)
    return start


def unfold(table):
    turned = pltpu.roll(table, D // 2, 1)
    first_lanes = lax.broadcasted_iota(jnp.int32, table.shape, 1) < D // 2
    return jnp.where(first_lanes, table, turned), jnp.where(first_lanes, -turned, table)


def rotate(x, cosine, sine):
    return x * cosine + pltpu.roll(x, D // 2, 1) * sine


def rotate_back(x, cosine, sine):
    return x * cosine - pltpu.roll(x, D // 2, 1) * sine


def unit_of(raw):
    x = raw.astype(F32)
    inverse = lax.rsqrt(jnp.mean(x * x, axis=1, keepdims=True) + norm_epsilon)
    return x * inverse, inverse


def prep_kernel(
    heads, token_ref, lengths, freq, q_raw, dout, gain_ref,
    table_ref, table_own, q_ref, qt_ref, do_ref, dot_ref, pos_ref,
):
    tokens_own = q_raw.shape[0]
    seq = table_ref.shape[0]
    row = lax.broadcasted_iota(jnp.int32, (D, D), 0)
    lane = lax.broadcasted_iota(jnp.int32, (D, D), 1)
    tokens = row * D + lane
    positions = tokens - starts_of(lengths, tokens)
    pos_ref[...] = positions.astype(F32).T
    first_lanes = lane < D // 2
    for i in range(seq // D):
        angle = pos_ref[:, i : i + 1] * freq[...]
        s, c = sin_cos(angle)
        table_ref[i * D : (i + 1) * D, :] = jnp.where(first_lanes, c, s)
    first = pl.multiple_of(token_ref[0], tokens_own)
    mine = table_ref[pl.ds(first, tokens_own), :]
    table_own[...] = mine
    cosine, sine = unfold(mine)
    for h in range(heads):
        cols = slice(h * D, (h + 1) * D)
        rows = slice(h * tokens_own, (h + 1) * tokens_own)
        unit, _ = unit_of(q_raw[:, cols])
        q = rotate(unit * gain_ref[0:1, :], cosine, sine)
        q_ref[rows, :] = q.astype(BF16)
        qt_ref[:, rows] = q.T.astype(BF16)
        g = dout[:, cols]
        do_ref[rows, :] = g
        dot_ref[:, rows] = g.astype(F32).T.astype(BF16)


def attend_kernel(
    heads, token_ref, lengths, kv_own, kv_other, table_ref, table_own, q_ref, qt_ref, do_ref, dot_ref,
    q_raw, gain_ref,
    out_ref, dq_ref, dkv_ref, gains_ref,
    s_buf, k_buf, kt_buf, vt_buf, ot_buf, dqt_buf, max_buf, sum_buf, row_buf, kg_buf,
):
    blocks, tokens_own, _ = kv_own.shape
    kb = 2 * tokens_own
    cols_all = heads * tokens_own
    cc = 2 * tokens_own
    chunks = cols_all // cc
    first = token_ref[0]
    end = jnp.int32(0)
    low = jnp.int32(0)
    for d in range(lengths.shape[1]):
        end = end + lengths[0, d]
        low = jnp.where(end <= first, end, low)
    lo = low // kb
    hi = (first + tokens_own - 1) // kb + 1
    tok = first + lax.broadcasted_iota(jnp.int32, (8, tokens_own), 1)
    start_row = starts_of(lengths, tok)[:1]
    tok_row = tok[:1]
    dkv_ref[...] = jnp.zeros_like(dkv_ref)
    max_buf[...] = jnp.full_like(max_buf, masked_value)
    sum_buf[...] = jnp.zeros_like(sum_buf)
    ot_buf[...] = jnp.zeros_like(ot_buf)
    dqt_buf[...] = jnp.zeros_like(dqt_buf)
    kg_buf[...] = jnp.zeros_like(kg_buf)
    factor = SCALE * LOG2E

    side = (first // tokens_own) % 2

    def tables(b):
        start = b * kb
        own = pl.multiple_of(start + side * tokens_own, tokens_own)
        other = pl.multiple_of(start + (1 - side) * tokens_own, tokens_own)
        rows = [table_ref[pl.ds(own, tokens_own), :], table_ref[pl.ds(other, tokens_own), :]]
        return unfold(jnp.concatenate(rows, 0))

    def keys_of(b):
        return jnp.concatenate([kv_own[b, :, :D], kv_other[b, :, :D]], 0)

    def values_of(b):
        return jnp.concatenate([kv_own[b, :, D:], kv_other[b, :, D:]], 0)

    row = lax.broadcasted_iota(jnp.int32, (kb, tokens_own), 0)
    key_shift = row + jnp.where(row < tokens_own, side * tokens_own, -side * tokens_own)

    def scores_step(b, carry):
        unit, _ = unit_of(keys_of(b))
        k = rotate(unit * gain_ref[1:2, :], *tables(b))
        k_rows = k.astype(BF16)
        k_buf[b] = k_rows
        kt_buf[b] = k.T.astype(BF16)
        vt_buf[b] = values_of(b).astype(F32).T.astype(BF16)
        key = b * kb + key_shift
        allowed = (key >= start_row) & (key <= tok_row)
        bias = jnp.where(allowed, 0.0, masked_value)
        for c in range(chunks):
            cs = slice(c * cc, (c + 1) * cc)
            s = dot(k_rows, qt_ref[:, cs]) * factor + jnp.concatenate([bias, bias], 1)
            s_buf[b, :, cs] = s
            max_buf[:, cs] = jnp.maximum(max_buf[:, cs], jnp.max(s.reshape(kb // 8, 8, cc), axis=0))
        return carry

    lax.fori_loop(lo, hi, scores_step, 0)
    row_buf[:1, :] = jnp.max(max_buf[...], axis=0, keepdims=True)

    def exp_step(b, carry):
        for c in range(chunks):
            cs = slice(c * cc, (c + 1) * cc)
            e = jnp.exp2(s_buf[b, :, cs] - row_buf[:1, cs])
            s_buf[b, :, cs] = e
            sum_buf[:, cs] += jnp.sum(e.reshape(kb // 8, 8, cc), axis=0)
            ot_buf[:, cs] += dot(vt_buf[b], e.astype(BF16))
        return carry

    lax.fori_loop(lo, hi, exp_step, 0)
    sum_buf[:1, :] = 1.0 / jnp.sum(sum_buf[...], axis=0, keepdims=True)
    for h in range(heads):
        hs = slice(h * tokens_own, (h + 1) * tokens_own)
        ot = (ot_buf[:, hs] * sum_buf[:1, hs]).astype(BF16).astype(F32)
        out_ref[:, h * D : (h + 1) * D] = ot.T.astype(BF16)
        row_buf[:1, hs] = jnp.sum(ot * dot_ref[:, hs].astype(F32), axis=0, keepdims=True)

    def back_step(b, carry):
        dk = jnp.zeros((kb, D), F32)
        dv = jnp.zeros((kb, D), F32)
        v_rows = values_of(b)
        for c in range(chunks):
            cs = slice(c * cc, (c + 1) * cc)
            dp = dot(v_rows, dot_ref[:, cs])
            prob = s_buf[b, :, cs] * sum_buf[:1, cs]
            dv = dv + dot(prob.astype(BF16), do_ref[cs, :])
            ds = (prob * (dp - row_buf[:1, cs])).astype(BF16)
            dk = dk + dot(ds, q_ref[cs, :])
            dqt_buf[:, cs] += dot(kt_buf[b], ds)
        dk = dk * SCALE
        dkv_ref[b, :, :D] = dk.astype(BF16)
        dkv_ref[b, :, D:] = dv.astype(BF16)
        unit, _ = unit_of(keys_of(b))
        terms = rotate_back(dk, *tables(b)) * unit
        kg_buf[...] += jnp.sum(terms.reshape(kb // 8, 8, D), axis=0)
        return carry

    lax.fori_loop(lo, hi, back_step, 0)
    cosine, sine = unfold(table_own[...])
    q_sum = jnp.zeros((8, D), F32)
    for h in range(heads):
        hs = slice(h * tokens_own, (h + 1) * tokens_own)
        back = rotate_back(dqt_buf[:, hs].T * SCALE, cosine, sine)
        unit, inverse = unit_of(q_raw[:, h * D : (h + 1) * D])
        q_sum = q_sum + jnp.sum((back * unit).reshape(tokens_own // 8, 8, D), axis=0)
        scaled = back * gain_ref[0:1, :]
        mean = jnp.mean(scaled * unit, axis=1, keepdims=True)
        dq_ref[:, h * D : (h + 1) * D] = (inverse * (scaled - unit * mean)).astype(BF16)
    gains_ref[:, :D] = jnp.broadcast_to(jnp.sum(q_sum, axis=0, keepdims=True), (8, D))
    gains_ref[:, D:] = jnp.broadcast_to(jnp.sum(kg_buf[...], axis=0, keepdims=True), (8, D))


def finish_kernel(own_ref, other_ref, k_raw, gain_ref, table_own, dk_ref, dv_ref):
    total = own_ref[...] + other_ref[...].astype(F32)
    unit, inverse = unit_of(k_raw[...])
    back = rotate_back(total[:, :D], *unfold(table_own[...]))
    scaled = back * gain_ref[1:2, :]
    mean = jnp.mean(scaled * unit, axis=1, keepdims=True)
    dk_ref[...] = (inverse * (scaled - unit * mean)).astype(BF16)
    dv_ref[...] = total[:, D:].astype(BF16)


def call_prep(token, lengths, freq, q_raw, dout, both_gains, seq, **kw):
    tokens_own, width = q_raw.shape
    heads = width // D
    rows = heads * tokens_own
    shapes = [
        ((seq, D), F32), ((tokens_own, D), F32),
        ((rows, D), BF16), ((D, rows), BF16), ((rows, D), BF16), ((D, rows), BF16),
    ]
    return pl.pallas_call(
        functools.partial(prep_kernel, heads),
        out_shape=[jax.ShapeDtypeStruct(s, t) for s, t in shapes],
        in_specs=[SM, SM, VM, VM, VM, VM],
        out_specs=[VM] * len(shapes),
        scratch_shapes=[pltpu.VMEM((D, D), F32)],
        compiler_params=pltpu.CompilerParams(vmem_limit_bytes=12 * 2**20),
        cost_estimate=pl.CostEstimate(flops=40_000_000, bytes_accessed=4_000_000, transcendentals=0),
        name="prep",
        **kw,
    )(token, lengths, freq, q_raw, dout, both_gains)


def call_attend(token, lengths, kv_own, kv_other, prepared, q_raw, both_gains, **kw):
    tokens_own, width = q_raw.shape
    heads = width // D
    blocks = kv_own.shape[0]
    kb = 2 * tokens_own
    rows = heads * tokens_own
    shapes = [
        ((tokens_own, width), BF16), ((tokens_own, width), BF16), ((blocks, kb, 2 * D), BF16), ((8, 2 * D), F32),
    ]
    scratch = [
        pltpu.VMEM((blocks, kb, rows), F32),
        pltpu.VMEM((blocks, kb, D), BF16), pltpu.VMEM((blocks, D, kb), BF16),
        pltpu.VMEM((blocks, D, kb), BF16), pltpu.VMEM((D, rows), F32), pltpu.VMEM((D, rows), F32),
        pltpu.VMEM((8, rows), F32), pltpu.VMEM((8, rows), F32), pltpu.VMEM((8, rows), F32),
        pltpu.VMEM((8, D), F32),
    ]
    return pl.pallas_call(
        functools.partial(attend_kernel, heads),
        out_shape=[jax.ShapeDtypeStruct(s, t) for s, t in shapes],
        in_specs=[SM, SM] + [VM] * 10,
        out_specs=[VM] * len(shapes),
        scratch_shapes=scratch,
        compiler_params=pltpu.CompilerParams(vmem_limit_bytes=20 * 2**20),
        cost_estimate=pl.CostEstimate(flops=3_200_000_000, bytes_accessed=8_000_000, transcendentals=2_000_000),
        name="attend",
        **kw,
    )(token, lengths, kv_own, kv_other, *prepared, q_raw, both_gains)


def call_finish(own, other, k_raw, both_gains, table_own, **kw):
    shape = jax.ShapeDtypeStruct(k_raw.shape, BF16)
    return pl.pallas_call(
        finish_kernel,
        out_shape=[shape, shape],
        in_specs=[VM] * 5,
        out_specs=[VM] * 2,
        name="finish",
        **kw,
    )(own, other, k_raw, both_gains, table_own)


def frequency_row():
    exponent = jnp.arange(D // 2, dtype=F32) * (2.0 / D)
    frequency = jnp.power(F32(rope_theta), -exponent)
    return jnp.concatenate([frequency, frequency])[None, :]


def strided(size, stride, count):
    span = stride * count
    return [
        [base + low + stride * k for k in range(count)]
        for base in range(0, size, span)
        for low in range(stride)
    ]


def body(query_raw, key_raw, values, out_grad, doc_lengths, query_gain, key_gain):
    tokens_own = query_raw.shape[1]
    ctx = lax.axis_size("ctx")
    dp = lax.axis_size("dp")
    seq = tokens_own * ctx
    half = ctx // 2
    me = lax.axis_index("ctx")
    token = (me * tokens_own)[None].astype(jnp.int32)
    both_gains = jnp.stack([query_gain, key_gain] * 4)
    columns = [[2 * y + z for y in range(half)] for z in range(2)]
    swap = [(i, i ^ 1) for i in range(ctx)]

    def exchange(blocks):
        return lax.all_to_all(blocks, "ctx", 0, 0, axis_index_groups=columns)

    def spread(rows):
        return jnp.broadcast_to(rows[None], (half,) + rows.shape)

    kv = jnp.concatenate([key_raw[0], values[0]], axis=1)
    kv_swapped = lax.ppermute(kv, "ctx", swap)
    kv_own = exchange(spread(kv))
    kv_other = exchange(spread(kv_swapped))
    prepared = call_prep(token, doc_lengths, frequency_row(), query_raw[0], out_grad[0], both_gains, seq)
    output, dq, parts, gains = call_attend(
        token, doc_lengths, kv_own, kv_other, prepared, query_raw[0], both_gains
    )
    received = exchange(parts)
    own = jnp.sum(received[:, :tokens_own].astype(F32), axis=0)
    theirs = jnp.sum(received[:, tokens_own:].astype(F32), axis=0).astype(BF16)
    gains = lax.psum(gains[0], "dp", axis_index_groups=strided(dp, 1, 2))
    gains = lax.psum(gains, "dp", axis_index_groups=strided(dp, 8, dp // 8))
    gains = lax.psum(gains, "ctx", axis_index_groups=strided(ctx, 1, 2))
    other = lax.ppermute(theirs, "ctx", swap)
    own, gains = lax.optimization_barrier((own, gains))
    groups = [
        [(8 * x + 2 * z + core) * ctx + 2 * y + side for z in range(4) for y in range(half)]
        for x in range(dp // 8) for core in range(2) for side in range(2)
    ]
    gains = lax.all_to_all(
        jnp.broadcast_to(gains[None, None], (4 * half, 1, 2 * D)), ("dp", "ctx"), 0, 0, axis_index_groups=groups
    )
    gains = jnp.sum(gains, axis=(0, 1))
    dk, dv = call_finish(own, other, key_raw[0], both_gains, prepared[1])
    return (output[None], dq[None], dk[None], dv[None], gains[:D], gains[D:])


def solution(mesh):
    return jax.shard_map(
        body,
        mesh=mesh,
        in_specs=(
            P("dp", "ctx", None),
            P("dp", "ctx", None),
            P("dp", "ctx", None),
            P("dp", "ctx", None),
            P("dp", None),
            P(),
            P(),
        ),
        out_specs=(
            P("dp", "ctx", None),
            P("dp", "ctx", None),
            P("dp", "ctx", None),
            P("dp", "ctx", None),
            P(),
            P(),
        ),
        check_vma=False,
    )
```

time: 128 us -> 121 us (0.945)
  waiting for transfers between devices: 51.2 us -> 14.4 us
  blocking collectives: 0 us -> 35.7 us
  starting transfers between devices: 55.4 us -> 50.3 us
    all_to_all x3 -> x4, waiting for transfers between devices: 48.2 us -> 12.2 us  [the longest x3 11.2 us: exchange(): return lax.all_to_all(blocks, 'ctx', 0, 0, axis_index_groups=columns)]
    psum x0 -> x3, blocking collectives: none -> 35.7 us  [the longest x1 18.8 us: body(): gains = lax.psum(gains, 'dp', axis_index_groups=strided(dp, 8, dp // 8))]
    all_to_all x3 -> x4, starting transfers between devices: 36.7 us -> 31.7 us  [the longest x3 18.2 us: exchange(): return lax.all_to_all(blocks, 'ctx', 0, 0, axis_index_groups=columns)]
    unnamed x24 -> x20, local copies, waits for them, and re-layouts: 4.51 us -> 3.59 us
  transfers between devices with their start and end apart: 5 -> 6, of which waited for: 4 -> 5; matrix products, arithmetic and copies ran while one was open for 1% -> 1% of each run, Pallas kernels for 4% -> 3%
where the time goes in v2:
time: 121 us; the launch traced here: 120 us
  starting transfers between devices  50.3 us (42%)
  blocking collectives  35.7 us (30%)
  waiting for transfers between devices  14.4 us (12%)
  Pallas kernels  10.6 us (9%)
  local copies, waits for them, and re-layouts  6.43 us (5%)
  other arithmetic  1.71 us (1%)
    psum x1, blocking collectives, body(): gains = lax.psum(gains, 'dp', axis_index_groups=strided(dp, 8, dp // 8))  18.8 us
    all_to_all x3, starting transfers between devices, exchange(): return lax.all_to_all(blocks, 'ctx', 0, 0, axis_index_groups=columns)  18.2 us
    all_to_all x1, starting transfers between devices, body(): lax.all_to_all(jnp.broadcast_to(gains[None, None], (4 * half, 1, 2 * D)),...  13.5 us
    psum x1, blocking collectives, body(): gains = lax.psum(gains, 'ctx', axis_index_groups=strided(ctx, 1, 2))  11.3 us
    all_to_all x3, waiting for transfers between devices, exchange(): return lax.all_to_all(blocks, 'ctx', 0, 0, axis_index_groups=columns)  11.2 us
    ppermute x1, starting transfers between devices, body(): kv_swapped = lax.ppermute(kv, 'ctx', swap)  10.6 us
    ppermute x1, starting transfers between devices, body(): other = lax.ppermute(theirs, 'ctx', swap)  7.95 us
    psum x1, blocking collectives, body(): gains = lax.psum(gains[0], 'dp', axis_index_groups=strided(dp, 1, 2))  5.6 us
  transfers between devices with their start and end apart: 6, of which 5 were waited for; matrix products, arithmetic and copies ran while one was open for 1% of the time, Pallas kernels for 3%

profile of v2, /device:TPU:1, one launch (start us, length us, event | category | flops | bytes accessed | tf_op | source)
XLA Modules:
  0.0 119.8 jit_solution(2221275170312509864)
XLA Ops:
  0.6 0.8 pad_maximum_fusion
  1.4 0.8 broadcast_in_dim.37
  2.2 7.7 %all-to-all-start = ((bf16[8,128,256]{2,1,0:T(8,128)(2,1)}), bf16[8,128,256]{2,1,0:T(8,128)(2,1)S(1)}, u32[]{:S(2)}, u32[]{:S(2)}) async-start(bf16[8,128,256]{2,1,0:T(8,128)(2,1)} %broadcast_in_dim.37), calls=%async_computation | async-start | bytes 1048576 | tf_op jit(solution)/shard_map/all_to_all | solution.py:327
  9.9 10.6 %collective-permute-start = (bf16[128,256]{1,0:T(8,128)(2,1)S(1)}, bf16[128,256]{1,0:T(8,128)(2,1)S(1)}, u32[]{:S(2)}, u32[]{:S(2)}) collective-permute-start(bf16[128,256]{1,0:T(8,128)(2,1)S(1)} %pad_maximum_fusion), channel_id=1, source_target_pairs={{0,1},{1,0},{2,3},{3,2},{4,5},{5,4},{6,7},{7,6},{8,9},{9,8},{10,11... | collective-permute-start | bytes 196616 | tf_op jit(solution)/shard_map/ppermute | solution.py:333
  20.5 1.7 %collective-permute-done = bf16[128,256]{1,0:T(8,128)(2,1)S(1)} collective-permute-done((bf16[128,256]{1,0:T(8,128)(2,1)S(1)}, bf16[128,256]{1,0:T(8,128)(2,1)S(1)}, u32[]{:S(2)}, u32[]{:S(2)}) %collective-permute-start) | collective-permute-done | bytes 65568 | tf_op jit(solution)/shard_map/ppermute | solution.py:333
  22.2 2.4 %all-to-all-done.kv_own = bf16[8,128,256]{2,1,0:T(8,128)(2,1)S(1)} async-done(((bf16[8,128,256]{2,1,0:T(8,128)(2,1)}), bf16[8,128,256]{2,1,0:T(8,128)(2,1)S(1)}, u32[]{:S(2)}, u32[]{:S(2)}) %all-to-all-start) | async-done | bytes 524320 | tf_op jit(solution)/shard_map/all_to_all | solution.py:327
  24.6 0.8 broadcast_in_dim.38
  25.5 4.4 %all-to-all-start.1 = ((bf16[8,128,256]{2,1,0:T(8,128)(2,1)}), bf16[8,128,256]{2,1,0:T(8,128)(2,1)S(1)}, u32[]{:S(2)}, u32[]{:S(2)}) async-start(bf16[8,128,256]{2,1,0:T(8,128)(2,1)} %broadcast_in_dim.38), calls=%async_computation.1 | async-start | bytes 1048576 | tf_op jit(solution)/shard_map/all_to_all | solution.py:327
  29.9 0.6 copy-done.8
  30.5 0.0 copy-done.9
  30.6 0.1 maximum_bitcast_fusion.freq
  30.7 0.7 copy-done.4
  31.3 3.5 %prep.1 = (f32[2048,128]{1,0:T(8,128)S(1)}, f32[128,128]{1,0:T(8,128)S(1)}, bf16[1024,128]{1,0:T(8,128)(2,1)S(1)}, bf16[128,1024]{1,0:T(8,128)(2,1)S(1)}, bf16[1...) custom-call(s32[1]{0:T(128)} %bitcast.token_ref, s32[1,32]{1,0:T(1,128)S(1)} %copy-done.4, ...), custom_call_target="tpu_custom_call" | custom-call | flops 40000000 | bytes 4000000 | tf_op jit(solution)/shard_map/prep/pallas_call | solution.py:245
  34.9 0.7 copy-done.5
  35.6 8.8 %all-to-all-done.1.kv_other = bf16[8,128,256]{2,1,0:T(8,128)(2,1)S(1)} async-done(((bf16[8,128,256]{2,1,0:T(8,128)(2,1)}), bf16[8,128,256]{2,1,0:T(8,128)(2,1)S(1)}, u32[]{:S(2)}, u32[]{:S(2)}) %all-to-all-start.1) | async-done | bytes 524320 | tf_op jit(solution)/shard_map/all_to_all | solution.py:327
  44.4 0.9 copy-done.6
  45.3 5.3 %attend.1 = (bf16[128,1024]{1,0:T(8,128)(2,1)}, bf16[128,1024]{1,0:T(8,128)(2,1)}, bf16[8,256,256]{2,1,0:T(8,128)(2,1)}, f32[8,256]{1,0:T(8,128)S(1)}) custom-call(s32[1]{0:T(128)} %bitcast.token_ref, s32[1,32]{1,0:T(1,128)S(1)} %copy-done.4, bf16[8,128,256]{2,1,0:T(8,128)(2,1)S(1)} %all-to-all-done.kv_own, ...), custom_call_target="tpu_custom_call" | custom-call | flops 3200000000 | bytes 8000000 | tf_op jit(solution)/shard_map/attend/pallas_call | solution.py:274
  50.7 6.2 %all-to-all-start.2 = ((bf16[8,256,256]{2,1,0:T(8,128)(2,1)}), bf16[8,256,256]{2,1,0:T(8,128)(2,1)S(1)}, u32[]{:S(2)}, u32[]{:S(2)}) async-start(bf16[8,256,256]{2,1,0:T(8,128)(2,1)} %get-tuple-element.28), calls=%async_computation.2 | async-start | bytes 2097152 | tf_op jit(solution)/shard_map/all_to_all | solution.py:327
  56.9 5.6 %psum.21 = f32[256]{0:T(256)S(1)} all-reduce(f32[256]{0:T(256)S(1)} %bitcast.28), channel_id=1, replica_groups={{0,16},{32,48},{64,80},{96,112},{128,144},{160,176},{192,208},{224,240}..., use_global_device_ids=true, to_apply=%region_1.0 | all-reduce | flops 256 | bytes 2048 | tf_op jit(solution)/shard_map/psum | solution.py:343
  62.5 18.8 %psum.22 = f32[256]{0:T(256)S(1)} all-reduce(f32[256]{0:T(256)S(1)} %psum.21), channel_id=1, replica_groups={{0,128,256,384},{16,144,272,400},{32,160,288,416},{48,176,304,432},{64,..., use_global_device_ids=true, to_apply=%region_2.0 | all-reduce | flops 256 | bytes 2048 | tf_op jit(solution)/shard_map/psum | solution.py:344
  81.2 11.3 %psum.23 = f32[256]{0:T(256)S(1)} all-reduce(f32[256]{0:T(256)S(1)} %psum.22), channel_id=1, replica_groups={{0,1},{2,3},{4,5},{6,7},{8,9},{10,11},{12,13},{14,15},{16,17},{18,19},{..., use_global_device_ids=true, to_apply=%region_3.0 | all-reduce | flops 256 | bytes 2048 | tf_op jit(solution)/shard_map/psum | solution.py:345
  92.5 0.7 convert_reduce_fusion.own_ref
  93.2 0.6 broadcast_in_dim.44
  93.9 13.5 %all-to-all-start.3 = ((f32[32,1,256]{2,1,0:T(1,128)}), f32[32,1,256]{2,1,0:T(1,128)S(1)}, u32[]{:S(2)}, u32[]{:S(2)}) async-start(f32[32,1,256]{2,1,0:T(1,128)} %broadcast_in_dim.44), calls=%async_computation.3 | async-start | bytes 65536 | tf_op jit(solution)/shard_map/all_to_all | solution.py:352
  107.3 0.1 slice_reduce_fusion
  107.4 7.9 %collective-permute-start.1 = (bf16[128,256]{1,0:T(8,128)(2,1)S(1)}, bf16[128,256]{1,0:T(8,128)(2,1)S(1)}, u32[]{:S(2)}, u32[]{:S(2)}) collective-permute-start(bf16[128,256]{1,0:T(8,128)(2,1)S(1)} %slice_reduce_fusion), channel_id=1, source_target_pairs={{0,1},{1,0},{2,3},{3,2},{4,5},{5,4},{6,7},{7,6},{8,9},{9,8},{10,11... | collective-permute-start | bytes 196616 | tf_op jit(solution)/shard_map/ppermute | solution.py:346
  115.4 1.0 all-to-all-done.3
  116.4 0.1 reduce_sum.32
  116.4 0.5 fusion
  116.9 0.4 collective-permute-done.1.other_ref
  117.4 0.6 copy-done.7
  118.0 1.8 %finish.1 = (bf16[128,128]{1,0:T(8,128)(2,1)}, bf16[128,128]{1,0:T(8,128)(2,1)}) custom-call(f32[128,256]{1,0:T(8,128)} %convert_reduce_fusion.own_ref, bf16[128,256]{1,0:T(8,128)(2,1)} %copy-done.7, bf16[128,128]{1,0:T(8,128)(2,1)} %bitcast.18, f32[8,128]{1,0:T(8,128)} %copy-done.3, f32[128,128]{1,0:T(8,128)} %copy-done.2), custom_call_target="tpu_custom_call" | custom-call | tf_op jit(solution)/shard_map/finish/pallas_call | solution.py:289
  (18 shorter events, 0.1 us)
Async XLA Ops:
  2.2 22.4 %all-to-all-start = ((bf16[8,128,256]{2,1,0:T(8,128)(2,1)}), bf16[8,128,256]{2,1,0:T(8,128)(2,1)S(1)}, u32[]{:S(2)}, u32[]{:S(2)}) async-start(bf16[8,128,256]{2,1,0:T(8,128)(2,1)} %broadcast_in_dim.37), calls=%async_computation | async-start | bytes 1048576 | tf_op jit(solution)/shard_map/all_to_all | solution.py:327
  9.9 12.3 %collective-permute-start = (bf16[128,256]{1,0:T(8,128)(2,1)S(1)}, bf16[128,256]{1,0:T(8,128)(2,1)S(1)}, u32[]{:S(2)}, u32[]{:S(2)}) collective-permute-start(bf16[128,256]{1,0:T(8,128)(2,1)S(1)} %pad_maximum_fusion), channel_id=1, source_target_pairs={{0,1},{1,0},{2,3},{3,2},{4,5},{5,4},{6,7},{7,6},{8,9},{9,8},{10,11... | collective-permute-start | bytes 196616 | tf_op jit(solution)/shard_map/ppermute | solution.py:333
  25.5 5.2 %copy-start = (bf16[1,128,1024]{2,1,0:T(8,128)(2,1)S(1)}, bf16[1,128,1024]{2,1,0:T(8,128)(2,1)}, u32[]{:S(2)}) copy-start(bf16[1,128,1024]{2,1,0:T(8,128)(2,1)} %param.10) | copy-start | bytes 786436
  25.5 5.2 %copy-start.1 = (bf16[1,128,1024]{2,1,0:T(8,128)(2,1)S(1)}, bf16[1,128,1024]{2,1,0:T(8,128)(2,1)}, u32[]{:S(2)}) copy-start(bf16[1,128,1024]{2,1,0:T(8,128)(2,1)} %param.7) | copy-start | bytes 786436
  25.5 18.9 %all-to-all-start.1 = ((bf16[8,128,256]{2,1,0:T(8,128)(2,1)}), bf16[8,128,256]{2,1,0:T(8,128)(2,1)S(1)}, u32[]{:S(2)}, u32[]{:S(2)}) async-start(bf16[8,128,256]{2,1,0:T(8,128)(2,1)} %broadcast_in_dim.38), calls=%async_computation.1 | async-start | bytes 1048576 | tf_op jit(solution)/shard_map/all_to_all | solution.py:327
  29.9 0.7 copy-start.8
  29.9 0.7 copy-start.9
  30.6 13.8 %copy-start.3 = (f32[8,128]{1,0:T(8,128)}, f32[8,128]{1,0:T(8,128)S(1)}, u32[]{:S(2)}) copy-start(f32[8,128]{1,0:T(8,128)S(1)} %stack.8.gain_ref) | copy-start | bytes 12292
  30.6 0.7 copy-start.4
  34.8 0.7 copy-start.5
  35.6 15.1 %copy-start.2 = (f32[128,128]{1,0:T(8,128)}, f32[128,128]{1,0:T(8,128)S(1)}, u32[]{:S(2)}) copy-start(f32[128,128]{1,0:T(8,128)S(1)} %get-tuple-element.21.table_own) | copy-start | bytes 196612
  44.4 1.0 copy-start.6
  50.7 41.9 %all-to-all-start.2 = ((bf16[8,256,256]{2,1,0:T(8,128)(2,1)}), bf16[8,256,256]{2,1,0:T(8,128)(2,1)S(1)}, u32[]{:S(2)}, u32[]{:S(2)}) async-start(bf16[8,256,256]{2,1,0:T(8,128)(2,1)} %get-tuple-element.28), calls=%async_computation.2 | async-start | bytes 2097152 | tf_op jit(solution)/shard_map/all_to_all | solution.py:327
  93.9 22.5 %all-to-all-start.3 = ((f32[32,1,256]{2,1,0:T(1,128)}), f32[32,1,256]{2,1,0:T(1,128)S(1)}, u32[]{:S(2)}, u32[]{:S(2)}) async-start(f32[32,1,256]{2,1,0:T(1,128)} %broadcast_in_dim.44), calls=%async_computation.3 | async-start | bytes 65536 | tf_op jit(solution)/shard_map/all_to_all | solution.py:352
  107.4 10.0 %collective-permute-start.1 = (bf16[128,256]{1,0:T(8,128)(2,1)S(1)}, bf16[128,256]{1,0:T(8,128)(2,1)S(1)}, u32[]{:S(2)}, u32[]{:S(2)}) collective-permute-start(bf16[128,256]{1,0:T(8,128)(2,1)S(1)} %slice_reduce_fusion), channel_id=1, source_target_pairs={{0,1},{1,0},{2,3},{3,2},{4,5},{5,4},{6,7},{7,6},{8,9},{9,8},{10,11... | collective-permute-start | bytes 196616 | tf_op jit(solution)/shard_map/ppermute | solution.py:346
  117.4 0.6 copy-start.7

commit v3 on v2

--- a/solution.py
+++ b/solution.py
@@ -110,10 +110,11 @@
     out_ref, dq_ref, dkv_ref, gains_ref,
     s_buf, k_buf, kt_buf, vt_buf, ot_buf, dqt_buf, max_buf, sum_buf, row_buf, kg_buf,
 ):
-    blocks, tokens_own, _ = kv_own.shape
-    kb = 2 * tokens_own
+    _, tokens_own, _ = kv_own.shape
+    kb = 4 * tokens_own
+    blocks = kv_own.shape[0] // 2
     cols_all = heads * tokens_own
-    cc = 2 * tokens_own
+    cc = cols_all
     chunks = cols_all // cc
     first = token_ref[0]
     end = jnp.int32(0)
@@ -137,20 +138,21 @@
     side = (first // tokens_own) % 2
 
     def tables(b):
-        start = b * kb
-        own = pl.multiple_of(start + side * tokens_own, tokens_own)
-        other = pl.multiple_of(start + (1 - side) * tokens_own, tokens_own)
-        rows = [table_ref[pl.ds(own, tokens_own), :], table_ref[pl.ds(other, tokens_own), :]]
+        rows = []
+        for i in range(2):
+            for s in (side, 1 - side):
+                start = b * kb + (2 * i + s) * tokens_own
+                rows.append(table_ref[pl.ds(pl.multiple_of(start, tokens_own), tokens_own), :])
         return unfold(jnp.concatenate(rows, 0))
 
     def keys_of(b):
-        return jnp.concatenate([kv_own[b, :, :D], kv_other[b, :, :D]], 0)
+        return jnp.concatenate([kv_own[2 * b, :, :D], kv_other[2 * b, :, :D], kv_own[2 * b + 1, :, :D], kv_other[2 * b + 1, :, :D]], 0)
 
     def values_of(b):
-        return jnp.concatenate([kv_own[b, :, D:], kv_other[b, :, D:]], 0)
+        return jnp.concatenate([kv_own[2 * b, :, D:], kv_other[2 * b, :, D:], kv_own[2 * b + 1, :, D:], kv_other[2 * b + 1, :, D:]], 0)
 
     row = lax.broadcasted_iota(jnp.int32, (kb, tokens_own), 0)
-    key_shift = row + jnp.where(row < tokens_own, side * tokens_own, -side * tokens_own)
+    key_shift = row + jnp.where(row % (2 * tokens_own) < tokens_own, side * tokens_own, -side * tokens_own)
 
     def scores_step(b, carry):
         unit, _ = unit_of(keys_of(b))
@@ -164,7 +166,7 @@
         bias = jnp.where(allowed, 0.0, masked_value)
         for c in range(chunks):
             cs = slice(c * cc, (c + 1) * cc)
-            s = dot(k_rows, qt_ref[:, cs]) * factor + jnp.concatenate([bias, bias], 1)
+            s = dot(k_rows, qt_ref[:, cs]) * factor + jnp.concatenate([bias] * (cc // tokens_own), 1)
             s_buf[b, :, cs] = s
             max_buf[:, cs] = jnp.maximum(max_buf[:, cs], jnp.max(s.reshape(kb // 8, 8, cc), axis=0))
         return carry
@@ -202,8 +204,10 @@
             dk = dk + dot(ds, q_ref[cs, :])
             dqt_buf[:, cs] += dot(kt_buf[b], ds)
         dk = dk * SCALE
-        dkv_ref[b, :, :D] = dk.astype(BF16)
-        dkv_ref[b, :, D:] = dv.astype(BF16)
+        for i in range(2):
+            half = slice(i * 2 * tokens_own, (i + 1) * 2 * tokens_own)
+            dkv_ref[2 * b + i, :, :D] = dk[half].astype(BF16)
+            dkv_ref[2 * b + i, :, D:] = dv[half].astype(BF16)
         unit, _ = unit_of(keys_of(b))
         terms = rotate_back(dk, *tables(b)) * unit
         kg_buf[...] += jnp.sum(terms.reshape(kb // 8, 8, D), axis=0)
@@ -258,11 +262,11 @@
 def call_attend(token, lengths, kv_own, kv_other, prepared, q_raw, both_gains, **kw):
     tokens_own, width = q_raw.shape
     heads = width // D
-    blocks = kv_own.shape[0]
-    kb = 2 * tokens_own
+    blocks = kv_own.shape[0] // 2
+    kb = 4 * tokens_own
     rows = heads * tokens_own
     shapes = [
-        ((tokens_own, width), BF16), ((tokens_own, width), BF16), ((blocks, kb, 2 * D), BF16), ((8, 2 * D), F32),
+        ((tokens_own, width), BF16), ((tokens_own, width), BF16), ((2 * blocks, kb // 2, 2 * D), BF16), ((8, 2 * D), F32),
     ]
     scratch = [
         pltpu.VMEM((blocks, kb, rows), F32),
@@ -291,6 +295,7 @@
         out_shape=[shape, shape],
         in_specs=[VM] * 5,
         out_specs=[VM] * 2,
+        cost_estimate=pl.CostEstimate(flops=0, bytes_accessed=100_000_000, transcendentals=0),
         name="finish",
         **kw,
     )(own, other, k_raw, both_gains, table_own)

time: 121 us -> 118 us (0.975)
  blocking collectives: 35.7 us -> 32.1 us
    psum x1, blocking collectives: 18.8 us -> 15.5 us  [body(): gains = lax.psum(gains, 'dp', axis_index_groups=strided(dp, 8, dp // 8))]
    all_to_all x1, starting transfers between devices: 13.5 us -> 14.7 us  [body(): lax.all_to_all(jnp.broadcast_to(gains[None, None], (4 * half, 1, 2 * D)),...]
where the time goes in v3:
time: 118 us; the launch traced here: 117 us
  starting transfers between devices  50.4 us (43%)
  blocking collectives  32.1 us (27%)
  waiting for transfers between devices  14.4 us (12%)
  Pallas kernels  11.5 us (10%)
  local copies, waits for them, and re-layouts  6.43 us (5%)
  other arithmetic  1.71 us (1%)
    all_to_all x3, starting transfers between devices, exchange(): return lax.all_to_all(blocks, 'ctx', 0, 0, axis_index_groups=columns)  17.1 us
    psum x1, blocking collectives, body(): gains = lax.psum(gains, 'dp', axis_index_groups=strided(dp, 8, dp // 8))  15.5 us
    all_to_all x1, starting transfers between devices, body(): lax.all_to_all(jnp.broadcast_to(gains[None, None], (4 * half, 1, 2 * D)),...  14.7 us
    all_to_all x3, waiting for transfers between devices, exchange(): return lax.all_to_all(blocks, 'ctx', 0, 0, axis_index_groups=columns)  11.2 us
    psum x1, blocking collectives, body(): gains = lax.psum(gains, 'ctx', axis_index_groups=strided(ctx, 1, 2))  11 us
    ppermute x1, starting transfers between devices, body(): kv_swapped = lax.ppermute(kv, 'ctx', swap)  10.6 us
    ppermute x1, starting transfers between devices, body(): other = lax.ppermute(theirs, 'ctx', swap)  8.01 us
    pallas_call x1, Pallas kernels, call_attend(): pl.pallas_call(functools.partial(attend_kernel, heads), out_shape=[jax.Sh...  6.16 us
  transfers between devices with their start and end apart: 6, of which 5 were waited for; matrix products, arithmetic and copies ran while one was open for 1% of the time, Pallas kernels for 3%

profile of v3, /device:TPU:1, one launch (start us, length us, event | category | flops | bytes accessed | tf_op | source)
XLA Modules:
  0.0 117.3 jit_solution(3093321734471838902)
XLA Ops:
  0.6 0.8 pad_maximum_fusion
  1.4 0.8 broadcast_in_dim.37
  2.2 7.7 %all-to-all-start = ((bf16[8,128,256]{2,1,0:T(8,128)(2,1)}), bf16[8,128,256]{2,1,0:T(8,128)(2,1)S(1)}, u32[]{:S(2)}, u32[]{:S(2)}) async-start(bf16[8,128,256]{2,1,0:T(8,128)(2,1)} %broadcast_in_dim.37), calls=%async_computation | async-start | bytes 1048576 | tf_op jit(solution)/shard_map/all_to_all | solution.py:332
  9.9 10.6 %collective-permute-start = (bf16[128,256]{1,0:T(8,128)(2,1)S(1)}, bf16[128,256]{1,0:T(8,128)(2,1)S(1)}, u32[]{:S(2)}, u32[]{:S(2)}) collective-permute-start(bf16[128,256]{1,0:T(8,128)(2,1)S(1)} %pad_maximum_fusion), channel_id=1, source_target_pairs={{0,1},{1,0},{2,3},{3,2},{4,5},{5,4},{6,7},{7,6},{8,9},{9,8},{10,11... | collective-permute-start | bytes 196616 | tf_op jit(solution)/shard_map/ppermute | solution.py:338
  20.5 1.7 %collective-permute-done = bf16[128,256]{1,0:T(8,128)(2,1)S(1)} collective-permute-done((bf16[128,256]{1,0:T(8,128)(2,1)S(1)}, bf16[128,256]{1,0:T(8,128)(2,1)S(1)}, u32[]{:S(2)}, u32[]{:S(2)}) %collective-permute-start) | collective-permute-done | bytes 65568 | tf_op jit(solution)/shard_map/ppermute | solution.py:338
  22.2 2.4 %all-to-all-done.kv_own = bf16[8,128,256]{2,1,0:T(8,128)(2,1)S(1)} async-done(((bf16[8,128,256]{2,1,0:T(8,128)(2,1)}), bf16[8,128,256]{2,1,0:T(8,128)(2,1)S(1)}, u32[]{:S(2)}, u32[]{:S(2)}) %all-to-all-start) | async-done | bytes 524320 | tf_op jit(solution)/shard_map/all_to_all | solution.py:332
  24.6 0.8 broadcast_in_dim.38
  25.5 4.4 %all-to-all-start.1 = ((bf16[8,128,256]{2,1,0:T(8,128)(2,1)}), bf16[8,128,256]{2,1,0:T(8,128)(2,1)S(1)}, u32[]{:S(2)}, u32[]{:S(2)}) async-start(bf16[8,128,256]{2,1,0:T(8,128)(2,1)} %broadcast_in_dim.38), calls=%async_computation.1 | async-start | bytes 1048576 | tf_op jit(solution)/shard_map/all_to_all | solution.py:332
  29.9 0.6 copy-done.8
  30.5 0.0 copy-done.9
  30.6 0.1 maximum_bitcast_fusion.freq
  30.7 0.7 copy-done.4
  31.3 3.5 %prep.1 = (f32[2048,128]{1,0:T(8,128)S(1)}, f32[128,128]{1,0:T(8,128)S(1)}, bf16[1024,128]{1,0:T(8,128)(2,1)S(1)}, bf16[128,1024]{1,0:T(8,128)(2,1)S(1)}, bf16[1...) custom-call(s32[1]{0:T(128)} %bitcast.token_ref, s32[1,32]{1,0:T(1,128)S(1)} %copy-done.4, ...), custom_call_target="tpu_custom_call" | custom-call | flops 40000000 | bytes 4000000 | tf_op jit(solution)/shard_map/prep/pallas_call | solution.py:249
  34.9 0.7 copy-done.5
  35.6 8.8 %all-to-all-done.1.kv_other = bf16[8,128,256]{2,1,0:T(8,128)(2,1)S(1)} async-done(((bf16[8,128,256]{2,1,0:T(8,128)(2,1)}), bf16[8,128,256]{2,1,0:T(8,128)(2,1)S(1)}, u32[]{:S(2)}, u32[]{:S(2)}) %all-to-all-start.1) | async-done | bytes 524320 | tf_op jit(solution)/shard_map/all_to_all | solution.py:332
  44.4 0.9 copy-done.6
  45.3 6.2 %attend.1 = (bf16[128,1024]{1,0:T(8,128)(2,1)}, bf16[128,1024]{1,0:T(8,128)(2,1)}, bf16[8,256,256]{2,1,0:T(8,128)(2,1)}, f32[8,256]{1,0:T(8,128)S(1)}) custom-call(s32[1]{0:T(128)} %bitcast.token_ref, s32[1,32]{1,0:T(1,128)S(1)} %copy-done.4, bf16[8,128,256]{2,1,0:T(8,128)(2,1)S(1)} %all-to-all-done.kv_own, ...), custom_call_target="tpu_custom_call" | custom-call | flops 3200000000 | bytes 8000000 | tf_op jit(solution)/shard_map/attend/pallas_call | solution.py:278
  51.5 5.1 %all-to-all-start.2 = ((bf16[8,256,256]{2,1,0:T(8,128)(2,1)}), bf16[8,256,256]{2,1,0:T(8,128)(2,1)S(1)}, u32[]{:S(2)}, u32[]{:S(2)}) async-start(bf16[8,256,256]{2,1,0:T(8,128)(2,1)} %get-tuple-element.28), calls=%async_computation.2 | async-start | bytes 2097152 | tf_op jit(solution)/shard_map/all_to_all | solution.py:332
  56.6 5.6 %psum.21 = f32[256]{0:T(256)S(1)} all-reduce(f32[256]{0:T(256)S(1)} %bitcast.28), channel_id=1, replica_groups={{0,16},{32,48},{64,80},{96,112},{128,144},{160,176},{192,208},{224,240}..., use_global_device_ids=true, to_apply=%region_1.0 | all-reduce | flops 256 | bytes 2048 | tf_op jit(solution)/shard_map/psum | solution.py:348
  62.2 15.5 %psum.22 = f32[256]{0:T(256)S(1)} all-reduce(f32[256]{0:T(256)S(1)} %psum.21), channel_id=1, replica_groups={{0,128,256,384},{16,144,272,400},{32,160,288,416},{48,176,304,432},{64,..., use_global_device_ids=true, to_apply=%region_2.0 | all-reduce | flops 256 | bytes 2048 | tf_op jit(solution)/shard_map/psum | solution.py:349
  77.7 11.0 %psum.23 = f32[256]{0:T(256)S(1)} all-reduce(f32[256]{0:T(256)S(1)} %psum.22), channel_id=1, replica_groups={{0,1},{2,3},{4,5},{6,7},{8,9},{10,11},{12,13},{14,15},{16,17},{18,19},{..., use_global_device_ids=true, to_apply=%region_3.0 | all-reduce | flops 256 | bytes 2048 | tf_op jit(solution)/shard_map/psum | solution.py:350
  88.7 0.7 convert_reduce_fusion.own_ref
  89.4 0.6 broadcast_in_dim.44
  90.1 14.7 %all-to-all-start.3 = ((f32[32,1,256]{2,1,0:T(1,128)}), f32[32,1,256]{2,1,0:T(1,128)S(1)}, u32[]{:S(2)}, u32[]{:S(2)}) async-start(f32[32,1,256]{2,1,0:T(1,128)} %broadcast_in_dim.44), calls=%async_computation.3 | async-start | bytes 65536 | tf_op jit(solution)/shard_map/all_to_all | solution.py:357
  104.8 0.1 slice_reduce_fusion
  104.9 8.0 %collective-permute-start.1 = (bf16[128,256]{1,0:T(8,128)(2,1)S(1)}, bf16[128,256]{1,0:T(8,128)(2,1)S(1)}, u32[]{:S(2)}, u32[]{:S(2)}) collective-permute-start(bf16[128,256]{1,0:T(8,128)(2,1)S(1)} %slice_reduce_fusion), channel_id=1, source_target_pairs={{0,1},{1,0},{2,3},{3,2},{4,5},{5,4},{6,7},{7,6},{8,9},{9,8},{10,11... | collective-permute-start | bytes 196616 | tf_op jit(solution)/shard_map/ppermute | solution.py:351
  112.9 0.9 all-to-all-done.3
  113.8 0.1 reduce_sum.32
  113.9 0.5 fusion
  114.4 0.5 collective-permute-done.1.other_ref
  114.9 0.6 copy-done.7
  115.5 1.8 %finish.1 = (bf16[128,128]{1,0:T(8,128)(2,1)}, bf16[128,128]{1,0:T(8,128)(2,1)}) custom-call(f32[128,256]{1,0:T(8,128)} %convert_reduce_fusion.own_ref, bf16[128,256]{1,0:T(8,128)(2,1)} %copy-done.7, bf16[128,128]{1,0:T(8,128)(2,1)} %bitcast.18, f32[8,128]{1,0:T(8,128)} %copy-done.3, f32[128,128]{1,0:T(8,128)} %copy-done.2), custom_call_target="tpu_custom_call" | custom-call | bytes 100000000 | tf_op jit(solution)/shard_map/finish/pallas_call | solution.py:293
  (18 shorter events, 0.1 us)
Async XLA Ops:
  2.2 22.4 %all-to-all-start = ((bf16[8,128,256]{2,1,0:T(8,128)(2,1)}), bf16[8,128,256]{2,1,0:T(8,128)(2,1)S(1)}, u32[]{:S(2)}, u32[]{:S(2)}) async-start(bf16[8,128,256]{2,1,0:T(8,128)(2,1)} %broadcast_in_dim.37), calls=%async_computation | async-start | bytes 1048576 | tf_op jit(solution)/shard_map/all_to_all | solution.py:332
  9.9 12.3 %collective-permute-start = (bf16[128,256]{1,0:T(8,128)(2,1)S(1)}, bf16[128,256]{1,0:T(8,128)(2,1)S(1)}, u32[]{:S(2)}, u32[]{:S(2)}) collective-permute-start(bf16[128,256]{1,0:T(8,128)(2,1)S(1)} %pad_maximum_fusion), channel_id=1, source_target_pairs={{0,1},{1,0},{2,3},{3,2},{4,5},{5,4},{6,7},{7,6},{8,9},{9,8},{10,11... | collective-permute-start | bytes 196616 | tf_op jit(solution)/shard_map/ppermute | solution.py:338
  25.5 5.2 %copy-start = (bf16[1,128,1024]{2,1,0:T(8,128)(2,1)S(1)}, bf16[1,128,1024]{2,1,0:T(8,128)(2,1)}, u32[]{:S(2)}) copy-start(bf16[1,128,1024]{2,1,0:T(8,128)(2,1)} %param.10) | copy-start | bytes 786436
  25.5 5.2 %copy-start.1 = (bf16[1,128,1024]{2,1,0:T(8,128)(2,1)S(1)}, bf16[1,128,1024]{2,1,0:T(8,128)(2,1)}, u32[]{:S(2)}) copy-start(bf16[1,128,1024]{2,1,0:T(8,128)(2,1)} %param.7) | copy-start | bytes 786436
  25.5 18.9 %all-to-all-start.1 = ((bf16[8,128,256]{2,1,0:T(8,128)(2,1)}), bf16[8,128,256]{2,1,0:T(8,128)(2,1)S(1)}, u32[]{:S(2)}, u32[]{:S(2)}) async-start(bf16[8,128,256]{2,1,0:T(8,128)(2,1)} %broadcast_in_dim.38), calls=%async_computation.1 | async-start | bytes 1048576 | tf_op jit(solution)/shard_map/all_to_all | solution.py:332
  29.9 0.7 copy-start.8
  29.9 0.7 copy-start.9
  30.6 13.8 %copy-start.3 = (f32[8,128]{1,0:T(8,128)}, f32[8,128]{1,0:T(8,128)S(1)}, u32[]{:S(2)}) copy-start(f32[8,128]{1,0:T(8,128)S(1)} %stack.8.gain_ref) | copy-start | bytes 12292
  30.6 0.7 copy-start.4
  34.8 0.7 copy-start.5
  35.6 15.9 %copy-start.2 = (f32[128,128]{1,0:T(8,128)}, f32[128,128]{1,0:T(8,128)S(1)}, u32[]{:S(2)}) copy-start(f32[128,128]{1,0:T(8,128)S(1)} %get-tuple-element.21.table_own) | copy-start | bytes 196612
  44.4 1.0 copy-start.6
  51.5 37.2 %all-to-all-start.2 = ((bf16[8,256,256]{2,1,0:T(8,128)(2,1)}), bf16[8,256,256]{2,1,0:T(8,128)(2,1)S(1)}, u32[]{:S(2)}, u32[]{:S(2)}) async-start(bf16[8,256,256]{2,1,0:T(8,128)(2,1)} %get-tuple-element.28), calls=%async_computation.2 | async-start | bytes 2097152 | tf_op jit(solution)/shard_map/all_to_all | solution.py:332
  90.1 23.8 %all-to-all-start.3 = ((f32[32,1,256]{2,1,0:T(1,128)}), f32[32,1,256]{2,1,0:T(1,128)S(1)}, u32[]{:S(2)}, u32[]{:S(2)}) async-start(f32[32,1,256]{2,1,0:T(1,128)} %broadcast_in_dim.44), calls=%async_computation.3 | async-start | bytes 65536 | tf_op jit(solution)/shard_map/all_to_all | solution.py:357
  104.9 10.0 %collective-permute-start.1 = (bf16[128,256]{1,0:T(8,128)(2,1)S(1)}, bf16[128,256]{1,0:T(8,128)(2,1)S(1)}, u32[]{:S(2)}, u32[]{:S(2)}) collective-permute-start(bf16[128,256]{1,0:T(8,128)(2,1)S(1)} %slice_reduce_fusion), channel_id=1, source_target_pairs={{0,1},{1,0},{2,3},{3,2},{4,5},{5,4},{6,7},{7,6},{8,9},{9,8},{10,11... | collective-permute-start | bytes 196616 | tf_op jit(solution)/shard_map/ppermute | solution.py:351
  114.9 0.6 copy-start.7

commit v4 on v3

--- a/solution.py
+++ b/solution.py
@@ -22,6 +22,10 @@
 
 def dot(a, b):
     return jnp.dot(a, b, preferred_element_type=F32)
+
+
+def dot_rows(a, b):
+    return lax.dot_general(a, b, (((1,), (1,)), ((), ())), preferred_element_type=F32)
 
 
 def sin_cos(angle):
@@ -74,7 +78,7 @@
 
 def prep_kernel(
     heads, token_ref, lengths, freq, q_raw, dout, gain_ref,
-    table_ref, table_own, q_ref, qt_ref, do_ref, dot_ref, pos_ref,
+    table_ref, table_own, q_ref, do_ref, pos_ref,
 ):
     tokens_own = q_raw.shape[0]
     seq = table_ref.shape[0]
@@ -98,17 +102,13 @@
         unit, _ = unit_of(q_raw[:, cols])
         q = rotate(unit * gain_ref[0:1, :], cosine, sine)
         q_ref[rows, :] = q.astype(BF16)
-        qt_ref[:, rows] = q.T.astype(BF16)
-        g = dout[:, cols]
-        do_ref[rows, :] = g
-        dot_ref[:, rows] = g.astype(F32).T.astype(BF16)
+        do_ref[rows, :] = dout[:, cols]
 
 
 def attend_kernel(
-    heads, token_ref, lengths, kv_own, kv_other, table_ref, table_own, q_ref, qt_ref, do_ref, dot_ref,
-    q_raw, gain_ref,
-    out_ref, dq_ref, dkv_ref, gains_ref,
-    s_buf, k_buf, kt_buf, vt_buf, ot_buf, dqt_buf, max_buf, sum_buf, row_buf, kg_buf,
+    heads, token_ref, lengths, kv_own, kv_other, table_ref, q_ref, do_ref, gain_ref,
+    out_ref, dqt_buf, dkv_ref, key_sum_ref,
+    s_buf, k_buf, kt_buf, vt_buf, ot_buf, max_buf, sum_buf, row_buf, kg_buf,
 ):
     _, tokens_own, _ = kv_own.shape
     kb = 4 * tokens_own
@@ -154,23 +154,26 @@
     row = lax.broadcasted_iota(jnp.int32, (kb, tokens_own), 0)
     key_shift = row + jnp.where(row % (2 * tokens_own) < tokens_own, side * tokens_own, -side * tokens_own)
 
-    def scores_step(b, carry):
+    def prepare(b):
         unit, _ = unit_of(keys_of(b))
         k = rotate(unit * gain_ref[1:2, :], *tables(b))
-        k_rows = k.astype(BF16)
-        k_buf[b] = k_rows
+        k_buf[b] = k.astype(BF16)
         kt_buf[b] = k.T.astype(BF16)
         vt_buf[b] = values_of(b).astype(F32).T.astype(BF16)
+
+    def scores_step(b, carry):
         key = b * kb + key_shift
         allowed = (key >= start_row) & (key <= tok_row)
         bias = jnp.where(allowed, 0.0, masked_value)
         for c in range(chunks):
             cs = slice(c * cc, (c + 1) * cc)
-            s = dot(k_rows, qt_ref[:, cs]) * factor + jnp.concatenate([bias] * (cc // tokens_own), 1)
+            s = dot_rows(k_buf[b], q_ref[cs, :]) * factor + jnp.concatenate([bias] * (cc // tokens_own), 1)
             s_buf[b, :, cs] = s
             max_buf[:, cs] = jnp.maximum(max_buf[:, cs], jnp.max(s.reshape(kb // 8, 8, cc), axis=0))
+        prepare(jnp.minimum(b + 1, blocks - 1))
         return carry
 
+    prepare(lo)
     lax.fori_loop(lo, hi, scores_step, 0)
     row_buf[:1, :] = jnp.max(max_buf[...], axis=0, keepdims=True)
 
@@ -189,7 +192,7 @@
         hs = slice(h * tokens_own, (h + 1) * tokens_own)
         ot = (ot_buf[:, hs] * sum_buf[:1, hs]).astype(BF16).astype(F32)
         out_ref[:, h * D : (h + 1) * D] = ot.T.astype(BF16)
-        row_buf[:1, hs] = jnp.sum(ot * dot_ref[:, hs].astype(F32), axis=0, keepdims=True)
+        row_buf[:1, hs] = jnp.sum(ot * do_ref[hs, :].T.astype(F32), axis=0, keepdims=True)
 
     def back_step(b, carry):
         dk = jnp.zeros((kb, D), F32)
@@ -197,7 +200,7 @@
         v_rows = values_of(b)
         for c in range(chunks):
             cs = slice(c * cc, (c + 1) * cc)
-            dp = dot(v_rows, dot_ref[:, cs])
+            dp = dot_rows(v_rows, do_ref[cs, :])
             prob = s_buf[b, :, cs] * sum_buf[:1, cs]
             dv = dv + dot(prob.astype(BF16), do_ref[cs, :])
             ds = (prob * (dp - row_buf[:1, cs])).astype(BF16)
@@ -214,18 +217,23 @@
         return carry
 
     lax.fori_loop(lo, hi, back_step, 0)
+    key_sum_ref[...] = kg_buf[...]
+
+
+def query_kernel(heads, dqt_ref, key_sum_ref, table_own, q_raw, gain_ref, dq_ref, gains_ref):
+    tokens_own = q_raw.shape[0]
     cosine, sine = unfold(table_own[...])
     q_sum = jnp.zeros((8, D), F32)
     for h in range(heads):
         hs = slice(h * tokens_own, (h + 1) * tokens_own)
-        back = rotate_back(dqt_buf[:, hs].T * SCALE, cosine, sine)
+        back = rotate_back(dqt_ref[:, hs].T * SCALE, cosine, sine)
         unit, inverse = unit_of(q_raw[:, h * D : (h + 1) * D])
         q_sum = q_sum + jnp.sum((back * unit).reshape(tokens_own // 8, 8, D), axis=0)
         scaled = back * gain_ref[0:1, :]
         mean = jnp.mean(scaled * unit, axis=1, keepdims=True)
         dq_ref[:, h * D : (h + 1) * D] = (inverse * (scaled - unit * mean)).astype(BF16)
     gains_ref[:, :D] = jnp.broadcast_to(jnp.sum(q_sum, axis=0, keepdims=True), (8, D))
-    gains_ref[:, D:] = jnp.broadcast_to(jnp.sum(kg_buf[...], axis=0, keepdims=True), (8, D))
+    gains_ref[:, D:] = jnp.broadcast_to(jnp.sum(key_sum_ref[...], axis=0, keepdims=True), (8, D))
 
 
 def finish_kernel(own_ref, other_ref, k_raw, gain_ref, table_own, dk_ref, dv_ref):
@@ -244,7 +252,7 @@
     rows = heads * tokens_own
     shapes = [
         ((seq, D), F32), ((tokens_own, D), F32),
-        ((rows, D), BF16), ((D, rows), BF16), ((rows, D), BF16), ((D, rows), BF16),
+        ((rows, D), BF16), ((rows, D), BF16),
     ]
     return pl.pallas_call(
         functools.partial(prep_kernel, heads),
@@ -259,33 +267,48 @@
     )(token, lengths, freq, q_raw, dout, both_gains)
 
 
-def call_attend(token, lengths, kv_own, kv_other, prepared, q_raw, both_gains, **kw):
-    tokens_own, width = q_raw.shape
-    heads = width // D
+def call_attend(token, lengths, kv_own, kv_other, table, q_rows, do_rows, both_gains, **kw):
+    tokens_own = kv_own.shape[1]
+    heads = q_rows.shape[0] // tokens_own
+    width = heads * D
     blocks = kv_own.shape[0] // 2
     kb = 4 * tokens_own
     rows = heads * tokens_own
     shapes = [
-        ((tokens_own, width), BF16), ((tokens_own, width), BF16), ((2 * blocks, kb // 2, 2 * D), BF16), ((8, 2 * D), F32),
+        ((tokens_own, width), BF16), ((D, rows), F32), ((2 * blocks, kb // 2, 2 * D), BF16), ((8, D), F32),
     ]
     scratch = [
         pltpu.VMEM((blocks, kb, rows), F32),
         pltpu.VMEM((blocks, kb, D), BF16), pltpu.VMEM((blocks, D, kb), BF16),
-        pltpu.VMEM((blocks, D, kb), BF16), pltpu.VMEM((D, rows), F32), pltpu.VMEM((D, rows), F32),
+        pltpu.VMEM((blocks, D, kb), BF16), pltpu.VMEM((D, rows), F32),
         pltpu.VMEM((8, rows), F32), pltpu.VMEM((8, rows), F32), pltpu.VMEM((8, rows), F32),
         pltpu.VMEM((8, D), F32),
     ]
     return pl.pallas_call(
         functools.partial(attend_kernel, heads),
         out_shape=[jax.ShapeDtypeStruct(s, t) for s, t in shapes],
-        in_specs=[SM, SM] + [VM] * 10,
+        in_specs=[SM, SM] + [VM] * 6,
         out_specs=[VM] * len(shapes),
         scratch_shapes=scratch,
         compiler_params=pltpu.CompilerParams(vmem_limit_bytes=20 * 2**20),
         cost_estimate=pl.CostEstimate(flops=3_200_000_000, bytes_accessed=8_000_000, transcendentals=2_000_000),
         name="attend",
         **kw,
-    )(token, lengths, kv_own, kv_other, *prepared, q_raw, both_gains)
+    )(token, lengths, kv_own, kv_other, table, q_rows, do_rows, both_gains)
+
+
+def call_query(dqt, key_sum, table_own, q_raw, both_gains, **kw):
+    heads = q_raw.shape[1] // D
+    return pl.pallas_call(
+        functools.partial(query_kernel, heads),
+        out_shape=[jax.ShapeDtypeStruct(q_raw.shape, BF16), jax.ShapeDtypeStruct((8, 2 * D), F32)],
+        in_specs=[VM] * 5,
+        out_specs=[VM] * 2,
+        compiler_params=pltpu.CompilerParams(vmem_limit_bytes=12 * 2**20),
+        cost_estimate=pl.CostEstimate(flops=5_000_000, bytes_accessed=2_000_000, transcendentals=0),
+        name="query",
+        **kw,
+    )(dqt, key_sum, table_own, q_raw, both_gains)
 
 
 def call_finish(own, other, k_raw, both_gains, table_own, **kw):
@@ -338,11 +361,12 @@
     kv_swapped = lax.ppermute(kv, "ctx", swap)
     kv_own = exchange(spread(kv))
     kv_other = exchange(spread(kv_swapped))
-    prepared = call_prep(token, doc_lengths, frequency_row(), query_raw[0], out_grad[0], both_gains, seq)
-    output, dq, parts, gains = call_attend(
-        token, doc_lengths, kv_own, kv_other, prepared, query_raw[0], both_gains
+    table, table_own, q_rows, do_rows = call_prep(token, doc_lengths, frequency_row(), query_raw[0], out_grad[0], both_gains, seq)
+    output, dqt, parts, key_sum = call_attend(
+        token, doc_lengths, kv_own, kv_other, table, q_rows, do_rows, both_gains
     )
     received = exchange(parts)
+    dq, gains = call_query(dqt, key_sum, table_own, query_raw[0], both_gains)
     own = jnp.sum(received[:, :tokens_own].astype(F32), axis=0)
     theirs = jnp.sum(received[:, tokens_own:].astype(F32), axis=0).astype(BF16)
     gains = lax.psum(gains[0], "dp", axis_index_groups=strided(dp, 1, 2))
@@ -358,7 +382,7 @@
         jnp.broadcast_to(gains[None, None], (4 * half, 1, 2 * D)), ("dp", "ctx"), 0, 0, axis_index_groups=groups
     )
     gains = jnp.sum(gains, axis=(0, 1))
-    dk, dv = call_finish(own, other, key_raw[0], both_gains, prepared[1])
+    dk, dv = call_finish(own, other, key_raw[0], both_gains, table_own)
     return (output[None], dq[None], dk[None], dv[None], gains[:D], gains[D:])
 
 

time: 118 us -> 115 us (0.975); the launches traced: 117 us -> 112 us
  blocking collectives: 32.1 us -> 29.7 us
  starting transfers between devices: 50.4 us -> 48.3 us
  local copies, waits for them, and re-layouts: 6.43 us -> 4.77 us
    psum x1, blocking collectives: 15.5 us -> 13.1 us  [body(): gains = lax.psum(gains, 'dp', axis_index_groups=strided(dp, 8, dp // 8))]
    pallas_call x0 -> x1, Pallas kernels: none -> 2.09 us  [call_query(): pl.pallas_call(functools.partial(query_kernel, heads), out_shape=[jax.Sha...]
    all_to_all x1, starting transfers between devices: 14.7 us -> 12.7 us  [body(): lax.all_to_all(jnp.broadcast_to(gains[None, None], (4 * half, 1, 2 * D)),...]
    unnamed x20 -> x16, local copies, waits for them, and re-layouts: 3.59 us -> 1.95 us
    pallas_call x1, Pallas kernels: 6.16 us -> 4.66 us  [call_attend(): pl.pallas_call(functools.partial(attend_kernel, heads), out_shape=[jax.Sh...]
  transfers between devices with their start and end apart: 6 -> 6, of which waited for: 5 -> 5; matrix products, arithmetic and copies ran while one was open for 1% -> 1% of each run, Pallas kernels for 3% -> 5%
where the time goes in v4:
time: 115 us; the launch traced here: 112 us
  starting transfers between devices  48.3 us (42%)
  blocking collectives  29.7 us (26%)
  waiting for transfers between devices  15.4 us (13%)
  Pallas kernels  11.7 us (10%)
  local copies, waits for them, and re-layouts  4.77 us (4%)
  other arithmetic  1.71 us (1%)
    all_to_all x3, starting transfers between devices, exchange(): return lax.all_to_all(blocks, 'ctx', 0, 0, axis_index_groups=columns)  16.6 us
    psum x1, blocking collectives, body(): gains = lax.psum(gains, 'dp', axis_index_groups=strided(dp, 8, dp // 8))  13.1 us
    all_to_all x1, starting transfers between devices, body(): lax.all_to_all(jnp.broadcast_to(gains[None, None], (4 * half, 1, 2 * D)),...  12.7 us
    all_to_all x3, waiting for transfers between devices, exchange(): return lax.all_to_all(blocks, 'ctx', 0, 0, axis_index_groups=columns)  12.3 us
    psum x1, blocking collectives, body(): gains = lax.psum(gains, 'ctx', axis_index_groups=strided(ctx, 1, 2))  11 us
    ppermute x1, starting transfers between devices, body(): kv_swapped = lax.ppermute(kv, 'ctx', swap)  10.6 us
    ppermute x1, starting transfers between devices, body(): other = lax.ppermute(theirs, 'ctx', swap)  8.38 us
    psum x1, blocking collectives, body(): gains = lax.psum(gains[0], 'dp', axis_index_groups=strided(dp, 1, 2))  5.58 us
  transfers between devices with their start and end apart: 6, of which 5 were waited for; matrix products, arithmetic and copies ran while one was open for 1% of the time, Pallas kernels for 5%

profile of v4, /device:TPU:1, one launch (start us, length us, event | category | flops | bytes accessed | tf_op | source)
XLA Modules:
  0.0 112.3 jit_solution(1126190464511204548)
XLA Ops:
  0.6 0.8 pad_maximum_fusion
  1.4 0.8 broadcast_in_dim.37
  2.2 7.7 %all-to-all-start = ((bf16[8,128,256]{2,1,0:T(8,128)(2,1)}), bf16[8,128,256]{2,1,0:T(8,128)(2,1)S(1)}, u32[]{:S(2)}, u32[]{:S(2)}) async-start(bf16[8,128,256]{2,1,0:T(8,128)(2,1)} %broadcast_in_dim.37), calls=%async_computation | async-start | bytes 1048576 | tf_op jit(solution)/shard_map/all_to_all | solution.py:355
  9.9 10.6 %collective-permute-start = (bf16[128,256]{1,0:T(8,128)(2,1)S(1)}, bf16[128,256]{1,0:T(8,128)(2,1)S(1)}, u32[]{:S(2)}, u32[]{:S(2)}) collective-permute-start(bf16[128,256]{1,0:T(8,128)(2,1)S(1)} %pad_maximum_fusion), channel_id=1, source_target_pairs={{0,1},{1,0},{2,3},{3,2},{4,5},{5,4},{6,7},{7,6},{8,9},{9,8},{10,11... | collective-permute-start | bytes 196616 | tf_op jit(solution)/shard_map/ppermute | solution.py:361
  20.5 1.7 %collective-permute-done = bf16[128,256]{1,0:T(8,128)(2,1)S(1)} collective-permute-done((bf16[128,256]{1,0:T(8,128)(2,1)S(1)}, bf16[128,256]{1,0:T(8,128)(2,1)S(1)}, u32[]{:S(2)}, u32[]{:S(2)}) %collective-permute-start) | collective-permute-done | bytes 65568 | tf_op jit(solution)/shard_map/ppermute | solution.py:361
  22.2 2.4 %all-to-all-done.kv_own = bf16[8,128,256]{2,1,0:T(8,128)(2,1)S(1)} async-done(((bf16[8,128,256]{2,1,0:T(8,128)(2,1)}), bf16[8,128,256]{2,1,0:T(8,128)(2,1)S(1)}, u32[]{:S(2)}, u32[]{:S(2)}) %all-to-all-start) | async-done | bytes 524320 | tf_op jit(solution)/shard_map/all_to_all | solution.py:355
  24.6 0.8 broadcast_in_dim.38
  25.5 4.4 %all-to-all-start.1 = ((bf16[8,128,256]{2,1,0:T(8,128)(2,1)}), bf16[8,128,256]{2,1,0:T(8,128)(2,1)S(1)}, u32[]{:S(2)}, u32[]{:S(2)}) async-start(bf16[8,128,256]{2,1,0:T(8,128)(2,1)} %broadcast_in_dim.38), calls=%async_computation.1 | async-start | bytes 1048576 | tf_op jit(solution)/shard_map/all_to_all | solution.py:355
  29.8 0.0 copy-start.7
  29.9 0.6 copy-done.6
  30.5 0.0 copy-done.7
  30.6 0.1 maximum_bitcast_fusion.freq
  30.6 0.7 copy-done.4
  31.3 3.2 %prep.1 = (f32[2048,128]{1,0:T(8,128)S(1)}, f32[128,128]{1,0:T(8,128)S(1)}, bf16[1024,128]{1,0:T(8,128)(2,1)S(1)}, bf16[1024,128]{1,0:T(8,128)(2,1)S(1)}) custom-call(s32[1]{0:T(128)} %bitcast.token_ref, s32[1,32]{1,0:T(1,128)S(1)} %copy-done.4, f32[1,128]{1,0:T(1,128)S(1)} %maximum_bitcast_fusion.freq, bf16[128,1024]{1,0:T(8,128)(2,1)S(1)} %bitcast.14, ...), custom_call_target="tpu_custom_call" | custom-call | flops 40000000 | bytes 4000000 | tf_op jit(solution)/shard_map/prep/pallas_call | solution.py:257
  34.5 9.8 %all-to-all-done.1.kv_other = bf16[8,128,256]{2,1,0:T(8,128)(2,1)S(1)} async-done(((bf16[8,128,256]{2,1,0:T(8,128)(2,1)}), bf16[8,128,256]{2,1,0:T(8,128)(2,1)S(1)}, u32[]{:S(2)}, u32[]{:S(2)}) %all-to-all-start.1) | async-done | bytes 524320 | tf_op jit(solution)/shard_map/all_to_all | solution.py:355
  44.4 4.7 %attend.1 = (bf16[128,1024]{1,0:T(8,128)(2,1)}, f32[128,1024]{1,0:T(8,128)S(1)}, bf16[8,256,256]{2,1,0:T(8,128)(2,1)}, f32[8,128]{1,0:T(8,128)S(1)}) custom-call(s32[1]{0:T(128)} %bitcast.token_ref, s32[1,32]{1,0:T(1,128)S(1)} %copy-done.4, bf16[8,128,256]{2,1,0:T(8,128)(2,1)S(1)} %all-to-all-done.kv_own, bf16[8,128,256]{2,1,0:T(8,128)(2,1)S(1)} %all-to-all-done.1.kv_other, ...), custom_call_target="tpu_custom_call" | custom-call | flops 3200000000 | bytes 8000000 | tf_op jit(solution)/shard_map/attend/pallas_call | solution.py:287
  49.0 4.5 %all-to-all-start.2 = ((bf16[8,256,256]{2,1,0:T(8,128)(2,1)}), bf16[8,256,256]{2,1,0:T(8,128)(2,1)S(1)}, u32[]{:S(2)}, u32[]{:S(2)}) async-start(bf16[8,256,256]{2,1,0:T(8,128)(2,1)} %get-tuple-element.28), calls=%async_computation.2 | async-start | bytes 2097152 | tf_op jit(solution)/shard_map/all_to_all | solution.py:355
  53.6 2.1 %query.1 = (bf16[128,1024]{1,0:T(8,128)(2,1)}, f32[8,256]{1,0:T(8,128)S(1)}) custom-call(f32[128,1024]{1,0:T(8,128)S(1)} %get-tuple-element.24.dqt_ref, f32[8,128]{1,0:T(8,128)S(1)} %get-tuple-element.25.key_sum_ref, f32[128,128]{1,0:T(8,128)S(1)} %get-tuple-element.26.table_own, bf16[128,1024]{1,0:T(8,128)(2,1)S(1)} %bitcast.15, f32[8,128]{1,0:T(8,128)S(1)} %stack.8.gain_ref), custom_call_target="tpu_custom_call" | custom-call | flops 5000000 | bytes 2000000 | tf_op jit(solution)/shard_map/query/pallas_call | solution.py:302
  55.7 5.6 %psum.21 = f32[256]{0:T(256)S(1)} all-reduce(f32[256]{0:T(256)S(1)} %bitcast.28), channel_id=1, replica_groups={{0,16},{32,48},{64,80},{96,112},{128,144},{160,176},{192,208},{224,240}..., use_global_device_ids=true, to_apply=%region_1.0 | all-reduce | flops 256 | bytes 2048 | tf_op jit(solution)/shard_map/psum | solution.py:372
  61.3 13.1 %psum.22 = f32[256]{0:T(256)S(1)} all-reduce(f32[256]{0:T(256)S(1)} %psum.21), channel_id=1, replica_groups={{0,128,256,384},{16,144,272,400},{32,160,288,416},{48,176,304,432},{64,..., use_global_device_ids=true, to_apply=%region_2.0 | all-reduce | flops 256 | bytes 2048 | tf_op jit(solution)/shard_map/psum | solution.py:373
  74.3 11.0 %psum.23 = f32[256]{0:T(256)S(1)} all-reduce(f32[256]{0:T(256)S(1)} %psum.22), channel_id=1, replica_groups={{0,1},{2,3},{4,5},{6,7},{8,9},{10,11},{12,13},{14,15},{16,17},{18,19},{..., use_global_device_ids=true, to_apply=%region_3.0 | all-reduce | flops 256 | bytes 2048 | tf_op jit(solution)/shard_map/psum | solution.py:374
  85.4 0.7 convert_reduce_fusion.own_ref
  86.1 0.6 broadcast_in_dim.44
  86.7 12.7 %all-to-all-start.3 = ((f32[32,1,256]{2,1,0:T(1,128)}), f32[32,1,256]{2,1,0:T(1,128)S(1)}, u32[]{:S(2)}, u32[]{:S(2)}) async-start(f32[32,1,256]{2,1,0:T(1,128)} %broadcast_in_dim.44), calls=%async_computation.3 | async-start | bytes 65536 | tf_op jit(solution)/shard_map/all_to_all | solution.py:381
  99.5 0.1 slice_reduce_fusion
  99.5 8.4 %collective-permute-start.1 = (bf16[128,256]{1,0:T(8,128)(2,1)S(1)}, bf16[128,256]{1,0:T(8,128)(2,1)S(1)}, u32[]{:S(2)}, u32[]{:S(2)}) collective-permute-start(bf16[128,256]{1,0:T(8,128)(2,1)S(1)} %slice_reduce_fusion), channel_id=1, source_target_pairs={{0,1},{1,0},{2,3},{3,2},{4,5},{5,4},{6,7},{7,6},{8,9},{9,8},{10,11... | collective-permute-start | bytes 196616 | tf_op jit(solution)/shard_map/ppermute | solution.py:375
  107.9 0.6 all-to-all-done.3
  108.5 0.1 reduce_sum.32
  108.5 0.5 fusion
  109.1 0.9 collective-permute-done.1.other_ref
  109.9 0.6 copy-done.5
  110.5 1.8 %finish.1 = (bf16[128,128]{1,0:T(8,128)(2,1)}, bf16[128,128]{1,0:T(8,128)(2,1)}) custom-call(f32[128,256]{1,0:T(8,128)} %convert_reduce_fusion.own_ref, bf16[128,256]{1,0:T(8,128)(2,1)} %copy-done.5, bf16[128,128]{1,0:T(8,128)(2,1)} %bitcast.18, f32[8,128]{1,0:T(8,128)} %copy-done.3, f32[128,128]{1,0:T(8,128)} %copy-done.2), custom_call_target="tpu_custom_call" | custom-call | bytes 100000000 | tf_op jit(solution)/shard_map/finish/pallas_call | solution.py:316
  (15 shorter events, 0.1 us)
Async XLA Ops:
  2.2 22.4 %all-to-all-start = ((bf16[8,128,256]{2,1,0:T(8,128)(2,1)}), bf16[8,128,256]{2,1,0:T(8,128)(2,1)S(1)}, u32[]{:S(2)}, u32[]{:S(2)}) async-start(bf16[8,128,256]{2,1,0:T(8,128)(2,1)} %broadcast_in_dim.37), calls=%async_computation | async-start | bytes 1048576 | tf_op jit(solution)/shard_map/all_to_all | solution.py:355
  9.9 12.3 %collective-permute-start = (bf16[128,256]{1,0:T(8,128)(2,1)S(1)}, bf16[128,256]{1,0:T(8,128)(2,1)S(1)}, u32[]{:S(2)}, u32[]{:S(2)}) collective-permute-start(bf16[128,256]{1,0:T(8,128)(2,1)S(1)} %pad_maximum_fusion), channel_id=1, source_target_pairs={{0,1},{1,0},{2,3},{3,2},{4,5},{5,4},{6,7},{7,6},{8,9},{9,8},{10,11... | collective-permute-start | bytes 196616 | tf_op jit(solution)/shard_map/ppermute | solution.py:361
  25.5 5.2 %copy-start = (bf16[1,128,1024]{2,1,0:T(8,128)(2,1)S(1)}, bf16[1,128,1024]{2,1,0:T(8,128)(2,1)}, u32[]{:S(2)}) copy-start(bf16[1,128,1024]{2,1,0:T(8,128)(2,1)} %param.7) | copy-start | bytes 786436
  25.5 5.2 %copy-start.1 = (bf16[1,128,1024]{2,1,0:T(8,128)(2,1)S(1)}, bf16[1,128,1024]{2,1,0:T(8,128)(2,1)}, u32[]{:S(2)}) copy-start(bf16[1,128,1024]{2,1,0:T(8,128)(2,1)} %param.10) | copy-start | bytes 786436
  25.5 18.9 %all-to-all-start.1 = ((bf16[8,128,256]{2,1,0:T(8,128)(2,1)}), bf16[8,128,256]{2,1,0:T(8,128)(2,1)S(1)}, u32[]{:S(2)}, u32[]{:S(2)}) async-start(bf16[8,128,256]{2,1,0:T(8,128)(2,1)} %broadcast_in_dim.38), calls=%async_computation.1 | async-start | bytes 1048576 | tf_op jit(solution)/shard_map/all_to_all | solution.py:355
  29.8 0.7 copy-start.6
  29.8 0.7 copy-start.7
  30.5 23.0 %copy-start.3 = (f32[8,128]{1,0:T(8,128)}, f32[8,128]{1,0:T(8,128)S(1)}, u32[]{:S(2)}) copy-start(f32[8,128]{1,0:T(8,128)S(1)} %stack.8.gain_ref) | copy-start | bytes 12292
  30.6 0.7 copy-start.4
  34.5 19.1 %copy-start.2 = (f32[128,128]{1,0:T(8,128)}, f32[128,128]{1,0:T(8,128)S(1)}, u32[]{:S(2)}) copy-start(f32[128,128]{1,0:T(8,128)S(1)} %get-tuple-element.26.table_own) | copy-start | bytes 196612
  49.0 36.4 %all-to-all-start.2 = ((bf16[8,256,256]{2,1,0:T(8,128)(2,1)}), bf16[8,256,256]{2,1,0:T(8,128)(2,1)S(1)}, u32[]{:S(2)}, u32[]{:S(2)}) async-start(bf16[8,256,256]{2,1,0:T(8,128)(2,1)} %get-tuple-element.28), calls=%async_computation.2 | async-start | bytes 2097152 | tf_op jit(solution)/shard_map/all_to_all | solution.py:355
  86.7 21.8 %all-to-all-start.3 = ((f32[32,1,256]{2,1,0:T(1,128)}), f32[32,1,256]{2,1,0:T(1,128)S(1)}, u32[]{:S(2)}, u32[]{:S(2)}) async-start(f32[32,1,256]{2,1,0:T(1,128)} %broadcast_in_dim.44), calls=%async_computation.3 | async-start | bytes 65536 | tf_op jit(solution)/shard_map/all_to_all | solution.py:381
  99.5 10.4 %collective-permute-start.1 = (bf16[128,256]{1,0:T(8,128)(2,1)S(1)}, bf16[128,256]{1,0:T(8,128)(2,1)S(1)}, u32[]{:S(2)}, u32[]{:S(2)}) collective-permute-start(bf16[128,256]{1,0:T(8,128)(2,1)S(1)} %slice_reduce_fusion), channel_id=1, source_target_pairs={{0,1},{1,0},{2,3},{3,2},{4,5},{5,4},{6,7},{7,6},{8,9},{9,8},{10,11... | collective-permute-start | bytes 196616 | tf_op jit(solution)/shard_map/ppermute | solution.py:375
  109.9 0.6 copy-start.5

commit v5 on v4

--- a/solution.py
+++ b/solution.py
@@ -318,7 +318,8 @@
         out_shape=[shape, shape],
         in_specs=[VM] * 5,
         out_specs=[VM] * 2,
-        cost_estimate=pl.CostEstimate(flops=0, bytes_accessed=100_000_000, transcendentals=0),
+        compiler_params=pltpu.CompilerParams(vmem_limit_bytes=4 * 2**20),
+        cost_estimate=pl.CostEstimate(flops=1_000_000, bytes_accessed=500_000, transcendentals=0),
         name="finish",
         **kw,
     )(own, other, k_raw, both_gains, table_own)
@@ -359,7 +360,9 @@
 
     kv = jnp.concatenate([key_raw[0], values[0]], axis=1)
     kv_swapped = lax.ppermute(kv, "ctx", swap)
-    kv_own = exchange(spread(kv))
+    kv_own = exchange(
+        jnp.concatenate([spread(key_raw[0]), spread(values[0])], axis=2)
+    )
     kv_other = exchange(spread(kv_swapped))
     table, table_own, q_rows, do_rows = call_prep(token, doc_lengths, frequency_row(), query_raw[0], out_grad[0], both_gains, seq)
     output, dqt, parts, key_sum = call_attend(
@@ -369,17 +372,18 @@
     dq, gains = call_query(dqt, key_sum, table_own, query_raw[0], both_gains)
     own = jnp.sum(received[:, :tokens_own].astype(F32), axis=0)
     theirs = jnp.sum(received[:, tokens_own:].astype(F32), axis=0).astype(BF16)
+    def flat(x, y, z, core):
+        return ((x * 4 + z % 4) * 2 + core) * ctx + 2 * y + z // 4
+
+    xs, ys, zs, cores = range(dp // 8), range(half), range(8), range(2)
+    along_z = [[flat(x, y, z, core) for z in zs] for x in xs for y in ys for core in cores]
+    along_xy = [[flat(x, y, z, core) for x in xs for y in ys] for z in zs for core in cores]
     gains = lax.psum(gains[0], "dp", axis_index_groups=strided(dp, 1, 2))
-    gains = lax.psum(gains, "dp", axis_index_groups=strided(dp, 8, dp // 8))
-    gains = lax.psum(gains, "ctx", axis_index_groups=strided(ctx, 1, 2))
+    gains = lax.psum(gains, ("dp", "ctx"), axis_index_groups=along_z)
+    theirs, gains = lax.optimization_barrier((theirs, gains))
     other = lax.ppermute(theirs, "ctx", swap)
-    own, gains = lax.optimization_barrier((own, gains))
-    groups = [
-        [(8 * x + 2 * z + core) * ctx + 2 * y + side for z in range(4) for y in range(half)]
-        for x in range(dp // 8) for core in range(2) for side in range(2)
-    ]
     gains = lax.all_to_all(
-        jnp.broadcast_to(gains[None, None], (4 * half, 1, 2 * D)), ("dp", "ctx"), 0, 0, axis_index_groups=groups
+        jnp.broadcast_to(gains[None, None], (len(along_xy[0]), 1, 2 * D)), ("dp", "ctx"), 0, 0, axis_index_groups=along_xy
     )
     gains = jnp.sum(gains, axis=(0, 1))
     dk, dv = call_finish(own, other, key_raw[0], both_gains, table_own)

time: 115 us -> 113 us (0.983)
  the two profiles are of different devices: /device:TPU:1 before, /device:TPU:2 now
where the time goes in v5:
time: 113 us
  starting transfers between devices  48 us (42%)
  waiting for transfers between devices  24.8 us (22%)
  blocking collectives  22.9 us (20%)
  Pallas kernels  10.8 us (10%)
  local copies, waits for them, and re-layouts  4.17 us (4%)
  other arithmetic  1.15 us (1%)
    psum x1, blocking collectives, body(): gains = lax.psum(gains, ('dp', 'ctx'), axis_index_groups=along_z)  20.5 us
    all_to_all x3, starting transfers between devices, exchange(): return lax.all_to_all(blocks, 'ctx', 0, 0, axis_index_groups=columns)  19.3 us
    all_to_all x3, waiting for transfers between devices, exchange(): return lax.all_to_all(blocks, 'ctx', 0, 0, axis_index_groups=columns)  17 us
    all_to_all x1, starting transfers between devices, body(): lax.all_to_all(jnp.broadcast_to(gains[None, None], (len(along_xy[0]), 1,...  13 us
    ppermute x1, starting transfers between devices, body(): kv_swapped = lax.ppermute(kv, 'ctx', swap)  10.9 us
    ppermute x1, starting transfers between devices, body(): other = lax.ppermute(theirs, 'ctx', swap)  4.75 us
    pallas_call x1, Pallas kernels, call_attend(): pl.pallas_call(functools.partial(attend_kernel, heads), out_shape=[jax.Sh...  4.65 us
    all_to_all x1, waiting for transfers between devices, body(): lax.all_to_all(jnp.broadcast_to(gains[None, None], (len(along_xy[0]), 1,...  3.84 us
  transfers between devices with their start and end apart: 6, of which 5 were waited for; matrix products, arithmetic and copies ran while one was open for 1% of the time, Pallas kernels for 5%

profile of v5, /device:TPU:2, one launch (start us, length us, event | category | flops | bytes accessed | tf_op | source)
XLA Modules:
  0.0 112.6 jit_solution(16273902882695477138)
XLA Ops:
  0.6 0.8 broadcast_in_dim.46
  1.5 0.9 pad_maximum_fusion
  2.4 7.2 %all-to-all-start = ((bf16[8,128,256]{2,1,0:T(8,128)(2,1)}), bf16[8,128,256]{2,1,0:T(8,128)(2,1)S(1)}, u32[]{:S(2)}, u32[]{:S(2)}) async-start(bf16[8,128,256]{2,1,0:T(8,128)(2,1)} %pad_maximum_fusion), calls=%async_computation | async-start | bytes 1048576 | tf_op jit(solution)/shard_map/all_to_all | solution.py:356
  9.6 10.9 %collective-permute-start = (bf16[128,256]{1,0:T(8,128)(2,1)S(1)}, bf16[128,256]{1,0:T(8,128)(2,1)S(1)}, u32[]{:S(2)}, u32[]{:S(2)}) collective-permute-start(bf16[128,256]{1,0:T(8,128)(2,1)S(1)} %pad_maximum_fusion.1), channel_id=1, source_target_pairs={{0,1},{1,0},{2,3},{3,2},{4,5},{5,4},{6,7},{7,6},{8,9},{9,8},{10,11... | collective-permute-start | bytes 196616 | tf_op jit(solution)/shard_map/ppermute | solution.py:362
  20.5 2.8 %collective-permute-done = bf16[128,256]{1,0:T(8,128)(2,1)S(1)} collective-permute-done((bf16[128,256]{1,0:T(8,128)(2,1)S(1)}, bf16[128,256]{1,0:T(8,128)(2,1)S(1)}, u32[]{:S(2)}, u32[]{:S(2)}) %collective-permute-start) | collective-permute-done | bytes 65568 | tf_op jit(solution)/shard_map/ppermute | solution.py:362
  23.3 3.8 %all-to-all-done.kv_own = bf16[8,128,256]{2,1,0:T(8,128)(2,1)S(1)} async-done(((bf16[8,128,256]{2,1,0:T(8,128)(2,1)}), bf16[8,128,256]{2,1,0:T(8,128)(2,1)S(1)}, u32[]{:S(2)}, u32[]{:S(2)}) %all-to-all-start) | async-done | bytes 524320 | tf_op jit(solution)/shard_map/all_to_all | solution.py:356
  27.1 0.8 broadcast_in_dim.49
  27.9 3.6 %all-to-all-start.1 = ((bf16[8,128,256]{2,1,0:T(8,128)(2,1)}), bf16[8,128,256]{2,1,0:T(8,128)(2,1)S(1)}, u32[]{:S(2)}, u32[]{:S(2)}) async-start(bf16[8,128,256]{2,1,0:T(8,128)(2,1)} %broadcast_in_dim.49), calls=%async_computation.1 | async-start | bytes 1048576 | tf_op jit(solution)/shard_map/all_to_all | solution.py:356
  31.5 0.0 copy-start.5
  31.6 0.0 copy-start.6
  31.6 0.6 copy-done.5
  32.2 0.0 copy-done.6
  32.3 0.1 maximum_bitcast_fusion.freq
  32.3 0.7 copy-done.3
  33.0 3.2 %prep.1 = (f32[2048,128]{1,0:T(8,128)S(1)}, f32[128,128]{1,0:T(8,128)S(1)}, bf16[1024,128]{1,0:T(8,128)(2,1)S(1)}, bf16[1024,128]{1,0:T(8,128)(2,1)S(1)}) custom-call(s32[1]{0:T(128)} %bitcast.token_ref, s32[1,32]{1,0:T(1,128)S(1)} %copy-done.3, f32[1,128]{1,0:T(1,128)S(1)} %maximum_bitcast_fusion.freq, bf16[128,1024]{1,0:T(8,128)(2,1)S(1)} %bitcast.14, ...), custom_call_target="tpu_custom_call" | custom-call | flops 40000000 | bytes 4000000 | tf_op jit(solution)/shard_map/prep/pallas_call | solution.py:257
  36.2 13.2 %all-to-all-done.1.kv_other = bf16[8,128,256]{2,1,0:T(8,128)(2,1)S(1)} async-done(((bf16[8,128,256]{2,1,0:T(8,128)(2,1)}), bf16[8,128,256]{2,1,0:T(8,128)(2,1)S(1)}, u32[]{:S(2)}, u32[]{:S(2)}) %all-to-all-start.1) | async-done | bytes 524320 | tf_op jit(solution)/shard_map/all_to_all | solution.py:356
  49.4 4.6 %attend.1 = (bf16[128,1024]{1,0:T(8,128)(2,1)}, f32[128,1024]{1,0:T(8,128)S(1)}, bf16[8,256,256]{2,1,0:T(8,128)(2,1)}, f32[8,128]{1,0:T(8,128)S(1)}) custom-call(s32[1]{0:T(128)} %bitcast.token_ref, s32[1,32]{1,0:T(1,128)S(1)} %copy-done.3, bf16[8,128,256]{2,1,0:T(8,128)(2,1)S(1)} %all-to-all-done.kv_own, bf16[8,128,256]{2,1,0:T(8,128)(2,1)S(1)} %all-to-all-done.1.kv_other, ...), custom_call_target="tpu_custom_call" | custom-call | flops 3200000000 | bytes 8000000 | tf_op jit(solution)/shard_map/attend/pallas_call | solution.py:287
  54.1 8.5 %all-to-all-start.2 = ((bf16[8,256,256]{2,1,0:T(8,128)(2,1)}), bf16[8,256,256]{2,1,0:T(8,128)(2,1)S(1)}, u32[]{:S(2)}, u32[]{:S(2)}) async-start(bf16[8,256,256]{2,1,0:T(8,128)(2,1)} %get-tuple-element.28), calls=%async_computation.2 | async-start | bytes 2097152 | tf_op jit(solution)/shard_map/all_to_all | solution.py:356
  62.5 2.1 %query.1 = (bf16[128,1024]{1,0:T(8,128)(2,1)}, f32[8,256]{1,0:T(8,128)S(1)}) custom-call(f32[128,1024]{1,0:T(8,128)S(1)} %get-tuple-element.24.dqt_ref, f32[8,128]{1,0:T(8,128)S(1)} %get-tuple-element.25.key_sum_ref, f32[128,128]{1,0:T(8,128)S(1)} %get-tuple-element.26.table_own, bf16[128,1024]{1,0:T(8,128)(2,1)S(1)} %bitcast.15, f32[8,128]{1,0:T(8,128)S(1)} %stack.8.gain_ref), custom_call_target="tpu_custom_call" | custom-call | flops 5000000 | bytes 2000000 | tf_op jit(solution)/shard_map/query/pallas_call | solution.py:302
  64.6 2.4 %psum.14 = f32[256]{0:T(256)S(1)} all-reduce(f32[256]{0:T(256)S(1)} %bitcast.30), channel_id=1, replica_groups={{0,16},{32,48},{64,80},{96,112},{128,144},{160,176},{192,208},{224,240}..., use_global_device_ids=true, to_apply=%region_2.0 | all-reduce | flops 256 | bytes 2048 | tf_op jit(solution)/shard_map/psum | solution.py:381
  67.1 20.5 %psum.15 = f32[256]{0:T(256)S(1)} all-reduce(f32[256]{0:T(256)S(1)} %psum.14), channel_id=1, replica_groups={{0,32,64,96,1,33,65,97},{16,48,80,112,17,49,81,113},{2,34,66,98,3,35,67..., use_global_device_ids=true, to_apply=%region_3.0 | all-reduce | flops 256 | bytes 2048 | tf_op jit(solution)/shard_map/psum | solution.py:382
  87.6 0.0 all-to-all-done.2
  87.6 0.1 slice_reduce_fusion
  87.6 0.6 broadcast_in_dim.55
  88.3 13.0 %all-to-all-start.3 = ((f32[32,1,256]{2,1,0:T(1,128)}), f32[32,1,256]{2,1,0:T(1,128)S(1)}, u32[]{:S(2)}, u32[]{:S(2)}) async-start(f32[32,1,256]{2,1,0:T(1,128)} %broadcast_in_dim.55), calls=%async_computation.3 | async-start | bytes 65536 | tf_op jit(solution)/shard_map/all_to_all | solution.py:385
  101.3 4.8 %collective-permute-start.1 = (bf16[128,256]{1,0:T(8,128)(2,1)S(1)}, bf16[128,256]{1,0:T(8,128)(2,1)S(1)}, u32[]{:S(2)}, u32[]{:S(2)}) collective-permute-start(bf16[128,256]{1,0:T(8,128)(2,1)S(1)} %slice_reduce_fusion), channel_id=1, source_target_pairs={{0,1},{1,0},{2,3},{3,2},{4,5},{5,4},{6,7},{7,6},{8,9},{9,8},{10,11... | collective-permute-start | bytes 196616 | tf_op jit(solution)/shard_map/ppermute | solution.py:384
  106.1 0.1 convert_reduce_fusion.own_ref
  106.1 3.8 %all-to-all-done.3 = f32[32,1,256]{2,1,0:T(1,128)S(1)} async-done(((f32[32,1,256]{2,1,0:T(1,128)}), f32[32,1,256]{2,1,0:T(1,128)S(1)}, u32[]{:S(2)}, u32[]{:S(2)}) %all-to-all-start.3) | async-done | bytes 32800 | tf_op jit(solution)/shard_map/all_to_all | solution.py:385
  110.0 0.1 reduce_sum.32
  110.0 0.5 fusion
  110.6 1.2 %collective-permute-done.1.other_ref = bf16[128,256]{1,0:T(8,128)(2,1)S(1)} collective-permute-done((bf16[128,256]{1,0:T(8,128)(2,1)S(1)}, bf16[128,256]{1,0:T(8,128)(2,1)S(1)}, u32[]{:S(2)}, u32[]{:S(2)}) %collective-permute-start.1) | collective-permute-done | bytes 65568 | tf_op jit(solution)/shard_map/ppermute | solution.py:384
  111.8 0.8 finish.1
  (14 shorter events, 0.1 us)
Async XLA Ops:
  0.6 0.8 copy-start.4
  2.4 7.2 %copy-start.1 = (bf16[1,128,128]{2,1,0:T(8,128)(2,1)S(1)}, bf16[1,128,128]{2,1,0:T(8,128)(2,1)}, u32[]{:S(2)}) copy-start(bf16[1,128,128]{2,1,0:T(8,128)(2,1)} %param.8) | copy-start | bytes 98308
  2.4 24.7 %all-to-all-start = ((bf16[8,128,256]{2,1,0:T(8,128)(2,1)}), bf16[8,128,256]{2,1,0:T(8,128)(2,1)S(1)}, u32[]{:S(2)}, u32[]{:S(2)}) async-start(bf16[8,128,256]{2,1,0:T(8,128)(2,1)} %pad_maximum_fusion), calls=%async_computation | async-start | bytes 1048576 | tf_op jit(solution)/shard_map/all_to_all | solution.py:356
  9.6 13.7 %collective-permute-start = (bf16[128,256]{1,0:T(8,128)(2,1)S(1)}, bf16[128,256]{1,0:T(8,128)(2,1)S(1)}, u32[]{:S(2)}, u32[]{:S(2)}) collective-permute-start(bf16[128,256]{1,0:T(8,128)(2,1)S(1)} %pad_maximum_fusion.1), channel_id=1, source_target_pairs={{0,1},{1,0},{2,3},{3,2},{4,5},{5,4},{6,7},{7,6},{8,9},{9,8},{10,11... | collective-permute-start | bytes 196616 | tf_op jit(solution)/shard_map/ppermute | solution.py:362
  27.9 4.4 %copy-start = (bf16[1,128,1024]{2,1,0:T(8,128)(2,1)S(1)}, bf16[1,128,1024]{2,1,0:T(8,128)(2,1)}, u32[]{:S(2)}) copy-start(bf16[1,128,1024]{2,1,0:T(8,128)(2,1)} %param.7) | copy-start | bytes 786436
  27.9 4.4 %copy-start.2 = (bf16[1,128,1024]{2,1,0:T(8,128)(2,1)S(1)}, bf16[1,128,1024]{2,1,0:T(8,128)(2,1)}, u32[]{:S(2)}) copy-start(bf16[1,128,1024]{2,1,0:T(8,128)(2,1)} %param.10) | copy-start | bytes 786436
  27.9 21.5 %all-to-all-start.1 = ((bf16[8,128,256]{2,1,0:T(8,128)(2,1)}), bf16[8,128,256]{2,1,0:T(8,128)(2,1)S(1)}, u32[]{:S(2)}, u32[]{:S(2)}) async-start(bf16[8,128,256]{2,1,0:T(8,128)(2,1)} %broadcast_in_dim.49), calls=%async_computation.1 | async-start | bytes 1048576 | tf_op jit(solution)/shard_map/all_to_all | solution.py:356
  31.5 0.7 copy-start.5
  31.6 0.7 copy-start.6
  32.3 0.7 copy-start.3
  54.1 33.5 %all-to-all-start.2 = ((bf16[8,256,256]{2,1,0:T(8,128)(2,1)}), bf16[8,256,256]{2,1,0:T(8,128)(2,1)S(1)}, u32[]{:S(2)}, u32[]{:S(2)}) async-start(bf16[8,256,256]{2,1,0:T(8,128)(2,1)} %get-tuple-element.28), calls=%async_computation.2 | async-start | bytes 2097152 | tf_op jit(solution)/shard_map/all_to_all | solution.py:356
  88.3 21.7 %all-to-all-start.3 = ((f32[32,1,256]{2,1,0:T(1,128)}), f32[32,1,256]{2,1,0:T(1,128)S(1)}, u32[]{:S(2)}, u32[]{:S(2)}) async-start(f32[32,1,256]{2,1,0:T(1,128)} %broadcast_in_dim.55), calls=%async_computation.3 | async-start | bytes 65536 | tf_op jit(solution)/shard_map/all_to_all | solution.py:385
  101.3 10.5 %collective-permute-start.1 = (bf16[128,256]{1,0:T(8,128)(2,1)S(1)}, bf16[128,256]{1,0:T(8,128)(2,1)S(1)}, u32[]{:S(2)}, u32[]{:S(2)}) collective-permute-start(bf16[128,256]{1,0:T(8,128)(2,1)S(1)} %slice_reduce_fusion), channel_id=1, source_target_pairs={{0,1},{1,0},{2,3},{3,2},{4,5},{5,4},{6,7},{7,6},{8,9},{9,8},{10,11... | collective-permute-start | bytes 196616 | tf_op jit(solution)/shard_map/ppermute | solution.py:384

commit v6 on v5

--- a/solution.py
+++ b/solution.py
@@ -236,6 +236,13 @@
     gains_ref[:, D:] = jnp.broadcast_to(jnp.sum(key_sum_ref[...], axis=0, keepdims=True), (8, D))
 
 
+def copies_kernel(*refs):
+    out_ref = refs[-1]
+    rows = jnp.concatenate([ref[...] for ref in refs[:-1]], axis=1)
+    for i in range(out_ref.shape[0]):
+        out_ref[i] = rows
+
+
 def finish_kernel(own_ref, other_ref, k_raw, gain_ref, table_own, dk_ref, dv_ref):
     total = own_ref[...] + other_ref[...].astype(F32)
     unit, inverse = unit_of(k_raw[...])
@@ -297,6 +304,20 @@
     )(token, lengths, kv_own, kv_other, table, q_rows, do_rows, both_gains)
 
 
+def call_copies(count, *parts):
+    shape = (count, parts[0].shape[0], sum(part.shape[1] for part in parts))
+    size = math.prod(shape) * parts[0].dtype.itemsize
+    return pl.pallas_call(
+        copies_kernel,
+        out_shape=jax.ShapeDtypeStruct(shape, parts[0].dtype),
+        in_specs=[VM] * len(parts),
+        out_specs=VM,
+        compiler_params=pltpu.CompilerParams(vmem_limit_bytes=4 * 2**20),
+        cost_estimate=pl.CostEstimate(flops=0, bytes_accessed=size, transcendentals=0),
+        name="copies",
+    )(*parts)
+
+
 def call_query(dqt, key_sum, table_own, q_raw, both_gains, **kw):
     heads = q_raw.shape[1] // D
     return pl.pallas_call(
@@ -363,7 +384,7 @@
     kv_own = exchange(
         jnp.concatenate([spread(key_raw[0]), spread(values[0])], axis=2)
     )
-    kv_other = exchange(spread(kv_swapped))
+    kv_other = exchange(call_copies(half, kv_swapped))
     table, table_own, q_rows, do_rows = call_prep(token, doc_lengths, frequency_row(), query_raw[0], out_grad[0], both_gains, seq)
     output, dqt, parts, key_sum = call_attend(
         token, doc_lengths, kv_own, kv_other, table, q_rows, do_rows, both_gains
@@ -380,11 +401,10 @@
     along_xy = [[flat(x, y, z, core) for x in xs for y in ys] for z in zs for core in cores]
     gains = lax.psum(gains[0], "dp", axis_index_groups=strided(dp, 1, 2))
     gains = lax.psum(gains, ("dp", "ctx"), axis_index_groups=along_z)
-    theirs, gains = lax.optimization_barrier((theirs, gains))
+    copies = call_copies(len(along_xy[0]), gains[None])
+    theirs, copies = lax.optimization_barrier((theirs, copies))
     other = lax.ppermute(theirs, "ctx", swap)
-    gains = lax.all_to_all(
-        jnp.broadcast_to(gains[None, None], (len(along_xy[0]), 1, 2 * D)), ("dp", "ctx"), 0, 0, axis_index_groups=along_xy
-    )
+    gains = lax.all_to_all(copies, ("dp", "ctx"), 0, 0, axis_index_groups=along_xy)
     gains = jnp.sum(gains, axis=(0, 1))
     dk, dv = call_finish(own, other, key_raw[0], both_gains, table_own)
     return (output[None], dq[None], dk[None], dv[None], gains[:D], gains[D:])

time: 113 us -> 112 us (level)
  starting transfers between devices: 48 us -> 44.8 us
  blocking collectives: 22.9 us -> 24.9 us
  local copies, waits for them, and re-layouts: 4.17 us -> 2.71 us
  Pallas kernels: 10.8 us -> 12.2 us
    psum x1, blocking collectives: 20.5 us -> 22.4 us  [body(): gains = lax.psum(gains, ('dp', 'ctx'), axis_index_groups=along_z)]
    all_to_all x1, starting transfers between devices: 13 us -> 11.1 us  [body(): lax.all_to_all(copies, ('dp', 'ctx'), 0, 0, axis_index_groups=along_xy)]
    ppermute x1, starting transfers between devices: 4.75 us -> 3.06 us  [body(): other = lax.ppermute(theirs, 'ctx', swap)]
    all_to_all x1, waiting for transfers between devices: 3.84 us -> 5.52 us  [body(): lax.all_to_all(copies, ('dp', 'ctx'), 0, 0, axis_index_groups=along_xy)]
    pallas_call x0 -> x2, Pallas kernels: none -> 1.45 us  [call_copies(): pl.pallas_call(copies_kernel, out_shape=jax.ShapeDtypeStruct(shape, parts...]
    all_to_all x3, waiting for transfers between devices: 17 us -> 15.6 us  [exchange(): return lax.all_to_all(blocks, 'ctx', 0, 0, axis_index_groups=columns)]
  transfers between devices with their start and end apart: 6 -> 6, of which waited for: 5 -> 5; matrix products, arithmetic and copies ran while one was open for 1% -> 1% of each run, Pallas kernels for 5% -> 6%
where the time goes in v6:
time: 112 us; the launch traced here: 111 us
  starting transfers between devices  44.8 us (40%)
  blocking collectives  24.9 us (22%)
  waiting for transfers between devices  24.7 us (22%)
  Pallas kernels  12.2 us (11%)
  local copies, waits for them, and re-layouts  2.71 us (2%)
  other arithmetic  1.15 us (1%)
    psum x1, blocking collectives, body(): gains = lax.psum(gains, ('dp', 'ctx'), axis_index_groups=along_z)  22.4 us
    all_to_all x3, starting transfers between devices, exchange(): return lax.all_to_all(blocks, 'ctx', 0, 0, axis_index_groups=columns)  19.7 us
    all_to_all x3, waiting for transfers between devices, exchange(): return lax.all_to_all(blocks, 'ctx', 0, 0, axis_index_groups=columns)  15.6 us
    all_to_all x1, starting transfers between devices, body(): lax.all_to_all(copies, ('dp', 'ctx'), 0, 0, axis_index_groups=along_xy)  11.1 us
    ppermute x1, starting transfers between devices, body(): kv_swapped = lax.ppermute(kv, 'ctx', swap)  10.9 us
    all_to_all x1, waiting for transfers between devices, body(): lax.all_to_all(copies, ('dp', 'ctx'), 0, 0, axis_index_groups=along_xy)  5.52 us
    pallas_call x1, Pallas kernels, call_attend(): pl.pallas_call(functools.partial(attend_kernel, heads), out_shape=[jax.Sh...  4.65 us
    pallas_call x1, Pallas kernels, call_prep(): pl.pallas_call(functools.partial(prep_kernel, heads), out_shape=[jax.Shap...  3.2 us
  transfers between devices with their start and end apart: 6, of which 5 were waited for; matrix products, arithmetic and copies ran while one was open for 1% of the time, Pallas kernels for 6%

profile of v6, /device:TPU:2, one launch (start us, length us, event | category | flops | bytes accessed | tf_op | source)
XLA Modules:
  0.0 111.3 jit_solution(8717274197243525244)
XLA Ops:
  0.6 0.8 broadcast_in_dim.37
  1.4 0.0 copy-done.4
  1.5 0.9 pad_maximum_fusion
  2.4 7.2 %all-to-all-start = ((bf16[8,128,256]{2,1,0:T(8,128)(2,1)}), bf16[8,128,256]{2,1,0:T(8,128)(2,1)S(1)}, u32[]{:S(2)}, u32[]{:S(2)}) async-start(bf16[8,128,256]{2,1,0:T(8,128)(2,1)} %pad_maximum_fusion), calls=%async_computation | async-start | bytes 1048576 | tf_op jit(solution)/shard_map/all_to_all | solution.py:377
  9.6 10.9 %collective-permute-start = (bf16[128,256]{1,0:T(8,128)(2,1)S(1)}, bf16[128,256]{1,0:T(8,128)(2,1)S(1)}, u32[]{:S(2)}, u32[]{:S(2)}) collective-permute-start(bf16[128,256]{1,0:T(8,128)(2,1)S(1)} %pad_maximum_fusion.1), channel_id=1, source_target_pairs={{0,1},{1,0},{2,3},{3,2},{4,5},{5,4},{6,7},{7,6},{8,9},{9,8},{10,11... | collective-permute-start | bytes 196616 | tf_op jit(solution)/shard_map/ppermute | solution.py:383
  20.5 2.8 %collective-permute-done.refs_0_ = bf16[128,256]{1,0:T(8,128)(2,1)S(1)} collective-permute-done((bf16[128,256]{1,0:T(8,128)(2,1)S(1)}, bf16[128,256]{1,0:T(8,128)(2,1)S(1)}, u32[]{:S(2)}, u32[]{:S(2)}) %collective-permute-start) | collective-permute-done | bytes 65568 | tf_op jit(solution)/shard_map/ppermute | solution.py:383
  23.3 0.8 copies.2
  24.1 3.0 %all-to-all-done.kv_own = bf16[8,128,256]{2,1,0:T(8,128)(2,1)S(1)} async-done(((bf16[8,128,256]{2,1,0:T(8,128)(2,1)}), bf16[8,128,256]{2,1,0:T(8,128)(2,1)S(1)}, u32[]{:S(2)}, u32[]{:S(2)}) %all-to-all-start) | async-done | bytes 524320 | tf_op jit(solution)/shard_map/all_to_all | solution.py:377
  27.1 4.1 %all-to-all-start.1 = ((bf16[8,128,256]{2,1,0:T(8,128)(2,1)}), bf16[8,128,256]{2,1,0:T(8,128)(2,1)S(1)}, u32[]{:S(2)}, u32[]{:S(2)}) async-start(bf16[8,128,256]{2,1,0:T(8,128)(2,1)} %copies.2), calls=%async_computation.1 | async-start | bytes 1048576 | tf_op jit(solution)/shard_map/all_to_all | solution.py:377
  31.1 0.0 copy-start.6
  31.2 0.6 copy-done.5
  31.8 0.0 copy-done.6
  31.9 0.1 maximum_bitcast_fusion.freq
  31.9 0.7 copy-done.3
  32.6 3.2 %prep.1 = (f32[2048,128]{1,0:T(8,128)S(1)}, f32[128,128]{1,0:T(8,128)S(1)}, bf16[1024,128]{1,0:T(8,128)(2,1)S(1)}, bf16[1024,128]{1,0:T(8,128)(2,1)S(1)}) custom-call(s32[1]{0:T(128)} %bitcast.token_ref, s32[1,32]{1,0:T(1,128)S(1)} %copy-done.3, f32[1,128]{1,0:T(1,128)S(1)} %maximum_bitcast_fusion.freq, bf16[128,1024]{1,0:T(8,128)(2,1)S(1)} %bitcast.15, ...), custom_call_target="tpu_custom_call" | custom-call | flops 40000000 | bytes 4000000 | tf_op jit(solution)/shard_map/prep/pallas_call | solution.py:264
  35.8 12.6 %all-to-all-done.1.kv_other = bf16[8,128,256]{2,1,0:T(8,128)(2,1)S(1)} async-done(((bf16[8,128,256]{2,1,0:T(8,128)(2,1)}), bf16[8,128,256]{2,1,0:T(8,128)(2,1)S(1)}, u32[]{:S(2)}, u32[]{:S(2)}) %all-to-all-start.1) | async-done | bytes 524320 | tf_op jit(solution)/shard_map/all_to_all | solution.py:377
  48.4 4.6 %attend.1 = (bf16[128,1024]{1,0:T(8,128)(2,1)}, f32[128,1024]{1,0:T(8,128)S(1)}, bf16[8,256,256]{2,1,0:T(8,128)(2,1)}, f32[8,128]{1,0:T(8,128)S(1)}) custom-call(s32[1]{0:T(128)} %bitcast.token_ref, s32[1,32]{1,0:T(1,128)S(1)} %copy-done.3, bf16[8,128,256]{2,1,0:T(8,128)(2,1)S(1)} %all-to-all-done.kv_own, bf16[8,128,256]{2,1,0:T(8,128)(2,1)S(1)} %all-to-all-done.1.kv_other, ...), custom_call_target="tpu_custom_call" | custom-call | flops 3200000000 | bytes 8000000 | tf_op jit(solution)/shard_map/attend/pallas_call | solution.py:294
  53.1 8.4 %all-to-all-start.2 = ((bf16[8,256,256]{2,1,0:T(8,128)(2,1)}), bf16[8,256,256]{2,1,0:T(8,128)(2,1)S(1)}, u32[]{:S(2)}, u32[]{:S(2)}) async-start(bf16[8,256,256]{2,1,0:T(8,128)(2,1)} %get-tuple-element.28), calls=%async_computation.2 | async-start | bytes 2097152 | tf_op jit(solution)/shard_map/all_to_all | solution.py:377
  61.5 2.1 %query.1 = (bf16[128,1024]{1,0:T(8,128)(2,1)}, f32[8,256]{1,0:T(8,128)S(1)}) custom-call(f32[128,1024]{1,0:T(8,128)S(1)} %get-tuple-element.24.dqt_ref, f32[8,128]{1,0:T(8,128)S(1)} %get-tuple-element.25.key_sum_ref, f32[128,128]{1,0:T(8,128)S(1)} %get-tuple-element.26.table_own, bf16[128,1024]{1,0:T(8,128)(2,1)S(1)} %bitcast.16, f32[8,128]{1,0:T(8,128)S(1)} %stack.8.gain_ref), custom_call_target="tpu_custom_call" | custom-call | flops 5000000 | bytes 2000000 | tf_op jit(solution)/shard_map/query/pallas_call | solution.py:323
  63.6 2.4 %psum.14 = f32[256]{0:T(256)S(1)} all-reduce(f32[256]{0:T(256)S(1)} %bitcast.31), channel_id=1, replica_groups={{0,16},{32,48},{64,80},{96,112},{128,144},{160,176},{192,208},{224,240}..., use_global_device_ids=true, to_apply=%region_2.0 | all-reduce | flops 256 | bytes 2048 | tf_op jit(solution)/shard_map/psum | solution.py:402
  66.1 22.4 %psum.15.refs_0_ = f32[1,256]{1,0:T(1,128)S(1)} all-reduce(f32[1,256]{1,0:T(1,128)S(1)} %bitcast.32), channel_id=1, replica_groups={{0,32,64,96,1,33,65,97},{16,48,80,112,17,49,81,113},{2,34,66,98,3,35,67..., use_global_device_ids=true, to_apply=%region_3.0 | all-reduce | flops 256 | bytes 2048 | tf_op jit(solution)/shard_map/psum | solution.py:403
  88.5 0.6 copies.3
  89.2 0.0 all-to-all-done.2
  89.2 0.1 slice_reduce_fusion
  89.2 11.1 %all-to-all-start.3 = ((f32[32,1,256]{2,1,0:T(1,128)}), f32[32,1,256]{2,1,0:T(1,128)S(1)}, u32[]{:S(2)}, u32[]{:S(2)}) async-start(f32[32,1,256]{2,1,0:T(1,128)} %copies.3), calls=%async_computation.3 | async-start | bytes 65536 | tf_op jit(solution)/shard_map/all_to_all | solution.py:407
  100.4 3.1 %collective-permute-start.1 = (bf16[128,256]{1,0:T(8,128)(2,1)S(1)}, bf16[128,256]{1,0:T(8,128)(2,1)S(1)}, u32[]{:S(2)}, u32[]{:S(2)}) collective-permute-start(bf16[128,256]{1,0:T(8,128)(2,1)S(1)} %slice_reduce_fusion), channel_id=1, source_target_pairs={{0,1},{1,0},{2,3},{3,2},{4,5},{5,4},{6,7},{7,6},{8,9},{9,8},{10,11... | collective-permute-start | bytes 196616 | tf_op jit(solution)/shard_map/ppermute | solution.py:406
  103.4 0.1 convert_reduce_fusion.own_ref
  103.5 5.5 %all-to-all-done.3 = f32[32,1,256]{2,1,0:T(1,128)S(1)} async-done(((f32[32,1,256]{2,1,0:T(1,128)}), f32[32,1,256]{2,1,0:T(1,128)S(1)}, u32[]{:S(2)}, u32[]{:S(2)}) %all-to-all-start.3) | async-done | bytes 32800 | tf_op jit(solution)/shard_map/all_to_all | solution.py:407
  109.0 0.1 reduce_sum.32
  109.1 0.5 fusion
  109.6 0.8 collective-permute-done.1.other_ref
  110.4 0.8 finish.1
  (14 shorter events, 0.1 us)
Async XLA Ops:
  0.6 0.8 copy-start.4
  2.4 7.2 %copy-start.1 = (bf16[1,128,128]{2,1,0:T(8,128)(2,1)S(1)}, bf16[1,128,128]{2,1,0:T(8,128)(2,1)}, u32[]{:S(2)}) copy-start(bf16[1,128,128]{2,1,0:T(8,128)(2,1)} %param.8) | copy-start | bytes 98308
  2.4 24.7 %all-to-all-start = ((bf16[8,128,256]{2,1,0:T(8,128)(2,1)}), bf16[8,128,256]{2,1,0:T(8,128)(2,1)S(1)}, u32[]{:S(2)}, u32[]{:S(2)}) async-start(bf16[8,128,256]{2,1,0:T(8,128)(2,1)} %pad_maximum_fusion), calls=%async_computation | async-start | bytes 1048576 | tf_op jit(solution)/shard_map/all_to_all | solution.py:377
  9.6 13.7 %collective-permute-start = (bf16[128,256]{1,0:T(8,128)(2,1)S(1)}, bf16[128,256]{1,0:T(8,128)(2,1)S(1)}, u32[]{:S(2)}, u32[]{:S(2)}) collective-permute-start(bf16[128,256]{1,0:T(8,128)(2,1)S(1)} %pad_maximum_fusion.1), channel_id=1, source_target_pairs={{0,1},{1,0},{2,3},{3,2},{4,5},{5,4},{6,7},{7,6},{8,9},{9,8},{10,11... | collective-permute-start | bytes 196616 | tf_op jit(solution)/shard_map/ppermute | solution.py:383
  24.1 7.8 %copy-start = (bf16[1,128,1024]{2,1,0:T(8,128)(2,1)S(1)}, bf16[1,128,1024]{2,1,0:T(8,128)(2,1)}, u32[]{:S(2)}) copy-start(bf16[1,128,1024]{2,1,0:T(8,128)(2,1)} %param.7) | copy-start | bytes 786436
  24.1 7.8 %copy-start.2 = (bf16[1,128,1024]{2,1,0:T(8,128)(2,1)S(1)}, bf16[1,128,1024]{2,1,0:T(8,128)(2,1)}, u32[]{:S(2)}) copy-start(bf16[1,128,1024]{2,1,0:T(8,128)(2,1)} %param.10) | copy-start | bytes 786436
  27.1 21.4 %all-to-all-start.1 = ((bf16[8,128,256]{2,1,0:T(8,128)(2,1)}), bf16[8,128,256]{2,1,0:T(8,128)(2,1)S(1)}, u32[]{:S(2)}, u32[]{:S(2)}) async-start(bf16[8,128,256]{2,1,0:T(8,128)(2,1)} %copies.2), calls=%async_computation.1 | async-start | bytes 1048576 | tf_op jit(solution)/shard_map/all_to_all | solution.py:377
  31.1 0.7 copy-start.5
  31.1 0.7 copy-start.6
  31.9 0.7 copy-start.3
  53.1 36.1 %all-to-all-start.2 = ((bf16[8,256,256]{2,1,0:T(8,128)(2,1)}), bf16[8,256,256]{2,1,0:T(8,128)(2,1)S(1)}, u32[]{:S(2)}, u32[]{:S(2)}) async-start(bf16[8,256,256]{2,1,0:T(8,128)(2,1)} %get-tuple-element.28), calls=%async_computation.2 | async-start | bytes 2097152 | tf_op jit(solution)/shard_map/all_to_all | solution.py:377
  89.2 19.8 %all-to-all-start.3 = ((f32[32,1,256]{2,1,0:T(1,128)}), f32[32,1,256]{2,1,0:T(1,128)S(1)}, u32[]{:S(2)}, u32[]{:S(2)}) async-start(f32[32,1,256]{2,1,0:T(1,128)} %copies.3), calls=%async_computation.3 | async-start | bytes 65536 | tf_op jit(solution)/shard_map/all_to_all | solution.py:407
  100.4 10.1 %collective-permute-start.1 = (bf16[128,256]{1,0:T(8,128)(2,1)S(1)}, bf16[128,256]{1,0:T(8,128)(2,1)S(1)}, u32[]{:S(2)}, u32[]{:S(2)}) collective-permute-start(bf16[128,256]{1,0:T(8,128)(2,1)S(1)} %slice_reduce_fusion), channel_id=1, source_target_pairs={{0,1},{1,0},{2,3},{3,2},{4,5},{5,4},{6,7},{7,6},{8,9},{9,8},{10,11... | collective-permute-start | bytes 196616 | tf_op jit(solution)/shard_map/ppermute | solution.py:406

commit v7 on v6

--- a/solution.py
+++ b/solution.py
@@ -398,13 +398,13 @@
 
     xs, ys, zs, cores = range(dp // 8), range(half), range(8), range(2)
     along_z = [[flat(x, y, z, core) for z in zs] for x in xs for y in ys for core in cores]
-    along_xy = [[flat(x, y, z, core) for x in xs for y in ys] for z in zs for core in cores]
-    gains = lax.psum(gains[0], "dp", axis_index_groups=strided(dp, 1, 2))
+    along_y = [[flat(x, y, z, core) for y in ys for core in cores] for x in xs for z in zs]
+    gains = lax.psum(gains[0], "dp", axis_index_groups=strided(dp, 8, dp // 8))
     gains = lax.psum(gains, ("dp", "ctx"), axis_index_groups=along_z)
-    copies = call_copies(len(along_xy[0]), gains[None])
+    copies = call_copies(len(along_y[0]), gains[None])
     theirs, copies = lax.optimization_barrier((theirs, copies))
     other = lax.ppermute(theirs, "ctx", swap)
-    gains = lax.all_to_all(copies, ("dp", "ctx"), 0, 0, axis_index_groups=along_xy)
+    gains = lax.all_to_all(copies, ("dp", "ctx"), 0, 0, axis_index_groups=along_y)
     gains = jnp.sum(gains, axis=(0, 1))
     dk, dv = call_finish(own, other, key_raw[0], both_gains, table_own)
     return (output[None], dq[None], dk[None], dv[None], gains[:D], gains[D:])

time: 112 us -> 116 us (1.036)
  the two profiles are of different devices: /device:TPU:2 before, /device:TPU:1 now
where the time goes in v7:
time: 116 us; the launch traced here: 115 us
  starting transfers between devices  43.6 us (38%)
  blocking collectives  34.6 us (30%)
  waiting for transfers between devices  20.1 us (17%)
  Pallas kernels  12.2 us (11%)
  local copies, waits for them, and re-layouts  2.71 us (2%)
    psum x1, blocking collectives, body(): gains = lax.psum(gains, ('dp', 'ctx'), axis_index_groups=along_z)  19.5 us
    all_to_all x3, starting transfers between devices, exchange(): return lax.all_to_all(blocks, 'ctx', 0, 0, axis_index_groups=columns)  18.5 us
    psum x1, blocking collectives, body(): gains = lax.psum(gains[0], 'dp', axis_index_groups=strided(dp, 8, dp // 8))  15.1 us
    all_to_all x3, waiting for transfers between devices, exchange(): return lax.all_to_all(blocks, 'ctx', 0, 0, axis_index_groups=columns)  11.8 us
    all_to_all x1, starting transfers between devices, body(): lax.all_to_all(copies, ('dp', 'ctx'), 0, 0, axis_index_groups=along_y)  10.7 us
    ppermute x1, starting transfers between devices, body(): kv_swapped = lax.ppermute(kv, 'ctx', swap)  10.6 us
    pallas_call x1, Pallas kernels, call_attend(): pl.pallas_call(functools.partial(attend_kernel, heads), out_shape=[jax.Sh...  4.65 us
    ppermute x1, starting transfers between devices, body(): other = lax.ppermute(theirs, 'ctx', swap)  3.83 us
  transfers between devices with their start and end apart: 6, of which 5 were waited for; matrix products, arithmetic and copies ran while one was open for 1% of the time, Pallas kernels for 6%

profile of v7, /device:TPU:1, one launch (start us, length us, event | category | flops | bytes accessed | tf_op | source)
XLA Modules:
  0.0 115.0 jit_solution(12767469925207409418)
XLA Ops:
  0.6 0.8 broadcast_in_dim.37
  1.5 0.9 pad_maximum_fusion
  2.4 7.8 %all-to-all-start = ((bf16[8,128,256]{2,1,0:T(8,128)(2,1)}), bf16[8,128,256]{2,1,0:T(8,128)(2,1)S(1)}, u32[]{:S(2)}, u32[]{:S(2)}) async-start(bf16[8,128,256]{2,1,0:T(8,128)(2,1)} %pad_maximum_fusion), calls=%async_computation | async-start | bytes 1048576 | tf_op jit(solution)/shard_map/all_to_all | solution.py:377
  10.1 0.0 copy-done.1
  10.2 10.6 %collective-permute-start = (bf16[128,256]{1,0:T(8,128)(2,1)S(1)}, bf16[128,256]{1,0:T(8,128)(2,1)S(1)}, u32[]{:S(2)}, u32[]{:S(2)}) collective-permute-start(bf16[128,256]{1,0:T(8,128)(2,1)S(1)} %pad_maximum_fusion.1), channel_id=1, source_target_pairs={{0,1},{1,0},{2,3},{3,2},{4,5},{5,4},{6,7},{7,6},{8,9},{9,8},{10,11... | collective-permute-start | bytes 196616 | tf_op jit(solution)/shard_map/ppermute | solution.py:383
  20.8 1.7 %collective-permute-done.refs_0_ = bf16[128,256]{1,0:T(8,128)(2,1)S(1)} collective-permute-done((bf16[128,256]{1,0:T(8,128)(2,1)S(1)}, bf16[128,256]{1,0:T(8,128)(2,1)S(1)}, u32[]{:S(2)}, u32[]{:S(2)}) %collective-permute-start) | collective-permute-done | bytes 65568 | tf_op jit(solution)/shard_map/ppermute | solution.py:383
  22.5 0.8 copies.2
  23.3 1.5 %all-to-all-done.kv_own = bf16[8,128,256]{2,1,0:T(8,128)(2,1)S(1)} async-done(((bf16[8,128,256]{2,1,0:T(8,128)(2,1)}), bf16[8,128,256]{2,1,0:T(8,128)(2,1)S(1)}, u32[]{:S(2)}, u32[]{:S(2)}) %all-to-all-start) | async-done | bytes 524320 | tf_op jit(solution)/shard_map/all_to_all | solution.py:377
  24.9 5.2 %all-to-all-start.1 = ((bf16[8,128,256]{2,1,0:T(8,128)(2,1)}), bf16[8,128,256]{2,1,0:T(8,128)(2,1)S(1)}, u32[]{:S(2)}, u32[]{:S(2)}) async-start(bf16[8,128,256]{2,1,0:T(8,128)(2,1)} %copies.2), calls=%async_computation.1 | async-start | bytes 1048576 | tf_op jit(solution)/shard_map/all_to_all | solution.py:377
  30.1 0.0 copy-start.6
  30.1 0.6 copy-done.5
  30.8 0.0 copy-done.6
  30.8 0.1 maximum_bitcast_fusion.freq
  30.9 0.0 copy-done
  30.9 0.7 copy-done.3
  31.6 3.2 %prep.1 = (f32[2048,128]{1,0:T(8,128)S(1)}, f32[128,128]{1,0:T(8,128)S(1)}, bf16[1024,128]{1,0:T(8,128)(2,1)S(1)}, bf16[1024,128]{1,0:T(8,128)(2,1)S(1)}) custom-call(s32[1]{0:T(128)} %bitcast.token_ref, s32[1,32]{1,0:T(1,128)S(1)} %copy-done.3, f32[1,128]{1,0:T(1,128)S(1)} %maximum_bitcast_fusion.freq, bf16[128,1024]{1,0:T(8,128)(2,1)S(1)} %bitcast.15, ...), custom_call_target="tpu_custom_call" | custom-call | flops 40000000 | bytes 4000000 | tf_op jit(solution)/shard_map/prep/pallas_call | solution.py:264
  34.8 10.3 %all-to-all-done.1.kv_other = bf16[8,128,256]{2,1,0:T(8,128)(2,1)S(1)} async-done(((bf16[8,128,256]{2,1,0:T(8,128)(2,1)}), bf16[8,128,256]{2,1,0:T(8,128)(2,1)S(1)}, u32[]{:S(2)}, u32[]{:S(2)}) %all-to-all-start.1) | async-done | bytes 524320 | tf_op jit(solution)/shard_map/all_to_all | solution.py:377
  45.1 4.6 %attend.1 = (bf16[128,1024]{1,0:T(8,128)(2,1)}, f32[128,1024]{1,0:T(8,128)S(1)}, bf16[8,256,256]{2,1,0:T(8,128)(2,1)}, f32[8,128]{1,0:T(8,128)S(1)}) custom-call(s32[1]{0:T(128)} %bitcast.token_ref, s32[1,32]{1,0:T(1,128)S(1)} %copy-done.3, bf16[8,128,256]{2,1,0:T(8,128)(2,1)S(1)} %all-to-all-done.kv_own, bf16[8,128,256]{2,1,0:T(8,128)(2,1)S(1)} %all-to-all-done.1.kv_other, ...), custom_call_target="tpu_custom_call" | custom-call | flops 3200000000 | bytes 8000000 | tf_op jit(solution)/shard_map/attend/pallas_call | solution.py:294
  49.7 5.5 %all-to-all-start.2 = ((bf16[8,256,256]{2,1,0:T(8,128)(2,1)}), bf16[8,256,256]{2,1,0:T(8,128)(2,1)S(1)}, u32[]{:S(2)}, u32[]{:S(2)}) async-start(bf16[8,256,256]{2,1,0:T(8,128)(2,1)} %get-tuple-element.28), calls=%async_computation.2 | async-start | bytes 2097152 | tf_op jit(solution)/shard_map/all_to_all | solution.py:377
  55.2 2.1 %query.1 = (bf16[128,1024]{1,0:T(8,128)(2,1)}, f32[8,256]{1,0:T(8,128)S(1)}) custom-call(f32[128,1024]{1,0:T(8,128)S(1)} %get-tuple-element.24.dqt_ref, f32[8,128]{1,0:T(8,128)S(1)} %get-tuple-element.25.key_sum_ref, f32[128,128]{1,0:T(8,128)S(1)} %get-tuple-element.26.table_own, bf16[128,1024]{1,0:T(8,128)(2,1)S(1)} %bitcast.16, f32[8,128]{1,0:T(8,128)S(1)} %stack.8.gain_ref), custom_call_target="tpu_custom_call" | custom-call | flops 5000000 | bytes 2000000 | tf_op jit(solution)/shard_map/query/pallas_call | solution.py:323
  57.3 15.1 %psum.14 = f32[256]{0:T(256)S(1)} all-reduce(f32[256]{0:T(256)S(1)} %bitcast.31), channel_id=1, replica_groups={{0,128,256,384},{16,144,272,400},{32,160,288,416},{48,176,304,432},{64,..., use_global_device_ids=true, to_apply=%region_2.0 | all-reduce | flops 256 | bytes 2048 | tf_op jit(solution)/shard_map/psum | solution.py:402
  72.4 19.5 %psum.15.refs_0_ = f32[1,256]{1,0:T(1,128)S(1)} all-reduce(f32[1,256]{1,0:T(1,128)S(1)} %bitcast.32), channel_id=1, replica_groups={{0,32,64,96,1,33,65,97},{16,48,80,112,17,49,81,113},{2,34,66,98,3,35,67..., use_global_device_ids=true, to_apply=%region_3.0 | all-reduce | flops 256 | bytes 2048 | tf_op jit(solution)/shard_map/psum | solution.py:403
  91.9 0.6 copies.3
  92.5 0.0 all-to-all-done.2
  92.5 0.1 slice_reduce_fusion
  92.6 10.7 %all-to-all-start.3 = ((f32[16,1,256]{2,1,0:T(1,128)}), f32[16,1,256]{2,1,0:T(1,128)S(1)}, u32[]{:S(2)}, u32[]{:S(2)}) async-start(f32[16,1,256]{2,1,0:T(1,128)} %copies.3), calls=%async_computation.3 | async-start | bytes 32768 | tf_op jit(solution)/shard_map/all_to_all | solution.py:407
  103.2 3.8 %collective-permute-start.1 = (bf16[128,256]{1,0:T(8,128)(2,1)S(1)}, bf16[128,256]{1,0:T(8,128)(2,1)S(1)}, u32[]{:S(2)}, u32[]{:S(2)}) collective-permute-start(bf16[128,256]{1,0:T(8,128)(2,1)S(1)} %slice_reduce_fusion), channel_id=1, source_target_pairs={{0,1},{1,0},{2,3},{3,2},{4,5},{5,4},{6,7},{7,6},{8,9},{9,8},{10,11... | collective-permute-start | bytes 196616 | tf_op jit(solution)/shard_map/ppermute | solution.py:406
  107.1 0.1 convert_reduce_fusion.own_ref
  107.1 3.4 %all-to-all-done.3 = f32[16,1,256]{2,1,0:T(1,128)S(1)} async-done(((f32[16,1,256]{2,1,0:T(1,128)}), f32[16,1,256]{2,1,0:T(1,128)S(1)}, u32[]{:S(2)}, u32[]{:S(2)}) %all-to-all-start.3) | async-done | bytes 16416 | tf_op jit(solution)/shard_map/all_to_all | solution.py:407
  110.6 0.5 fusion
  111.1 3.1 %collective-permute-done.1.other_ref = bf16[128,256]{1,0:T(8,128)(2,1)S(1)} collective-permute-done((bf16[128,256]{1,0:T(8,128)(2,1)S(1)}, bf16[128,256]{1,0:T(8,128)(2,1)S(1)}, u32[]{:S(2)}, u32[]{:S(2)}) %collective-permute-start.1) | collective-permute-done | bytes 65568 | tf_op jit(solution)/shard_map/ppermute | solution.py:406
  114.2 0.8 finish.1
  (14 shorter events, 0.1 us)
Async XLA Ops:
  0.6 0.8 copy-start.4
  2.4 7.8 %copy-start.1 = (bf16[1,128,128]{2,1,0:T(8,128)(2,1)S(1)}, bf16[1,128,128]{2,1,0:T(8,128)(2,1)}, u32[]{:S(2)}) copy-start(bf16[1,128,128]{2,1,0:T(8,128)(2,1)} %param.8) | copy-start | bytes 98308
  2.4 22.5 %all-to-all-start = ((bf16[8,128,256]{2,1,0:T(8,128)(2,1)}), bf16[8,128,256]{2,1,0:T(8,128)(2,1)S(1)}, u32[]{:S(2)}, u32[]{:S(2)}) async-start(bf16[8,128,256]{2,1,0:T(8,128)(2,1)} %pad_maximum_fusion), calls=%async_computation | async-start | bytes 1048576 | tf_op jit(solution)/shard_map/all_to_all | solution.py:377
  10.2 12.4 %collective-permute-start = (bf16[128,256]{1,0:T(8,128)(2,1)S(1)}, bf16[128,256]{1,0:T(8,128)(2,1)S(1)}, u32[]{:S(2)}, u32[]{:S(2)}) collective-permute-start(bf16[128,256]{1,0:T(8,128)(2,1)S(1)} %pad_maximum_fusion.1), channel_id=1, source_target_pairs={{0,1},{1,0},{2,3},{3,2},{4,5},{5,4},{6,7},{7,6},{8,9},{9,8},{10,11... | collective-permute-start | bytes 196616 | tf_op jit(solution)/shard_map/ppermute | solution.py:383
  23.3 7.6 %copy-start = (bf16[1,128,1024]{2,1,0:T(8,128)(2,1)S(1)}, bf16[1,128,1024]{2,1,0:T(8,128)(2,1)}, u32[]{:S(2)}) copy-start(bf16[1,128,1024]{2,1,0:T(8,128)(2,1)} %param.7) | copy-start | bytes 786436
  23.3 7.6 %copy-start.2 = (bf16[1,128,1024]{2,1,0:T(8,128)(2,1)S(1)}, bf16[1,128,1024]{2,1,0:T(8,128)(2,1)}, u32[]{:S(2)}) copy-start(bf16[1,128,1024]{2,1,0:T(8,128)(2,1)} %param.10) | copy-start | bytes 786436
  24.9 20.2 %all-to-all-start.1 = ((bf16[8,128,256]{2,1,0:T(8,128)(2,1)}), bf16[8,128,256]{2,1,0:T(8,128)(2,1)S(1)}, u32[]{:S(2)}, u32[]{:S(2)}) async-start(bf16[8,128,256]{2,1,0:T(8,128)(2,1)} %copies.2), calls=%async_computation.1 | async-start | bytes 1048576 | tf_op jit(solution)/shard_map/all_to_all | solution.py:377
  30.1 0.7 copy-start.5
  30.1 0.7 copy-start.6
  30.9 0.7 copy-start.3
  49.7 42.8 %all-to-all-start.2 = ((bf16[8,256,256]{2,1,0:T(8,128)(2,1)}), bf16[8,256,256]{2,1,0:T(8,128)(2,1)S(1)}, u32[]{:S(2)}, u32[]{:S(2)}) async-start(bf16[8,256,256]{2,1,0:T(8,128)(2,1)} %get-tuple-element.28), calls=%async_computation.2 | async-start | bytes 2097152 | tf_op jit(solution)/shard_map/all_to_all | solution.py:377
  92.6 18.0 %all-to-all-start.3 = ((f32[16,1,256]{2,1,0:T(1,128)}), f32[16,1,256]{2,1,0:T(1,128)S(1)}, u32[]{:S(2)}, u32[]{:S(2)}) async-start(f32[16,1,256]{2,1,0:T(1,128)} %copies.3), calls=%async_computation.3 | async-start | bytes 32768 | tf_op jit(solution)/shard_map/all_to_all | solution.py:407
  103.2 11.0 %collective-permute-start.1 = (bf16[128,256]{1,0:T(8,128)(2,1)S(1)}, bf16[128,256]{1,0:T(8,128)(2,1)S(1)}, u32[]{:S(2)}, u32[]{:S(2)}) collective-permute-start(bf16[128,256]{1,0:T(8,128)(2,1)S(1)} %slice_reduce_fusion), channel_id=1, source_target_pairs={{0,1},{1,0},{2,3},{3,2},{4,5},{5,4},{6,7},{7,6},{8,9},{9,8},{10,11... | collective-permute-start | bytes 196616 | tf_op jit(solution)/shard_map/ppermute | solution.py:406

commit v8 on v6

--- a/solution.py
+++ b/solution.py
@@ -127,7 +127,12 @@
     tok = first + lax.broadcasted_iota(jnp.int32, (8, tokens_own), 1)
     start_row = starts_of(lengths, tok)[:1]
     tok_row = tok[:1]
-    dkv_ref[...] = jnp.zeros_like(dkv_ref)
+    for i in range(2 * blocks):
+
+        @pl.when((i // 2 < lo) | (i // 2 >= hi))
+        def _():
+            dkv_ref[i] = jnp.zeros(dkv_ref.shape[1:], BF16)
+
     max_buf[...] = jnp.full_like(max_buf, masked_value)
     sum_buf[...] = jnp.zeros_like(sum_buf)
     ot_buf[...] = jnp.zeros_like(ot_buf)

time: 112 us -> 111 us (level)
  blocking collectives: 24.9 us -> 30 us
  starting transfers between devices: 44.8 us -> 40 us
  waiting for transfers between devices: 24.7 us -> 22.9 us
    psum x1, blocking collectives: 22.4 us -> 27.5 us  [body(): gains = lax.psum(gains, ('dp', 'ctx'), axis_index_groups=along_z)]
    all_to_all x3, starting transfers between devices: 19.7 us -> 15.4 us  [exchange(): return lax.all_to_all(blocks, 'ctx', 0, 0, axis_index_groups=columns)]
    all_to_all x1, starting transfers between devices: 11.1 us -> 8.84 us  [body(): lax.all_to_all(copies, ('dp', 'ctx'), 0, 0, axis_index_groups=along_xy)]
    ppermute x1, starting transfers between devices: 3.06 us -> 4.89 us  [body(): other = lax.ppermute(theirs, 'ctx', swap)]
    all_to_all x1, waiting for transfers between devices: 5.52 us -> 3.7 us  [body(): lax.all_to_all(copies, ('dp', 'ctx'), 0, 0, axis_index_groups=along_xy)]
where the time goes in v8:
time: 111 us; the launch traced here: 110 us
  starting transfers between devices  40 us (36%)
  blocking collectives  30 us (27%)
  waiting for transfers between devices  22.9 us (21%)
  Pallas kernels  12.2 us (11%)
  local copies, waits for them, and re-layouts  2.71 us (2%)
  other arithmetic  1.15 us (1%)
    psum x1, blocking collectives, body(): gains = lax.psum(gains, ('dp', 'ctx'), axis_index_groups=along_z)  27.5 us
    all_to_all x3, waiting for transfers between devices, exchange(): return lax.all_to_all(blocks, 'ctx', 0, 0, axis_index_groups=columns)  15.6 us
    all_to_all x3, starting transfers between devices, exchange(): return lax.all_to_all(blocks, 'ctx', 0, 0, axis_index_groups=columns)  15.4 us
    ppermute x1, starting transfers between devices, body(): kv_swapped = lax.ppermute(kv, 'ctx', swap)  10.9 us
    all_to_all x1, starting transfers between devices, body(): lax.all_to_all(copies, ('dp', 'ctx'), 0, 0, axis_index_groups=along_xy)  8.84 us
    ppermute x1, starting transfers between devices, body(): other = lax.ppermute(theirs, 'ctx', swap)  4.89 us
    pallas_call x1, Pallas kernels, call_attend(): pl.pallas_call(functools.partial(attend_kernel, heads), out_shape=[jax.Sh...  4.63 us
    all_to_all x1, waiting for transfers between devices, body(): lax.all_to_all(copies, ('dp', 'ctx'), 0, 0, axis_index_groups=along_xy)  3.7 us
  transfers between devices with their start and end apart: 6, of which 5 were waited for; matrix products, arithmetic and copies ran while one was open for 1% of the time, Pallas kernels for 6%

profile of v8, /device:TPU:2, one launch (start us, length us, event | category | flops | bytes accessed | tf_op | source)
XLA Modules:
  0.0 109.7 jit_solution(1168698356652579886)
XLA Ops:
  0.6 0.0 copy-start.4
  0.6 0.8 broadcast_in_dim.37
  1.5 0.9 pad_maximum_fusion
  2.4 7.2 %all-to-all-start = ((bf16[8,128,256]{2,1,0:T(8,128)(2,1)}), bf16[8,128,256]{2,1,0:T(8,128)(2,1)S(1)}, u32[]{:S(2)}, u32[]{:S(2)}) async-start(bf16[8,128,256]{2,1,0:T(8,128)(2,1)} %pad_maximum_fusion), calls=%async_computation | async-start | bytes 1048576 | tf_op jit(solution)/shard_map/all_to_all | solution.py:382
  9.6 10.9 %collective-permute-start = (bf16[128,256]{1,0:T(8,128)(2,1)S(1)}, bf16[128,256]{1,0:T(8,128)(2,1)S(1)}, u32[]{:S(2)}, u32[]{:S(2)}) collective-permute-start(bf16[128,256]{1,0:T(8,128)(2,1)S(1)} %pad_maximum_fusion.1), channel_id=1, source_target_pairs={{0,1},{1,0},{2,3},{3,2},{4,5},{5,4},{6,7},{7,6},{8,9},{9,8},{10,11... | collective-permute-start | bytes 196616 | tf_op jit(solution)/shard_map/ppermute | solution.py:388
  20.5 2.8 %collective-permute-done.refs_0_ = bf16[128,256]{1,0:T(8,128)(2,1)S(1)} collective-permute-done((bf16[128,256]{1,0:T(8,128)(2,1)S(1)}, bf16[128,256]{1,0:T(8,128)(2,1)S(1)}, u32[]{:S(2)}, u32[]{:S(2)}) %collective-permute-start) | collective-permute-done | bytes 65568 | tf_op jit(solution)/shard_map/ppermute | solution.py:388
  23.3 0.8 copies.2
  24.1 3.0 %all-to-all-done.kv_own = bf16[8,128,256]{2,1,0:T(8,128)(2,1)S(1)} async-done(((bf16[8,128,256]{2,1,0:T(8,128)(2,1)}), bf16[8,128,256]{2,1,0:T(8,128)(2,1)S(1)}, u32[]{:S(2)}, u32[]{:S(2)}) %all-to-all-start) | async-done | bytes 524320 | tf_op jit(solution)/shard_map/all_to_all | solution.py:382
  27.1 4.1 %all-to-all-start.1 = ((bf16[8,128,256]{2,1,0:T(8,128)(2,1)}), bf16[8,128,256]{2,1,0:T(8,128)(2,1)S(1)}, u32[]{:S(2)}, u32[]{:S(2)}) async-start(bf16[8,128,256]{2,1,0:T(8,128)(2,1)} %copies.2), calls=%async_computation.1 | async-start | bytes 1048576 | tf_op jit(solution)/shard_map/all_to_all | solution.py:382
  31.1 0.0 copy-start.6
  31.2 0.6 copy-done.5
  31.8 0.0 copy-done.6
  31.9 0.1 maximum_bitcast_fusion.freq
  31.9 0.7 copy-done.3
  32.6 3.2 %prep.1 = (f32[2048,128]{1,0:T(8,128)S(1)}, f32[128,128]{1,0:T(8,128)S(1)}, bf16[1024,128]{1,0:T(8,128)(2,1)S(1)}, bf16[1024,128]{1,0:T(8,128)(2,1)S(1)}) custom-call(s32[1]{0:T(128)} %bitcast.token_ref, s32[1,32]{1,0:T(1,128)S(1)} %copy-done.3, f32[1,128]{1,0:T(1,128)S(1)} %maximum_bitcast_fusion.freq, bf16[128,1024]{1,0:T(8,128)(2,1)S(1)} %bitcast.15, ...), custom_call_target="tpu_custom_call" | custom-call | flops 40000000 | bytes 4000000 | tf_op jit(solution)/shard_map/prep/pallas_call | solution.py:269
  35.8 12.6 %all-to-all-done.1.kv_other = bf16[8,128,256]{2,1,0:T(8,128)(2,1)S(1)} async-done(((bf16[8,128,256]{2,1,0:T(8,128)(2,1)}), bf16[8,128,256]{2,1,0:T(8,128)(2,1)S(1)}, u32[]{:S(2)}, u32[]{:S(2)}) %all-to-all-start.1) | async-done | bytes 524320 | tf_op jit(solution)/shard_map/all_to_all | solution.py:382
  48.4 4.6 %attend.1 = (bf16[128,1024]{1,0:T(8,128)(2,1)}, f32[128,1024]{1,0:T(8,128)S(1)}, bf16[8,256,256]{2,1,0:T(8,128)(2,1)}, f32[8,128]{1,0:T(8,128)S(1)}) custom-call(s32[1]{0:T(128)} %bitcast.token_ref, s32[1,32]{1,0:T(1,128)S(1)} %copy-done.3, bf16[8,128,256]{2,1,0:T(8,128)(2,1)S(1)} %all-to-all-done.kv_own, bf16[8,128,256]{2,1,0:T(8,128)(2,1)S(1)} %all-to-all-done.1.kv_other, ...), custom_call_target="tpu_custom_call" | custom-call | flops 3200000000 | bytes 8000000 | tf_op jit(solution)/shard_map/attend/pallas_call | solution.py:299
  53.1 4.1 %all-to-all-start.2 = ((bf16[8,256,256]{2,1,0:T(8,128)(2,1)}), bf16[8,256,256]{2,1,0:T(8,128)(2,1)S(1)}, u32[]{:S(2)}, u32[]{:S(2)}) async-start(bf16[8,256,256]{2,1,0:T(8,128)(2,1)} %get-tuple-element.28), calls=%async_computation.2 | async-start | bytes 2097152 | tf_op jit(solution)/shard_map/all_to_all | solution.py:382
  57.2 2.1 %query.1 = (bf16[128,1024]{1,0:T(8,128)(2,1)}, f32[8,256]{1,0:T(8,128)S(1)}) custom-call(f32[128,1024]{1,0:T(8,128)S(1)} %get-tuple-element.24.dqt_ref, f32[8,128]{1,0:T(8,128)S(1)} %get-tuple-element.25.key_sum_ref, f32[128,128]{1,0:T(8,128)S(1)} %get-tuple-element.26.table_own, bf16[128,1024]{1,0:T(8,128)(2,1)S(1)} %bitcast.16, f32[8,128]{1,0:T(8,128)S(1)} %stack.8.gain_ref), custom_call_target="tpu_custom_call" | custom-call | flops 5000000 | bytes 2000000 | tf_op jit(solution)/shard_map/query/pallas_call | solution.py:328
  59.3 2.4 %psum.14 = f32[256]{0:T(256)S(1)} all-reduce(f32[256]{0:T(256)S(1)} %bitcast.31), channel_id=1, replica_groups={{0,16},{32,48},{64,80},{96,112},{128,144},{160,176},{192,208},{224,240}..., use_global_device_ids=true, to_apply=%region_2.0 | all-reduce | flops 256 | bytes 2048 | tf_op jit(solution)/shard_map/psum | solution.py:407
  61.7 27.5 %psum.15.refs_0_ = f32[1,256]{1,0:T(1,128)S(1)} all-reduce(f32[1,256]{1,0:T(1,128)S(1)} %bitcast.32), channel_id=1, replica_groups={{0,32,64,96,1,33,65,97},{16,48,80,112,17,49,81,113},{2,34,66,98,3,35,67..., use_global_device_ids=true, to_apply=%region_3.0 | all-reduce | flops 256 | bytes 2048 | tf_op jit(solution)/shard_map/psum | solution.py:408
  89.2 0.6 copies.3
  89.9 0.0 all-to-all-done.2
  89.9 0.1 slice_reduce_fusion
  89.9 8.8 %all-to-all-start.3 = ((f32[32,1,256]{2,1,0:T(1,128)}), f32[32,1,256]{2,1,0:T(1,128)S(1)}, u32[]{:S(2)}, u32[]{:S(2)}) async-start(f32[32,1,256]{2,1,0:T(1,128)} %copies.3), calls=%async_computation.3 | async-start | bytes 65536 | tf_op jit(solution)/shard_map/all_to_all | solution.py:412
  98.8 4.9 %collective-permute-start.1 = (bf16[128,256]{1,0:T(8,128)(2,1)S(1)}, bf16[128,256]{1,0:T(8,128)(2,1)S(1)}, u32[]{:S(2)}, u32[]{:S(2)}) collective-permute-start(bf16[128,256]{1,0:T(8,128)(2,1)S(1)} %slice_reduce_fusion), channel_id=1, source_target_pairs={{0,1},{1,0},{2,3},{3,2},{4,5},{5,4},{6,7},{7,6},{8,9},{9,8},{10,11... | collective-permute-start | bytes 196616 | tf_op jit(solution)/shard_map/ppermute | solution.py:411
  103.7 0.1 convert_reduce_fusion.own_ref
  103.7 3.7 %all-to-all-done.3 = f32[32,1,256]{2,1,0:T(1,128)S(1)} async-done(((f32[32,1,256]{2,1,0:T(1,128)}), f32[32,1,256]{2,1,0:T(1,128)S(1)}, u32[]{:S(2)}, u32[]{:S(2)}) %all-to-all-start.3) | async-done | bytes 32800 | tf_op jit(solution)/shard_map/all_to_all | solution.py:412
  107.4 0.1 reduce_sum.32
  107.5 0.5 fusion
  108.0 0.8 collective-permute-done.1.other_ref
  108.8 0.8 finish.1
  (14 shorter events, 0.1 us)
Async XLA Ops:
  0.6 0.8 copy-start.4
  2.4 7.2 %copy-start.1 = (bf16[1,128,128]{2,1,0:T(8,128)(2,1)S(1)}, bf16[1,128,128]{2,1,0:T(8,128)(2,1)}, u32[]{:S(2)}) copy-start(bf16[1,128,128]{2,1,0:T(8,128)(2,1)} %param.8) | copy-start | bytes 98308
  2.4 24.7 %all-to-all-start = ((bf16[8,128,256]{2,1,0:T(8,128)(2,1)}), bf16[8,128,256]{2,1,0:T(8,128)(2,1)S(1)}, u32[]{:S(2)}, u32[]{:S(2)}) async-start(bf16[8,128,256]{2,1,0:T(8,128)(2,1)} %pad_maximum_fusion), calls=%async_computation | async-start | bytes 1048576 | tf_op jit(solution)/shard_map/all_to_all | solution.py:382
  9.6 13.7 %collective-permute-start = (bf16[128,256]{1,0:T(8,128)(2,1)S(1)}, bf16[128,256]{1,0:T(8,128)(2,1)S(1)}, u32[]{:S(2)}, u32[]{:S(2)}) collective-permute-start(bf16[128,256]{1,0:T(8,128)(2,1)S(1)} %pad_maximum_fusion.1), channel_id=1, source_target_pairs={{0,1},{1,0},{2,3},{3,2},{4,5},{5,4},{6,7},{7,6},{8,9},{9,8},{10,11... | collective-permute-start | bytes 196616 | tf_op jit(solution)/shard_map/ppermute | solution.py:388
  24.1 7.8 %copy-start = (bf16[1,128,1024]{2,1,0:T(8,128)(2,1)S(1)}, bf16[1,128,1024]{2,1,0:T(8,128)(2,1)}, u32[]{:S(2)}) copy-start(bf16[1,128,1024]{2,1,0:T(8,128)(2,1)} %param.7) | copy-start | bytes 786436
  24.1 7.8 %copy-start.2 = (bf16[1,128,1024]{2,1,0:T(8,128)(2,1)S(1)}, bf16[1,128,1024]{2,1,0:T(8,128)(2,1)}, u32[]{:S(2)}) copy-start(bf16[1,128,1024]{2,1,0:T(8,128)(2,1)} %param.10) | copy-start | bytes 786436
  27.1 21.4 %all-to-all-start.1 = ((bf16[8,128,256]{2,1,0:T(8,128)(2,1)}), bf16[8,128,256]{2,1,0:T(8,128)(2,1)S(1)}, u32[]{:S(2)}, u32[]{:S(2)}) async-start(bf16[8,128,256]{2,1,0:T(8,128)(2,1)} %copies.2), calls=%async_computation.1 | async-start | bytes 1048576 | tf_op jit(solution)/shard_map/all_to_all | solution.py:382
  31.1 0.7 copy-start.5
  31.1 0.7 copy-start.6
  31.9 0.7 copy-start.3
  53.1 36.8 %all-to-all-start.2 = ((bf16[8,256,256]{2,1,0:T(8,128)(2,1)}), bf16[8,256,256]{2,1,0:T(8,128)(2,1)S(1)}, u32[]{:S(2)}, u32[]{:S(2)}) async-start(bf16[8,256,256]{2,1,0:T(8,128)(2,1)} %get-tuple-element.28), calls=%async_computation.2 | async-start | bytes 2097152 | tf_op jit(solution)/shard_map/all_to_all | solution.py:382
  89.9 17.5 %all-to-all-start.3 = ((f32[32,1,256]{2,1,0:T(1,128)}), f32[32,1,256]{2,1,0:T(1,128)S(1)}, u32[]{:S(2)}, u32[]{:S(2)}) async-start(f32[32,1,256]{2,1,0:T(1,128)} %copies.3), calls=%async_computation.3 | async-start | bytes 65536 | tf_op jit(solution)/shard_map/all_to_all | solution.py:412
  98.8 10.1 %collective-permute-start.1 = (bf16[128,256]{1,0:T(8,128)(2,1)S(1)}, bf16[128,256]{1,0:T(8,128)(2,1)S(1)}, u32[]{:S(2)}, u32[]{:S(2)}) collective-permute-start(bf16[128,256]{1,0:T(8,128)(2,1)S(1)} %slice_reduce_fusion), channel_id=1, source_target_pairs={{0,1},{1,0},{2,3},{3,2},{4,5},{5,4},{6,7},{7,6},{8,9},{9,8},{10,11... | collective-permute-start | bytes 196616 | tf_op jit(solution)/shard_map/ppermute | solution.py:411
